TPU v7x, 32 devices: a whole 2x2x4 slice. The times are simulated.
32 devices in a mesh: groups: 2 (over x), wide: 4 (over y, core), narrow: 4 (over z).
Axes of the slice: x: 2, y: 2, z: 4, core: 2. Of those that a mesh axis runs over, the one named last changes fastest.
Arguments:
- density: bfloat16 [3072, 1536], P(('groups', 'wide'), 'narrow'), parts along dimension 0, as said below
- pattern: int32 [96, 48], P(('groups', 'wide'), 'narrow'), parts along dimension 0, may hold values from 0 to 1, as said below
Outputs:
- purified: bfloat16 [3072, 1536], P(('groups', 'wide'), 'narrow'), parts along dimension 0
There are 2 independent parts, one for each index of `groups`. A program takes and returns all parts, laid end to end along the dimension named above; each array names one. Nothing has to cross between parts.
Inputs may be any that keep to these rules, and one draw needn't show every extreme that they name: density is symmetric and zero outside the blocks that pattern marks. pattern is symmetric; the blocks on the diagonal are always occupied.
All inputs are finite; a program needn't handle non-finite values.
Results may differ from a plain program's by a relative error of at most 0.0055.
Values may be sent and summed in bfloat16 or wider, within the bound.
No kernel may reach another device: no remote copies, remote signals or barrier semaphores. Data moves between devices by JAX's collectives and lax.ppermute only.
A program may use at most 64 MiB of HBM per device.

v0:
```python
import jax
import jax.numpy as jnp
from jax import lax
from jax.sharding import PartitionSpec as P


def expand(pattern, row_count, col_count):
    block_rows, block_cols = pattern.shape
    block_edge = row_count // block_rows
    spread_out = jnp.broadcast_to(
        pattern[:, None, :, None], (block_rows, block_edge, block_cols, block_edge)
    )
    return spread_out.reshape(row_count, col_count).astype(jnp.float32)


def body(density, pattern):
    row_count, col_count = density.shape
    tile_mask = expand(pattern, row_count, col_count)
    row_panel = lax.all_gather(density, "narrow", axis=1, tiled=True)
    left_part = row_panel
    square = (
        jnp.dot(
            left_part,
            lax.all_gather(density, "wide", axis=0, tiled=True),
            preferred_element_type=jnp.float32,
        )
        * tile_mask
    )
    square_low = square.astype(jnp.bfloat16)
    square_panel = lax.all_gather(square_low, "narrow", axis=1, tiled=True)
    left_part = square_panel
    cube_sum = (
        jnp.dot(
            left_part,
            lax.all_gather(density, "wide", axis=0, tiled=True),
            preferred_element_type=jnp.float32,
        )
        * tile_mask
    )
    return (3.0 * square - 2.0 * cube_sum).astype(jnp.bfloat16)


def solution(mesh):
    return jax.shard_map(
        body,
        mesh=mesh,
        in_specs=(P(("groups", "wide"), "narrow"), P(("groups", "wide"), "narrow")),
        out_specs=P(("groups", "wide"), "narrow"),
        check_vma=False,
    )
```

profile of v0, /device:TPU:0, one launch (start us, length us, event | category | flops | bytes accessed | tf_op | source)
XLA Modules:
  0.0 103.2 jit_solution(7753590284129241924)
XLA Ops:
  6.5 0.0 all-gather.6.cloned.1.call-start
  6.5 0.7 all-gather.6.cloned.1.call-update
  7.3 0.0 all-gather.4.cloned.1.call-start
  7.3 0.7 all-gather.4.cloned.1.call-update
  8.0 0.0 all-gather.8.cloned.1.call-start
  8.1 0.7 convert_element_type.13
  8.8 0.3 broadcast_in_dim.2
  9.0 1.7 %convert_element_type.14 = f32[384,384]{1,0:T(8,128)} reshape(f32[12,32,12,32]{3,2,1,0:T(8,128)S(1)} %broadcast_in_dim.2) | data formatting | bytes 1179648 | tf_op jit(solution)/shard_map/convert_element_type | solution.py:13
  10.7 0.0 copy-start
  10.7 18.4 %all-gather.6.cloned.1.call-done = bf16[1536,384]{1,0:T(8,128)(2,1)} async-done(((bf16[384,384]{1,0:T(8,128)(2,1)}), bf16[1536,384]{1,0:T(8,128)(2,1)}) %all-gather.6.cloned.1.call-update) | async-done | bytes 1179664 | tf_op jit(solution)/shard_map/all_gather | solution.py:24
  29.1 0.0 copy-start.1
  29.1 31.7 %all-gather.4.cloned.1.call-done = bf16[384,1536]{1,0:T(8,128)(2,1)} async-done(((bf16[384,384]{1,0:T(8,128)(2,1)}), bf16[384,1536]{1,0:T(8,128)(2,1)}) %all-gather.4.cloned.1.call-update) | async-done | bytes 1179664 | tf_op jit(solution)/shard_map/all_gather | solution.py:19
  60.9 3.3 %fusion.3 = (bf16[384,384]{1,0:T(8,128)(2,1)}, f32[384,384]{1,0:T(8,128)S(1)}) fusion(f32[384,384]{1,0:T(8,128)} %convert_element_type.14, bf16[384,1536]{1,0:T(8,128)(2,1)} %all-gather.4.cloned.1.call-done, bf16[1536,384]{1,0:T(8,128)(2,1)} %all-gather.6.cloned.1.call-done), kind=kOutput, calls=%fused_computation.5 | convolution fusion | flops 453279744 | bytes 3833856 | tf_op jit(solution)/shard_map/dot_general | solution.py:22
  64.1 0.0 all-gather.8.cloned.1.call-update
  64.1 29.7 %all-gather.8.cloned.1.call-done = bf16[384,1536]{1,0:T(8,128)(2,1)} async-done(((bf16[384,384]{1,0:T(8,128)(2,1)}), bf16[384,1536]{1,0:T(8,128)(2,1)}) %all-gather.8.cloned.1.call-update) | async-done | bytes 1179664 | tf_op jit(solution)/shard_map/all_gather | solution.py:30
  93.9 0.0 copy-done
  93.9 0.0 copy-done.1
  93.9 2.8 %fusion.2 = bf16[384,384]{1,0:T(8,128)(2,1)} fusion(f32[384,384]{1,0:T(8,128)S(1)} %copy-done, bf16[384,1536]{1,0:T(8,128)(2,1)} %all-gather.8.cloned.1.call-done, bf16[1536,384]{1,0:T(8,128)(2,1)S(1)} %copy-done.1, f32[384,384]{1,0:T(8,128)S(1)} %get-tuple-element.6), kind=kOutput, calls=%fused_computation.4 | convolution fusion | flops 453722112 | bytes 3833856 | tf_op jit(solution)/shard_map/dot_general | solution.py:33
Async XLA Ops:
  6.5 22.6 %all-gather.6.cloned.1.call-start = ((), (), s32[]{:S(2)}) async-start(), calls=%async_computation.1 | async-start | bytes 1474560 | tf_op jit(solution)/shard_map/all_gather | solution.py:24
  7.3 53.6 %all-gather.4.cloned.1.call-start = ((), (), s32[]{:S(2)}) async-start(), calls=%async_computation | async-start | bytes 1474560 | tf_op jit(solution)/shard_map/all_gather | solution.py:19
  8.0 85.9 %all-gather.8.cloned.1.call-start = ((), (), s32[]{:S(2)}) async-start(), calls=%async_computation.2 | async-start | bytes 1474560 | tf_op jit(solution)/shard_map/all_gather | solution.py:30
  10.7 83.1 %copy-start = (f32[384,384]{1,0:T(8,128)S(1)}, f32[384,384]{1,0:T(8,128)}, u32[]{:S(2)}) copy-start(f32[384,384]{1,0:T(8,128)} %convert_element_type.14) | copy-start | bytes 1769476
  29.1 64.8 %copy-start.1 = (bf16[1536,384]{1,0:T(8,128)(2,1)S(1)}, bf16[1536,384]{1,0:T(8,128)(2,1)}, u32[]{:S(2)}) copy-start(bf16[1536,384]{1,0:T(8,128)(2,1)} %all-gather.6.cloned.1.call-done) | copy-start | bytes 3538948
Sparse Core Ops, SparseCore 0:
  8.9 20.1 all-gather.5
  30.7 30.1 all-gather.3
  64.3 29.5 all-gather.7
where the time goes:
time: 103 us
  waiting for transfers between devices  81.3 us (79%)
  between operations  13.1 us (13%)
  matrix products  6.02 us (6%)
  local copies, waits for them, and re-layouts  1.98 us (2%)
    all_gather x1, waiting for transfers between devices, body(): row_panel = lax.all_gather(density, 'narrow', axis=1, tiled=True)  31.7 us
    all_gather x1, waiting for transfers between devices, body(): square_panel = lax.all_gather(square_low, 'narrow', axis=1, tiled=True)  29.7 us
    all_gather x1, waiting for transfers between devices, body(): lax.all_gather(density, 'wide', axis=0, tiled=True)  18.4 us
    dot_general x2, matrix products, body(): jnp.dot(left_part, lax.all_gather(density, 'wide', axis=0, tiled=True), p...  6.02 us
  transfers between devices with their start and end apart: 3, of which 3 were waited for; matrix products, arithmetic and copies ran while one was open for 3% of the time, Pallas kernels for 0%

commit v1 on v0

v1 whole, which is shorter than its diff:
```python
import functools

import jax
import jax.numpy as jnp
import numpy as np
from jax import lax
from jax.experimental import pallas as pl
from jax.experimental.pallas import tpu as pltpu
from jax.sharding import PartitionSpec as P

AXES = ("wide", "narrow")
F32, BF16 = jnp.float32, jnp.bfloat16


def expand(pattern, row_count, col_count):
    block_rows, block_cols = pattern.shape
    block_edge = row_count // block_rows
    spread_out = jnp.broadcast_to(
        pattern[:, None, :, None], (block_rows, block_edge, block_cols, block_edge)
    )
    return spread_out.reshape(row_count, col_count).astype(jnp.float32)


def panel_body(density, pattern):
    row_count, col_count = density.shape
    tile_mask = expand(pattern, row_count, col_count)
    row_panel = lax.all_gather(density, "narrow", axis=1, tiled=True)
    col_panel = lax.all_gather(density, "wide", axis=0, tiled=True)
    square = jnp.dot(row_panel, col_panel, preferred_element_type=F32) * tile_mask
    square_low = square.astype(BF16)
    square_panel = lax.all_gather(square_low, "narrow", axis=1, tiled=True)
    cube_sum = jnp.dot(square_panel, col_panel, preferred_element_type=F32) * tile_mask
    return (3.0 * square - 2.0 * cube_sum).astype(BF16)


def number(i, j):
    return 4 * i + j


def turned(moves):
    other = [((3 - a, 3 - b), (3 - c, 3 - d)) for (a, b), (c, d) in moves]
    return [(number(*s), number(*t)) for s, t in moves + other]


def swap_rows(bit):
    return [(number(i, j), number(i ^ bit, j)) for i in range(4) for j in range(4)]


LINE = turned(
    [
        ((2, 0), (2, 3)),
        ((2, 1), (3, 3)),
        ((3, 0), (2, 2)),
        ((3, 1), (3, 2)),
        ((2, 2), (2, 1)),
        ((3, 2), (3, 1)),
        ((2, 3), (2, 0)),
        ((3, 3), (3, 0)),
    ]
)
ACROSS = swap_rows(2)
CORES = swap_rows(1)
PAIRS = [(number(i, j), number(i, j ^ 1)) for i in range(4) for j in range(4)]


def send(array, moves):
    return lax.ppermute(array, AXES, moves)


def moved(names, moves):
    out = [None] * 16
    for source, target in moves:
        out[target] = names[source]
    return out


def whose_blocks():
    own = [(i, j) for i in range(4) for j in range(4)]
    line = moved(own, LINE)
    across = moved(own, ACROSS)
    line_across = moved(line, ACROSS)
    by_class = [own, line_across, across, line]
    picked = [by_class[(d // 4) ^ (d % 4)][d] for d in range(16)]
    pairs = moved(picked, PAIRS)
    mine = [own, across, line, line_across, pairs]
    theirs = [moved(names, CORES) for names in mine]
    table = np.array([[x[d] for x in mine + theirs] for d in range(16)], np.int32)
    for d in range(16):
        assert len({tuple(sorted(ab)) for ab in table[d].tolist()}) == 10
    return table.reshape(16, 20)


def pack_kernel(density, pattern, out):
    rows = density.shape[0]
    n = pattern.shape[0]
    out[:rows] = density[...]
    tile = out.shape[0] - rows
    r = lax.broadcasted_iota(jnp.int32, (tile, n), 0)
    c = lax.broadcasted_iota(jnp.int32, (tile, n), 1)
    left = jnp.where(r == c, 1.0, 0.0).astype(F32)
    r = lax.broadcasted_iota(jnp.int32, (n, 128), 0)
    c = lax.broadcasted_iota(jnp.int32, (n, 128), 1)
    right = jnp.where(r == c, 1.0, 0.0).astype(F32)
    p = pattern[...].astype(F32)
    plain = jnp.dot(jnp.dot(left, p), right)
    flipped = jnp.dot(
        lax.dot_general(left, p, (((1,), (1,)), ((), ())), preferred_element_type=F32), right
    )
    out[rows:] = jnp.zeros_like(out[rows:])
    out[rows:, 0:128] = plain.astype(BF16)
    out[rows:, 128:256] = flipped.astype(BF16)


def purify_kernel(n, where, *refs):
    blocks, out, full, mask, square, low = refs[:10], refs[10], *refs[11:]
    edge = out.shape[0]
    order = full.shape[0]
    step = edge // n
    i, j = where[20], where[21]
    r = lax.broadcasted_iota(jnp.int32, (128, edge), 0)
    c = lax.broadcasted_iota(jnp.int32, (128, edge), 1)
    widen = jnp.where(r == c // step, 1.0, 0.0).astype(BF16)

    def at(k):
        return pl.ds(pl.multiple_of(k * edge, 128), edge)

    def put_mask(small, k):
        rows = jnp.dot(small, widen, preferred_element_type=F32)[:n]
        tall = jnp.broadcast_to(rows[:, None, :], (n, step, edge)).reshape(edge, edge)
        mask[:, at(k)] = tall

    for k, ref in enumerate(blocks):
        a, b = where[2 * k], where[2 * k + 1]
        block = ref[:edge]
        full[at(a), at(b)] = block

        @pl.when(a != b)
        def _():
            full[at(b), at(a)] = block.T

        @pl.when(a == i)
        def _():
            put_mask(ref[edge:, 0:128], b)

        @pl.when((b == i) & (a != b))
        def _():
            put_mask(ref[edge:, 128:256], a)

    panel = full[at(i)]
    width = 256
    for t in range(order // width):
        cols = slice(t * width, (t + 1) * width)
        s = jnp.dot(panel, full[:, cols], preferred_element_type=F32) * mask[:, cols]
        square[:, cols] = s
        low[:, cols] = s.astype(BF16)
    cube = jnp.dot(low[...], full[:, at(j)], preferred_element_type=F32) * mask[:, at(j)]
    out[...] = (3.0 * square[:, at(j)] - 2.0 * cube).astype(BF16)


def block_body(density, pattern):
    edge = density.shape[0]
    order = 4 * edge
    n = pattern.shape[0]
    vmem = pl.BlockSpec(memory_space=pltpu.VMEM)
    own = pl.pallas_call(
        pack_kernel,
        out_shape=jax.ShapeDtypeStruct((edge + 16, edge), BF16),
        in_specs=[vmem] * 2,
        out_specs=vmem,
        name="pack",
    )(density, pattern)
    i, j = lax.axis_index("wide"), lax.axis_index("narrow")
    hold = lax.optimization_barrier
    line, across, own_c = send(own, LINE), send(own, ACROSS), send(own, CORES)
    line, across, own_c = hold((line, across, own_c))
    line_across = send(line, ACROSS)
    line_c, across_c = send(line, CORES), send(across, CORES)
    line_across, line_c, across_c = hold((line_across, line_c, across_c))
    kind = jnp.bitwise_xor(i, j)
    picked = jnp.where(
        kind == 0, own, jnp.where(kind == 1, line_across, jnp.where(kind == 2, across, line))
    )
    pairs = send(picked, PAIRS)
    line_across_c = send(line_across, CORES)
    pairs_c = send(pairs, CORES)
    table = jnp.asarray(whose_blocks())
    where = jnp.concatenate([table[number(i, j)], jnp.stack([i, j]).astype(jnp.int32)])
    return pl.pallas_call(
        functools.partial(purify_kernel, n),
        out_shape=jax.ShapeDtypeStruct((edge, edge), BF16),
        in_specs=[pl.BlockSpec(memory_space=pltpu.SMEM)] + [vmem] * 10,
        out_specs=vmem,
        scratch_shapes=[
            pltpu.VMEM((order, order), BF16),
            pltpu.VMEM((edge, order), F32),
            pltpu.VMEM((edge, order), F32),
            pltpu.VMEM((edge, order), BF16),
        ],
        compiler_params=pltpu.CompilerParams(vmem_limit_bytes=40 << 20),
        name="purify",
    )(where, own, across, line, line_across, pairs, own_c, across_c, line_c, line_across_c, pairs_c)


def solution(mesh):
    four = mesh.shape["wide"] == 4 and mesh.shape["narrow"] == 4

    def body(density, pattern):
        rows, cols = density.shape
        fits = rows == cols and rows % 128 == 0 and rows <= 512
        fits = fits and pattern.shape[0] == pattern.shape[1] <= 16
        return (block_body if four and fits else panel_body)(density, pattern)

    return jax.shard_map(
        body,
        mesh=mesh,
        in_specs=(P(("groups", "wide"), "narrow"), P(("groups", "wide"), "narrow")),
        out_specs=P(("groups", "wide"), "narrow"),
        check_vma=False,
    )
```

time: 103 us -> 47.8 us (0.46)
  waiting for transfers between devices: 81.3 us -> 30.6 us
  between operations: 13.1 us -> 0.01 us
  Pallas kernels: 0 us -> 7.78 us
  starting transfers between devices: 0.08 us -> 7.4 us
  matrix products: 6.02 us -> 0 us
  local copies, waits for them, and re-layouts: 1.98 us -> 0.7 us
    all_gather x3 -> x0, waiting for transfers between devices: 79.8 us -> none  [the longest x1 31.7 us: body(): row_panel = lax.all_gather(density, 'narrow', axis=1, tiled=True)]
    ppermute x0 -> x9, waiting for transfers between devices: none -> 30.6 us  [send(): return lax.ppermute(array, AXES, moves)]
    pallas_call x0 -> x2, Pallas kernels: none -> 7.78 us  [the longest x1 5.86 us: block_body(): pl.pallas_call(functools.partial(purify_kernel, n), out_shape=jax.ShapeDt...]
    ppermute x0 -> x9, starting transfers between devices: none -> 7.4 us  [send(): return lax.ppermute(array, AXES, moves)]
    dot_general x2 -> x0, matrix products: 6.02 us -> none  [body(): jnp.dot(left_part, lax.all_gather(density, 'wide', axis=0, tiled=True), p...]
    convert_element_type x1 -> x0, local copies, waits for them, and re-layouts: 1.7 us -> none  [expand(): return spread_out.reshape(row_count, col_count).astype(jnp.float32)]
    unnamed x3 -> x0, waiting for transfers between devices: 1.42 us -> none
    select_n x0 -> x1, other arithmetic: none -> 1.05 us  [block_body(): jnp.where(kind == 0, own, jnp.where(kind == 1, line_across, jnp.where(kin...]
  transfers between devices with their start and end apart: 3 -> 9, of which waited for: 3 -> 7; matrix products, arithmetic and copies ran while one was open for 3% -> 2% of each run, Pallas kernels for 0% -> 0%
where the time goes in v1:
time: 47.8 us; the launch traced here: 47.6 us
  waiting for transfers between devices  30.6 us (64%)
  Pallas kernels  7.78 us (16%)
  starting transfers between devices  7.4 us (15%)
  other arithmetic  1.13 us (2%)
  local copies, waits for them, and re-layouts  0.7 us (1%)
    ppermute x9, waiting for transfers between devices, send(): return lax.ppermute(array, AXES, moves)  30.6 us
    ppermute x9, starting transfers between devices, send(): return lax.ppermute(array, AXES, moves)  7.4 us
    pallas_call x1, Pallas kernels, block_body(): pl.pallas_call(functools.partial(purify_kernel, n), out_shape=jax.ShapeDt...  5.86 us
    pallas_call x1, Pallas kernels, block_body(): pl.pallas_call(pack_kernel, out_shape=jax.ShapeDtypeStruct((edge + 16, ed...  1.92 us
    select_n x1, other arithmetic, block_body(): jnp.where(kind == 0, own, jnp.where(kind == 1, line_across, jnp.where(kin...  1.05 us
  transfers between devices with their start and end apart: 9, of which 7 were waited for; matrix products, arithmetic and copies ran while one was open for 2% of the time, Pallas kernels for 0%

profile of v1, /device:TPU:0, one launch (start us, length us, event | category | flops | bytes accessed | tf_op | source)
XLA Modules:
  0.0 47.6 jit_solution(12517054812249709920)
XLA Ops:
  0.0 1.9 %pack.1.refs_0_ = bf16[400,384]{1,0:T(8,128)(2,1)} custom-call(bf16[384,384]{1,0:T(8,128)(2,1)} %density.1, s32[12,12]{1,0:T(8,128)} %pattern.1), custom_call_target="tpu_custom_call" | custom-call | tf_op jit(solution)/shard_map/pack/pallas_call | solution.py:165
  1.9 0.5 collective-permute-start.2
  2.4 2.5 %collective-permute-start.1 = (bf16[400,384]{1,0:T(8,128)(2,1)}, bf16[400,384]{1,0:T(8,128)(2,1)S(1)}, u32[]{:S(2)}, u32[]{:S(2)}) collective-permute-start(bf16[400,384]{1,0:T(8,128)(2,1)} %pack.1.refs_0_), channel_id=1, source_target_pairs={{0,8},{1,9},{2,10},{3,11},{4,12},{5,13},{6,14},{7,15},{8,0},{9,1},... | collective-permute-start | bytes 921608 | tf_op jit(solution)/shard_map/ppermute | solution.py:67
  4.9 3.6 %collective-permute-start = (bf16[400,384]{1,0:T(8,128)(2,1)}, bf16[400,384]{1,0:T(8,128)(2,1)S(1)}, u32[]{:S(2)}, u32[]{:S(2)}) collective-permute-start(bf16[400,384]{1,0:T(8,128)(2,1)} %pack.1.refs_0_), channel_id=1, source_target_pairs={{8,11},{9,15},{12,10},{13,14},{10,9},{14,13},{11,8},{15,12},{7,4},... | collective-permute-start | bytes 921608 | tf_op jit(solution)/shard_map/ppermute | solution.py:67
  8.5 0.0 collective-permute-done.2.refs_5_
  8.5 4.5 %collective-permute-done.1.refs_1_ = bf16[400,384]{1,0:T(8,128)(2,1)S(1)} collective-permute-done((bf16[400,384]{1,0:T(8,128)(2,1)}, bf16[400,384]{1,0:T(8,128)(2,1)S(1)}, u32[]{:S(2)}, u32[]{:S(2)}) %collective-permute-start.1) | collective-permute-done | bytes 307232 | tf_op jit(solution)/shard_map/ppermute | solution.py:67
  13.0 8.5 %collective-permute-done.refs_2_ = bf16[400,384]{1,0:T(8,128)(2,1)S(1)} collective-permute-done((bf16[400,384]{1,0:T(8,128)(2,1)}, bf16[400,384]{1,0:T(8,128)(2,1)S(1)}, u32[]{:S(2)}, u32[]{:S(2)}) %collective-permute-start) | collective-permute-done | bytes 307232 | tf_op jit(solution)/shard_map/ppermute | solution.py:67
  21.5 0.0 collective-permute-start.5
  21.5 0.5 %collective-permute-start.4 = (bf16[400,384]{1,0:T(8,128)(2,1)S(1)}, bf16[400,384]{1,0:T(8,128)(2,1)S(1)}, u32[]{:S(2)}, u32[]{:S(2)}) collective-permute-start(bf16[400,384]{1,0:T(8,128)(2,1)S(1)} %collective-permute-done.refs_2_), channel_id=1, source_target_pairs={{0,4},{1,5},{2,6},{3,7},{4,0},{5,1},{6,2},{7,3},{8,12},{9,13},{10,... | collective-permute-start | bytes 921608 | tf_op jit(solution)/shard_map/ppermute | solution.py:67
  22.0 0.0 collective-permute-start.3
  22.0 0.0 copy-start
  22.0 1.1 %collective-permute-done.5.refs_6_ = bf16[400,384]{1,0:T(8,128)(2,1)S(1)} collective-permute-done((bf16[400,384]{1,0:T(8,128)(2,1)S(1)}, bf16[400,384]{1,0:T(8,128)(2,1)S(1)}, u32[]{:S(2)}, u32[]{:S(2)}) %collective-permute-start.5) | collective-permute-done | bytes 307232 | tf_op jit(solution)/shard_map/ppermute | solution.py:67
  23.1 0.4 collective-permute-done.4.refs_7_
  23.5 7.7 %collective-permute-done.3.refs_3_ = bf16[400,384]{1,0:T(8,128)(2,1)S(1)} collective-permute-done((bf16[400,384]{1,0:T(8,128)(2,1)S(1)}, bf16[400,384]{1,0:T(8,128)(2,1)S(1)}, u32[]{:S(2)}, u32[]{:S(2)}) %collective-permute-start.3) | collective-permute-done | bytes 307232 | tf_op jit(solution)/shard_map/ppermute | solution.py:67
  31.2 1.1 %select_select_fusion = bf16[400,384]{1,0:T(8,128)(2,1)S(1)} fusion(bf16[400,384]{1,0:T(8,128)(2,1)} %pack.1.refs_0_, bf16[400,384]{1,0:T(8,128)(2,1)S(1)} %collective-permute-done.3.refs_3_, bf16[400,384]{1,0:T(8,128)(2,1)S(1)} %collective-permute-done.1.refs_1_, bf16[400,384]{1,0:T(8,128)(2,1)S(1)} %collective-permute-done.refs_2_, pred[]{:T(512)S(6)} %eq.11, ...), kind=kLoop, calls=%fused_computation | loop fusion | flops 460800 | bytes 1536003 | tf_op jit(solution)/shard_map/jit(_where)/select_n | solution.py:180
  32.3 0.3 collective-permute-start.6
  32.6 0.0 collective-permute-start.7
  32.6 7.5 %collective-permute-done.6.refs_4_ = bf16[400,384]{1,0:T(8,128)(2,1)S(1)} collective-permute-done((bf16[400,384]{1,0:T(8,128)(2,1)S(1)}, bf16[400,384]{1,0:T(8,128)(2,1)S(1)}, u32[]{:S(2)}, u32[]{:S(2)}) %collective-permute-start.6) | collective-permute-done | bytes 307232 | tf_op jit(solution)/shard_map/ppermute | solution.py:67
  40.1 0.0 collective-permute-start.8
  40.1 0.7 %dynamic-slice_bitcast_fusion = s32[20]{0:T(128)S(1)} fusion(s32[16,20]{1,0:T(8,128)} %constant.19.clone, s32[]{:T(128)S(6)} %select_n.23), kind=kLoop, calls=%fused_computation.2 | loop fusion | bytes 164 | tf_op jit(solution)/shard_map/squeeze | solution.py:187
  40.8 0.1 pad_add_fusion.where
  40.9 0.0 collective-permute-done.7.refs_8_
  40.9 0.8 %collective-permute-done.8.refs_9_ = bf16[400,384]{1,0:T(8,128)(2,1)S(1)} collective-permute-done((bf16[400,384]{1,0:T(8,128)(2,1)S(1)}, bf16[400,384]{1,0:T(8,128)(2,1)S(1)}, u32[]{:S(2)}, u32[]{:S(2)}) %collective-permute-start.8) | collective-permute-done | bytes 307232 | tf_op jit(solution)/shard_map/ppermute | solution.py:67
  41.7 0.0 copy-done
  41.7 5.9 %purify.1 = bf16[384,384]{1,0:T(8,128)(2,1)} custom-call(s32[22]{0:T(128)S(1)} %pad_add_fusion.where, bf16[400,384]{1,0:T(8,128)(2,1)S(1)} %copy-done, bf16[400,384]{1,0:T(8,128)(2,1)S(1)} %collective-permute-done.1.refs_1_, bf16[400,384]{1,0:T(8,128)(2,1)S(1)} %collective-permute-done.refs_2_, bf16[400,384]{1,0:T(8,128)(2,1)S(1)} %collective-permute-done.3.refs_3_, ...), custom_call_target="tpu_custom_call" | custom-call | tf_op jit(solution)/shard_map/purify/pallas_call | solution.py:188
Async XLA Ops:
  1.9 6.6 %collective-permute-start.2 = (bf16[400,384]{1,0:T(8,128)(2,1)}, bf16[400,384]{1,0:T(8,128)(2,1)S(1)}, u32[]{:S(2)}, u32[]{:S(2)}) collective-permute-start(bf16[400,384]{1,0:T(8,128)(2,1)} %pack.1.refs_0_), channel_id=1, source_target_pairs={{0,4},{1,5},{2,6},{3,7},{4,0},{5,1},{6,2},{7,3},{8,12},{9,13},{10,... | collective-permute-start | bytes 921608 | tf_op jit(solution)/shard_map/ppermute | solution.py:67
  2.4 10.7 %collective-permute-start.1 = (bf16[400,384]{1,0:T(8,128)(2,1)}, bf16[400,384]{1,0:T(8,128)(2,1)S(1)}, u32[]{:S(2)}, u32[]{:S(2)}) collective-permute-start(bf16[400,384]{1,0:T(8,128)(2,1)} %pack.1.refs_0_), channel_id=1, source_target_pairs={{0,8},{1,9},{2,10},{3,11},{4,12},{5,13},{6,14},{7,15},{8,0},{9,1},... | collective-permute-start | bytes 921608 | tf_op jit(solution)/shard_map/ppermute | solution.py:67
  4.9 16.6 %collective-permute-start = (bf16[400,384]{1,0:T(8,128)(2,1)}, bf16[400,384]{1,0:T(8,128)(2,1)S(1)}, u32[]{:S(2)}, u32[]{:S(2)}) collective-permute-start(bf16[400,384]{1,0:T(8,128)(2,1)} %pack.1.refs_0_), channel_id=1, source_target_pairs={{8,11},{9,15},{12,10},{13,14},{10,9},{14,13},{11,8},{15,12},{7,4},... | collective-permute-start | bytes 921608 | tf_op jit(solution)/shard_map/ppermute | solution.py:67
  21.5 1.6 %collective-permute-start.5 = (bf16[400,384]{1,0:T(8,128)(2,1)S(1)}, bf16[400,384]{1,0:T(8,128)(2,1)S(1)}, u32[]{:S(2)}, u32[]{:S(2)}) collective-permute-start(bf16[400,384]{1,0:T(8,128)(2,1)S(1)} %collective-permute-done.1.refs_1_), channel_id=1, source_target_pairs={{0,4},{1,5},{2,6},{3,7},{4,0},{5,1},{6,2},{7,3},{8,12},{9,13},{10,... | collective-permute-start | bytes 921608 | tf_op jit(solution)/shard_map/ppermute | solution.py:67
  21.5 2.0 %collective-permute-start.4 = (bf16[400,384]{1,0:T(8,128)(2,1)S(1)}, bf16[400,384]{1,0:T(8,128)(2,1)S(1)}, u32[]{:S(2)}, u32[]{:S(2)}) collective-permute-start(bf16[400,384]{1,0:T(8,128)(2,1)S(1)} %collective-permute-done.refs_2_), channel_id=1, source_target_pairs={{0,4},{1,5},{2,6},{3,7},{4,0},{5,1},{6,2},{7,3},{8,12},{9,13},{10,... | collective-permute-start | bytes 921608 | tf_op jit(solution)/shard_map/ppermute | solution.py:67
  22.0 9.2 %collective-permute-start.3 = (bf16[400,384]{1,0:T(8,128)(2,1)S(1)}, bf16[400,384]{1,0:T(8,128)(2,1)S(1)}, u32[]{:S(2)}, u32[]{:S(2)}) collective-permute-start(bf16[400,384]{1,0:T(8,128)(2,1)S(1)} %collective-permute-done.refs_2_), channel_id=1, source_target_pairs={{0,8},{1,9},{2,10},{3,11},{4,12},{5,13},{6,14},{7,15},{8,0},{9,1},... | collective-permute-start | bytes 921608 | tf_op jit(solution)/shard_map/ppermute | solution.py:67
  22.0 19.7 %copy-start = (bf16[400,384]{1,0:T(8,128)(2,1)S(1)}, bf16[400,384]{1,0:T(8,128)(2,1)}, u32[]{:S(2)}) copy-start(bf16[400,384]{1,0:T(8,128)(2,1)} %pack.1.refs_0_) | copy-start | bytes 921604
  32.3 7.9 %collective-permute-start.6 = (bf16[400,384]{1,0:T(8,128)(2,1)S(1)}, bf16[400,384]{1,0:T(8,128)(2,1)S(1)}, u32[]{:S(2)}, u32[]{:S(2)}) collective-permute-start(bf16[400,384]{1,0:T(8,128)(2,1)S(1)} %select_select_fusion), channel_id=1, source_target_pairs={{0,1},{1,0},{2,3},{3,2},{4,5},{5,4},{6,7},{7,6},{8,9},{9,8},{10,11... | collective-permute-start | bytes 921608 | tf_op jit(solution)/shard_map/ppermute | solution.py:67
  32.6 8.3 %collective-permute-start.7 = (bf16[400,384]{1,0:T(8,128)(2,1)S(1)}, bf16[400,384]{1,0:T(8,128)(2,1)S(1)}, u32[]{:S(2)}, u32[]{:S(2)}) collective-permute-start(bf16[400,384]{1,0:T(8,128)(2,1)S(1)} %collective-permute-done.3.refs_3_), channel_id=1, source_target_pairs={{0,4},{1,5},{2,6},{3,7},{4,0},{5,1},{6,2},{7,3},{8,12},{9,13},{10,... | collective-permute-start | bytes 921608 | tf_op jit(solution)/shard_map/ppermute | solution.py:67
  40.1 1.6 %collective-permute-start.8 = (bf16[400,384]{1,0:T(8,128)(2,1)S(1)}, bf16[400,384]{1,0:T(8,128)(2,1)S(1)}, u32[]{:S(2)}, u32[]{:S(2)}) collective-permute-start(bf16[400,384]{1,0:T(8,128)(2,1)S(1)} %collective-permute-done.6.refs_4_), channel_id=1, source_target_pairs={{0,4},{1,5},{2,6},{3,7},{4,0},{5,1},{6,2},{7,3},{8,12},{9,13},{10,... | collective-permute-start | bytes 921608 | tf_op jit(solution)/shard_map/ppermute | solution.py:67

commit v2 on v1

v2 whole, which is shorter than its diff:
```python
import jax
import jax.numpy as jnp
import numpy as np
from jax import lax
from jax.experimental import pallas as pl
from jax.experimental.pallas import tpu as pltpu
from jax.sharding import PartitionSpec as P

AXES = ("wide", "narrow")
F32, BF16 = jnp.float32, jnp.bfloat16


def expand(pattern, row_count, col_count):
    block_rows, block_cols = pattern.shape
    block_edge = row_count // block_rows
    spread_out = jnp.broadcast_to(
        pattern[:, None, :, None], (block_rows, block_edge, block_cols, block_edge)
    )
    return spread_out.reshape(row_count, col_count).astype(jnp.float32)


def panel_body(density, pattern):
    row_count, col_count = density.shape
    tile_mask = expand(pattern, row_count, col_count)
    row_panel = lax.all_gather(density, "narrow", axis=1, tiled=True)
    col_panel = lax.all_gather(density, "wide", axis=0, tiled=True)
    square = jnp.dot(row_panel, col_panel, preferred_element_type=F32) * tile_mask
    square_low = square.astype(BF16)
    square_panel = lax.all_gather(square_low, "narrow", axis=1, tiled=True)
    cube_sum = jnp.dot(square_panel, col_panel, preferred_element_type=F32) * tile_mask
    return (3.0 * square - 2.0 * cube_sum).astype(BF16)


def number(i, j):
    return 4 * i + j


def turned(moves):
    other = [((3 - a, 3 - b), (3 - c, 3 - d)) for (a, b), (c, d) in moves]
    return [(number(*s), number(*t)) for s, t in moves + other]


def moves_of(kinds, target):
    grid = [(i, j) for i in range(4) for j in range(4) if i ^ j in kinds]
    return [(number(i, j), number(*target(i, j))) for i, j in grid]


LINE = turned(
    [
        ((2, 0), (2, 3)),
        ((2, 1), (3, 3)),
        ((3, 0), (2, 2)),
        ((3, 1), (3, 2)),
        ((2, 2), (2, 1)),
        ((3, 2), (3, 1)),
        ((2, 3), (2, 0)),
        ((3, 3), (3, 0)),
    ]
)
ACROSS = moves_of((0, 1, 2, 3), lambda i, j: (i ^ 2, j))
CORES = moves_of((0, 1, 2, 3), lambda i, j: (i ^ 1, j))
NEAR_DIAGONAL = moves_of((0, 2), lambda i, j: (i ^ 1, j ^ 1))
FAR_DIAGONAL = moves_of((2,), lambda i, j: (i ^ 1, j ^ 2))
LAST_DIAGONAL = moves_of((3,), lambda i, j: (i ^ 1, j ^ 1))


def send(array, moves):
    return lax.ppermute(array, AXES, moves)


def moved(names, moves):
    out = [None] * 16
    for source, target in moves:
        out[target] = names[source]
    return out


def whose_blocks():
    own = [(i, j) for i in range(4) for j in range(4)]
    kind = [i ^ j for i, j in own]
    line = moved(own, LINE)
    across = moved(own, ACROSS)
    line_across = moved(line, ACROSS)
    near = moved([own[d] if kind[d] == 0 else across[d] for d in range(16)], NEAR_DIAGONAL)
    far = moved(across, FAR_DIAGONAL)
    last = moved(line, LAST_DIAGONAL)
    diagonal = [(near, far, near, last)[kind[d]][d] for d in range(16)]
    mine = [own, across, line, line_across, diagonal]
    theirs = [moved(names, CORES) for names in mine]
    order = [own, theirs[0], across, theirs[1], line, theirs[2]]
    order += [line_across, diagonal, theirs[3], theirs[4]]
    table = np.array([[x[d] for x in order] for d in range(16)], np.int32)
    for d in range(16):
        assert len({tuple(sorted(ab)) for ab in table[d].tolist()}) == 10
    return table.reshape(16, 20)


def purify_kernel(where, *refs):
    blocks, patterns, out = refs[:10], refs[10:14], refs[14]
    full, mask, square, low, sems = refs[15:]
    edge = out.shape[0]
    order = full.shape[0]
    n = patterns[0].shape[0]
    step = edge // n
    i, j = where[20], where[21]

    def at(k):
        return pl.ds(pl.multiple_of(k * edge, 128), edge)

    def copy(k):
        a, b = where[2 * k], where[2 * k + 1]
        return pltpu.make_async_copy(blocks[k], full.at[at(a), at(b)], sems.at[k])

    for k in range(10):
        copy(k).start()
    r = lax.broadcasted_iota(jnp.int32, (n, edge), 0)
    c = lax.broadcasted_iota(jnp.int32, (n, edge), 1)
    widen = jnp.where(r == c // step, 1.0, 0.0).astype(BF16)
    for k, ref in enumerate(patterns):
        rows = jnp.dot(ref[...].astype(BF16), widen, preferred_element_type=F32)
        tall = jnp.broadcast_to(rows[:, None, :], (n, step, edge)).reshape(edge, edge)
        mask[:, at(jnp.bitwise_xor(j, k))] = tall
    for k in range(10):
        a, b = where[2 * k], where[2 * k + 1]
        copy(k).wait()

        @pl.when(a != b)
        def _():
            full[at(b), at(a)] = full[at(a), at(b)].T

    panel = full[at(i)]
    width = 256
    for t in range(order // width):
        cols = slice(t * width, (t + 1) * width)
        s = jnp.dot(panel, full[:, cols], preferred_element_type=F32) * mask[:, cols]
        square[:, cols] = s
        low[:, cols] = s.astype(BF16)
    cube = jnp.dot(low[...], full[:, at(j)], preferred_element_type=F32) * mask[:, at(j)]
    out[...] = (3.0 * square[:, at(j)] - 2.0 * cube).astype(BF16)


def block_body(own, pattern):
    edge = own.shape[0]
    order = 4 * edge
    i, j = lax.axis_index("wide"), lax.axis_index("narrow")
    kind = jnp.bitwise_xor(i, j)
    hold = lax.optimization_barrier
    line, across = send(own, LINE), send(own, ACROSS)
    near = send(jnp.where(kind == 0, own, across), NEAR_DIAGONAL)
    far = send(across, FAR_DIAGONAL)
    own_c, across_c = send(own, CORES), send(across, CORES)
    line, near, own_c, across_c = hold((line, near, own_c, across_c))
    line_across, last = send(line, ACROSS), send(line, LAST_DIAGONAL)
    pattern, line = hold((pattern, line))
    patterns = [pattern]
    for k in (1, 2, 3):
        patterns.append(lax.ppermute(pattern, "narrow", [(c, c ^ k) for c in range(4)]))
    line_across, last, far, patterns = hold((line_across, last, far, patterns))
    diagonal = jnp.where(kind == 3, last, jnp.where(kind == 1, far, near))
    line_c = send(line, CORES)
    line_across_c, diagonal_c = send(line_across, CORES), send(diagonal, CORES)
    table = jnp.asarray(whose_blocks())
    where = jnp.concatenate([table[number(i, j)], jnp.stack([i, j]).astype(jnp.int32)])
    vmem = pl.BlockSpec(memory_space=pltpu.VMEM)
    anywhere = pl.BlockSpec(memory_space=pl.ANY)
    return pl.pallas_call(
        purify_kernel,
        out_shape=jax.ShapeDtypeStruct((edge, edge), BF16),
        in_specs=[pl.BlockSpec(memory_space=pltpu.SMEM)] + [anywhere] * 10 + [vmem] * 4,
        out_specs=vmem,
        scratch_shapes=[
            pltpu.VMEM((order, order), BF16),
            pltpu.VMEM((edge, order), F32),
            pltpu.VMEM((edge, order), F32),
            pltpu.VMEM((edge, order), BF16),
            pltpu.SemaphoreType.DMA((10,)),
        ],
        compiler_params=pltpu.CompilerParams(vmem_limit_bytes=40 << 20),
        name="purify",
    )(
        where,
        *(own, own_c, across, across_c, line, line_c),
        *(line_across, diagonal, line_across_c, diagonal_c),
        *patterns,
    )


def solution(mesh):
    four = mesh.shape["wide"] == 4 and mesh.shape["narrow"] == 4

    def body(density, pattern):
        rows, cols = density.shape
        fits = rows == cols and rows % 128 == 0 and rows <= 512
        fits = fits and pattern.shape[0] == pattern.shape[1] <= 16
        return (block_body if four and fits else panel_body)(density, pattern)

    return jax.shard_map(
        body,
        mesh=mesh,
        in_specs=(P(("groups", "wide"), "narrow"), P(("groups", "wide"), "narrow")),
        out_specs=P(("groups", "wide"), "narrow"),
        check_vma=False,
    )
```

time: 47.8 us -> 37.6 us (0.79)
  waiting for transfers between devices: 30.6 us -> 15.6 us
  starting transfers between devices: 7.4 us -> 14.4 us
  Pallas kernels: 7.78 us -> 5.49 us
    ppermute x9 -> x11, waiting for transfers between devices: 30.6 us -> 11.7 us  [send(): return lax.ppermute(array, AXES, moves)]
    ppermute x0 -> x3, waiting for transfers between devices: none -> 3.96 us  [block_body(): lax.ppermute(pattern, 'narrow', [(c, c ^ k) for c in range(4)])]
    ppermute x0 -> x3, starting transfers between devices: none -> 3.55 us  [block_body(): lax.ppermute(pattern, 'narrow', [(c, c ^ k) for c in range(4)])]
    ppermute x9 -> x11, starting transfers between devices: 7.4 us -> 10.8 us  [send(): return lax.ppermute(array, AXES, moves)]
    pallas_call x2 -> x1, Pallas kernels: 7.78 us -> 5.49 us  [block_body(): pl.pallas_call(purify_kernel, out_shape=jax.ShapeDtypeStruct((edge, edge)...]
    select_n x1 -> x2, other arithmetic: 1.05 us -> 1.05 us  [the longest x1 1 us: block_body(): near = send(jnp.where(kind == 0, own, across), NEAR_DIAGONAL)]
  transfers between devices with their start and end apart: 9 -> 14, of which waited for: 7 -> 7; matrix products, arithmetic and copies ran while one was open for 2% -> 5% of each run, Pallas kernels for 0% -> 0%
where the time goes in v2:
time: 37.6 us; the launch traced here: 37.4 us
  waiting for transfers between devices  15.6 us (41%)
  starting transfers between devices  14.4 us (38%)
  Pallas kernels  5.49 us (15%)
  other arithmetic  1.13 us (3%)
  local copies, waits for them, and re-layouts  0.7 us (2%)
    ppermute x11, waiting for transfers between devices, send(): return lax.ppermute(array, AXES, moves)  11.7 us
    ppermute x11, starting transfers between devices, send(): return lax.ppermute(array, AXES, moves)  10.8 us
    pallas_call x1, Pallas kernels, block_body(): pl.pallas_call(purify_kernel, out_shape=jax.ShapeDtypeStruct((edge, edge)...  5.49 us
    ppermute x3, waiting for transfers between devices, block_body(): lax.ppermute(pattern, 'narrow', [(c, c ^ k) for c in range(4)])  3.96 us
    ppermute x3, starting transfers between devices, block_body(): lax.ppermute(pattern, 'narrow', [(c, c ^ k) for c in range(4)])  3.55 us
    select_n x1, other arithmetic, block_body(): near = send(jnp.where(kind == 0, own, across), NEAR_DIAGONAL)  1 us
  transfers between devices with their start and end apart: 14, of which 7 were waited for; matrix products, arithmetic and copies ran while one was open for 5% of the time, Pallas kernels for 0%

profile of v2, /device:TPU:0, one launch (start us, length us, event | category | flops | bytes accessed | tf_op | source)
XLA Modules:
  0.0 37.4 jit_solution(17521159958198367486)
XLA Ops:
  0.0 3.0 %collective-permute-start.1 = (bf16[384,384]{1,0:T(8,128)(2,1)}, bf16[384,384]{1,0:T(8,128)(2,1)S(1)}, u32[]{:S(2)}, u32[]{:S(2)}) collective-permute-start(bf16[384,384]{1,0:T(8,128)(2,1)} %refs_0_.1), channel_id=1, source_target_pairs={{0,8},{1,9},{2,10},{3,11},{4,12},{5,13},{6,14},{7,15},{8,0},{9,1},... | collective-permute-start | bytes 884744 | tf_op jit(solution)/shard_map/ppermute | solution.py:68
  3.0 3.6 %collective-permute-start = (bf16[384,384]{1,0:T(8,128)(2,1)}, bf16[384,384]{1,0:T(8,128)(2,1)S(1)}, u32[]{:S(2)}, u32[]{:S(2)}) collective-permute-start(bf16[384,384]{1,0:T(8,128)(2,1)} %refs_0_.1), channel_id=1, source_target_pairs={{8,11},{9,15},{12,10},{13,14},{10,9},{14,13},{11,8},{15,12},{7,4},... | collective-permute-start | bytes 884744 | tf_op jit(solution)/shard_map/ppermute | solution.py:68
  6.6 0.0 collective-permute-start.3
  6.6 3.6 %collective-permute-done.1.refs_2_ = bf16[384,384]{1,0:T(8,128)(2,1)S(1)} collective-permute-done((bf16[384,384]{1,0:T(8,128)(2,1)}, bf16[384,384]{1,0:T(8,128)(2,1)S(1)}, u32[]{:S(2)}, u32[]{:S(2)}) %collective-permute-start.1) | collective-permute-done | bytes 294944 | tf_op jit(solution)/shard_map/ppermute | solution.py:68
  10.2 1.0 %broadcast_select_fusion = bf16[384,384]{1,0:T(8,128)(2,1)S(1)} fusion(bf16[384,384]{1,0:T(8,128)(2,1)} %refs_0_.1, bf16[384,384]{1,0:T(8,128)(2,1)S(1)} %collective-permute-done.1.refs_2_, pred[]{:T(512)S(6)} %eq.9), kind=kLoop, calls=%fused_computation.1 | loop fusion | flops 147456 | bytes 884737 | tf_op jit(solution)/shard_map/jit(_where)/select_n | solution.py:149
  11.2 2.3 %collective-permute-start.2 = (bf16[384,384]{1,0:T(8,128)(2,1)S(1)}, bf16[384,384]{1,0:T(8,128)(2,1)S(1)}, u32[]{:S(2)}, u32[]{:S(2)}) collective-permute-start(bf16[384,384]{1,0:T(8,128)(2,1)S(1)} %broadcast_select_fusion), channel_id=1, source_target_pairs={{0,5},{2,7},{5,0},{7,2},{8,13},{10,15},{13,8},{15,10},{16,21},{18,... | collective-permute-start | bytes 884744 | tf_op jit(solution)/shard_map/ppermute | solution.py:68
  13.5 0.1 collective-permute-start.4
  13.5 0.7 %collective-permute-start.8 = (bf16[384,384]{1,0:T(8,128)(2,1)S(1)}, bf16[384,384]{1,0:T(8,128)(2,1)S(1)}, u32[]{:S(2)}, u32[]{:S(2)}) collective-permute-start(bf16[384,384]{1,0:T(8,128)(2,1)S(1)} %collective-permute-done.1.refs_2_), channel_id=1, source_target_pairs={{2,4},{7,1},{8,14},{13,11},{18,20},{23,17},{24,30},{29,27}} | collective-permute-start | bytes 884744 | tf_op jit(solution)/shard_map/ppermute | solution.py:68
  14.2 5.2 %collective-permute-done.refs_4_ = bf16[384,384]{1,0:T(8,128)(2,1)S(1)} collective-permute-done((bf16[384,384]{1,0:T(8,128)(2,1)}, bf16[384,384]{1,0:T(8,128)(2,1)S(1)}, u32[]{:S(2)}, u32[]{:S(2)}) %collective-permute-start) | collective-permute-done | bytes 294944 | tf_op jit(solution)/shard_map/ppermute | solution.py:68
  19.5 0.0 collective-permute-done.3.refs_1_
  19.5 2.1 %collective-permute-done.2 = bf16[384,384]{1,0:T(8,128)(2,1)S(1)} collective-permute-done((bf16[384,384]{1,0:T(8,128)(2,1)S(1)}, bf16[384,384]{1,0:T(8,128)(2,1)S(1)}, u32[]{:S(2)}, u32[]{:S(2)}) %collective-permute-start.2) | collective-permute-done | bytes 294944 | tf_op jit(solution)/shard_map/ppermute | solution.py:68
  21.5 0.0 collective-permute-done.4.refs_3_
  21.6 0.0 collective-permute-start.6
  21.6 0.7 %collective-permute-start.7 = (bf16[384,384]{1,0:T(8,128)(2,1)S(1)}, bf16[384,384]{1,0:T(8,128)(2,1)S(1)}, u32[]{:S(2)}, u32[]{:S(2)}) collective-permute-start(bf16[384,384]{1,0:T(8,128)(2,1)S(1)} %collective-permute-done.refs_4_), channel_id=1, source_target_pairs={{3,6},{6,3},{9,12},{12,9},{19,22},{22,19},{25,28},{28,25}} | collective-permute-start | bytes 884744 | tf_op jit(solution)/shard_map/ppermute | solution.py:68
  22.2 2.1 %collective-permute-start.10 = (s32[12,12]{1,0:T(8,128)S(1)}, s32[12,12]{1,0:T(8,128)S(1)}, u32[]{:S(2)}, u32[]{:S(2)}) collective-permute-start(s32[12,12]{1,0:T(8,128)S(1)} %copy-done.1), channel_id=1, source_target_pairs={{0,2},{1,3},{2,0},{3,1},{4,6},{5,7},{6,4},{7,5},{8,10},{9,11},{10,... | collective-permute-start | bytes 1736 | tf_op jit(solution)/shard_map/ppermute | solution.py:157
  24.3 0.0 collective-permute-start.11
  24.3 0.0 collective-permute-done.8
  24.3 1.5 %collective-permute-start.9 = (s32[12,12]{1,0:T(8,128)S(1)}, s32[12,12]{1,0:T(8,128)S(1)}, u32[]{:S(2)}, u32[]{:S(2)}) collective-permute-start(s32[12,12]{1,0:T(8,128)S(1)} %copy-done.1), channel_id=1, source_target_pairs={{0,1},{1,0},{2,3},{3,2},{4,5},{5,4},{6,7},{7,6},{8,9},{9,8},{10,11... | collective-permute-start | bytes 1736 | tf_op jit(solution)/shard_map/ppermute | solution.py:157
  25.8 1.1 %collective-permute-done.10.refs_12_ = s32[12,12]{1,0:T(8,128)S(1)} collective-permute-done((s32[12,12]{1,0:T(8,128)S(1)}, s32[12,12]{1,0:T(8,128)S(1)}, u32[]{:S(2)}, u32[]{:S(2)}) %collective-permute-start.10) | collective-permute-done | bytes 608 | tf_op jit(solution)/shard_map/ppermute | solution.py:157
  26.9 0.0 collective-permute-start.5
  26.9 2.9 %collective-permute-done.11.refs_13_ = s32[12,12]{1,0:T(8,128)S(1)} collective-permute-done((s32[12,12]{1,0:T(8,128)S(1)}, s32[12,12]{1,0:T(8,128)S(1)}, u32[]{:S(2)}, u32[]{:S(2)}) %collective-permute-start.11) | collective-permute-done | bytes 608 | tf_op jit(solution)/shard_map/ppermute | solution.py:157
  29.8 0.0 collective-permute-done.9.refs_11_
  29.8 0.0 collective-permute-done.6.refs_6_
  29.8 0.1 select_select_fusion.refs_7_
  29.8 0.1 collective-permute-start.13
  29.9 0.5 %collective-permute-start.12 = (bf16[384,384]{1,0:T(8,128)(2,1)S(1)}, bf16[384,384]{1,0:T(8,128)(2,1)S(1)}, u32[]{:S(2)}, u32[]{:S(2)}) collective-permute-start(bf16[384,384]{1,0:T(8,128)(2,1)S(1)} %collective-permute-done.6.refs_6_), channel_id=1, source_target_pairs={{0,4},{1,5},{2,6},{3,7},{4,0},{5,1},{6,2},{7,3},{8,12},{9,13},{10,... | collective-permute-start | bytes 884744 | tf_op jit(solution)/shard_map/ppermute | solution.py:68
  30.4 0.7 %dynamic-slice_bitcast_fusion = s32[20]{0:T(128)S(1)} fusion(s32[16,20]{1,0:T(8,128)} %constant.19.clone, s32[]{:T(128)S(6)} %select_n.23), kind=kLoop, calls=%fused_computation.3 | loop fusion | bytes 164 | tf_op jit(solution)/shard_map/squeeze | solution.py:163
  31.1 0.1 pad_add_fusion.where
  31.2 0.0 collective-permute-done.5.refs_5_
  31.2 0.3 collective-permute-done.13.refs_9_
  31.5 0.4 %collective-permute-done.12.refs_8_ = bf16[384,384]{1,0:T(8,128)(2,1)S(1)} collective-permute-done((bf16[384,384]{1,0:T(8,128)(2,1)S(1)}, bf16[384,384]{1,0:T(8,128)(2,1)S(1)}, u32[]{:S(2)}, u32[]{:S(2)}) %collective-permute-start.12) | collective-permute-done | bytes 294944 | tf_op jit(solution)/shard_map/ppermute | solution.py:68
  31.9 5.5 %purify.1 = bf16[384,384]{1,0:T(8,128)(2,1)} custom-call(s32[22]{0:T(128)S(1)} %pad_add_fusion.where, bf16[384,384]{1,0:T(8,128)(2,1)S(1)} %copy-done, bf16[384,384]{1,0:T(8,128)(2,1)S(1)} %collective-permute-done.3.refs_1_, bf16[384,384]{1,0:T(8,128)(2,1)S(1)} %collective-permute-done.1.refs_2_, bf16[384,384]{1,0:T(8,128)(2,1)S(1)} %collective-permute-done.4.refs_3_, ...), custom_call_target="tpu_custom_call" | custom-call | tf_op jit(solution)/shard_map/purify/pallas_call | solution.py:166
  (5 shorter events, 0.0 us)
Async XLA Ops:
  0.0 10.2 %collective-permute-start.1 = (bf16[384,384]{1,0:T(8,128)(2,1)}, bf16[384,384]{1,0:T(8,128)(2,1)S(1)}, u32[]{:S(2)}, u32[]{:S(2)}) collective-permute-start(bf16[384,384]{1,0:T(8,128)(2,1)} %refs_0_.1), channel_id=1, source_target_pairs={{0,8},{1,9},{2,10},{3,11},{4,12},{5,13},{6,14},{7,15},{8,0},{9,1},... | collective-permute-start | bytes 884744 | tf_op jit(solution)/shard_map/ppermute | solution.py:68
  3.0 16.5 %collective-permute-start = (bf16[384,384]{1,0:T(8,128)(2,1)}, bf16[384,384]{1,0:T(8,128)(2,1)S(1)}, u32[]{:S(2)}, u32[]{:S(2)}) collective-permute-start(bf16[384,384]{1,0:T(8,128)(2,1)} %refs_0_.1), channel_id=1, source_target_pairs={{8,11},{9,15},{12,10},{13,14},{10,9},{14,13},{11,8},{15,12},{7,4},... | collective-permute-start | bytes 884744 | tf_op jit(solution)/shard_map/ppermute | solution.py:68
  6.6 12.9 %collective-permute-start.3 = (bf16[384,384]{1,0:T(8,128)(2,1)}, bf16[384,384]{1,0:T(8,128)(2,1)S(1)}, u32[]{:S(2)}, u32[]{:S(2)}) collective-permute-start(bf16[384,384]{1,0:T(8,128)(2,1)} %refs_0_.1), channel_id=1, source_target_pairs={{0,4},{1,5},{2,6},{3,7},{4,0},{5,1},{6,2},{7,3},{8,12},{9,13},{10,... | collective-permute-start | bytes 884744 | tf_op jit(solution)/shard_map/ppermute | solution.py:68
  6.6 15.7 %copy-start.1 = (s32[12,12]{1,0:T(8,128)S(1)}, s32[12,12]{1,0:T(8,128)}, u32[]{:S(2)}) copy-start(s32[12,12]{1,0:T(8,128)} %refs_10_) | copy-start | bytes 1732
  11.2 10.4 %collective-permute-start.2 = (bf16[384,384]{1,0:T(8,128)(2,1)S(1)}, bf16[384,384]{1,0:T(8,128)(2,1)S(1)}, u32[]{:S(2)}, u32[]{:S(2)}) collective-permute-start(bf16[384,384]{1,0:T(8,128)(2,1)S(1)} %broadcast_select_fusion), channel_id=1, source_target_pairs={{0,5},{2,7},{5,0},{7,2},{8,13},{10,15},{13,8},{15,10},{16,21},{18,... | collective-permute-start | bytes 884744 | tf_op jit(solution)/shard_map/ppermute | solution.py:68
  13.5 8.1 %collective-permute-start.4 = (bf16[384,384]{1,0:T(8,128)(2,1)S(1)}, bf16[384,384]{1,0:T(8,128)(2,1)S(1)}, u32[]{:S(2)}, u32[]{:S(2)}) collective-permute-start(bf16[384,384]{1,0:T(8,128)(2,1)S(1)} %collective-permute-done.1.refs_2_), channel_id=1, source_target_pairs={{0,4},{1,5},{2,6},{3,7},{4,0},{5,1},{6,2},{7,3},{8,12},{9,13},{10,... | collective-permute-start | bytes 884744 | tf_op jit(solution)/shard_map/ppermute | solution.py:68
  13.5 10.8 %collective-permute-start.8 = (bf16[384,384]{1,0:T(8,128)(2,1)S(1)}, bf16[384,384]{1,0:T(8,128)(2,1)S(1)}, u32[]{:S(2)}, u32[]{:S(2)}) collective-permute-start(bf16[384,384]{1,0:T(8,128)(2,1)S(1)} %collective-permute-done.1.refs_2_), channel_id=1, source_target_pairs={{2,4},{7,1},{8,14},{13,11},{18,20},{23,17},{24,30},{29,27}} | collective-permute-start | bytes 884744 | tf_op jit(solution)/shard_map/ppermute | solution.py:68
  21.6 8.2 %collective-permute-start.6 = (bf16[384,384]{1,0:T(8,128)(2,1)S(1)}, bf16[384,384]{1,0:T(8,128)(2,1)S(1)}, u32[]{:S(2)}, u32[]{:S(2)}) collective-permute-start(bf16[384,384]{1,0:T(8,128)(2,1)S(1)} %collective-permute-done.refs_4_), channel_id=1, source_target_pairs={{0,8},{1,9},{2,10},{3,11},{4,12},{5,13},{6,14},{7,15},{8,0},{9,1},... | collective-permute-start | bytes 884744 | tf_op jit(solution)/shard_map/ppermute | solution.py:68
  21.6 8.2 %collective-permute-start.7 = (bf16[384,384]{1,0:T(8,128)(2,1)S(1)}, bf16[384,384]{1,0:T(8,128)(2,1)S(1)}, u32[]{:S(2)}, u32[]{:S(2)}) collective-permute-start(bf16[384,384]{1,0:T(8,128)(2,1)S(1)} %collective-permute-done.refs_4_), channel_id=1, source_target_pairs={{3,6},{6,3},{9,12},{12,9},{19,22},{22,19},{25,28},{28,25}} | collective-permute-start | bytes 884744 | tf_op jit(solution)/shard_map/ppermute | solution.py:68
  22.2 4.6 %collective-permute-start.10 = (s32[12,12]{1,0:T(8,128)S(1)}, s32[12,12]{1,0:T(8,128)S(1)}, u32[]{:S(2)}, u32[]{:S(2)}) collective-permute-start(s32[12,12]{1,0:T(8,128)S(1)} %copy-done.1), channel_id=1, source_target_pairs={{0,2},{1,3},{2,0},{3,1},{4,6},{5,7},{6,4},{7,5},{8,10},{9,11},{10,... | collective-permute-start | bytes 1736 | tf_op jit(solution)/shard_map/ppermute | solution.py:157
  24.3 5.4 %collective-permute-start.11 = (s32[12,12]{1,0:T(8,128)S(1)}, s32[12,12]{1,0:T(8,128)S(1)}, u32[]{:S(2)}, u32[]{:S(2)}) collective-permute-start(s32[12,12]{1,0:T(8,128)S(1)} %copy-done.1), channel_id=1, source_target_pairs={{0,3},{1,2},{2,1},{3,0},{4,7},{5,6},{6,5},{7,4},{8,11},{9,10},{10,... | collective-permute-start | bytes 1736 | tf_op jit(solution)/shard_map/ppermute | solution.py:157
  24.3 5.4 %collective-permute-start.9 = (s32[12,12]{1,0:T(8,128)S(1)}, s32[12,12]{1,0:T(8,128)S(1)}, u32[]{:S(2)}, u32[]{:S(2)}) collective-permute-start(s32[12,12]{1,0:T(8,128)S(1)} %copy-done.1), channel_id=1, source_target_pairs={{0,1},{1,0},{2,3},{3,2},{4,5},{5,4},{6,7},{7,6},{8,9},{9,8},{10,11... | collective-permute-start | bytes 1736 | tf_op jit(solution)/shard_map/ppermute | solution.py:157
  25.8 6.1 %copy-start = (bf16[384,384]{1,0:T(8,128)(2,1)S(1)}, bf16[384,384]{1,0:T(8,128)(2,1)}, u32[]{:S(2)}) copy-start(bf16[384,384]{1,0:T(8,128)(2,1)} %refs_0_.1) | copy-start | bytes 884740
  26.9 4.3 %collective-permute-start.5 = (bf16[384,384]{1,0:T(8,128)(2,1)S(1)}, bf16[384,384]{1,0:T(8,128)(2,1)S(1)}, u32[]{:S(2)}, u32[]{:S(2)}) collective-permute-start(bf16[384,384]{1,0:T(8,128)(2,1)S(1)} %collective-permute-done.refs_4_), channel_id=1, source_target_pairs={{0,4},{1,5},{2,6},{3,7},{4,0},{5,1},{6,2},{7,3},{8,12},{9,13},{10,... | collective-permute-start | bytes 884744 | tf_op jit(solution)/shard_map/ppermute | solution.py:68
  29.8 1.6 %collective-permute-start.13 = (bf16[384,384]{1,0:T(8,128)(2,1)S(1)}, bf16[384,384]{1,0:T(8,128)(2,1)S(1)}, u32[]{:S(2)}, u32[]{:S(2)}) collective-permute-start(bf16[384,384]{1,0:T(8,128)(2,1)S(1)} %select_select_fusion.refs_7_), channel_id=1, source_target_pairs={{0,4},{1,5},{2,6},{3,7},{4,0},{5,1},{6,2},{7,3},{8,12},{9,13},{10,... | collective-permute-start | bytes 884744 | tf_op jit(solution)/shard_map/ppermute | solution.py:68
  29.9 2.0 %collective-permute-start.12 = (bf16[384,384]{1,0:T(8,128)(2,1)S(1)}, bf16[384,384]{1,0:T(8,128)(2,1)S(1)}, u32[]{:S(2)}, u32[]{:S(2)}) collective-permute-start(bf16[384,384]{1,0:T(8,128)(2,1)S(1)} %collective-permute-done.6.refs_6_), channel_id=1, source_target_pairs={{0,4},{1,5},{2,6},{3,7},{4,0},{5,1},{6,2},{7,3},{8,12},{9,13},{10,... | collective-permute-start | bytes 884744 | tf_op jit(solution)/shard_map/ppermute | solution.py:68

commit v3 on v2

--- a/solution.py
+++ b/solution.py
@@ -1,6 +1,5 @@
 import jax
 import jax.numpy as jnp
-import numpy as np
 from jax import lax
 from jax.experimental import pallas as pl
 from jax.experimental.pallas import tpu as pltpu
@@ -89,59 +88,135 @@
     theirs = [moved(names, CORES) for names in mine]
     order = [own, theirs[0], across, theirs[1], line, theirs[2]]
     order += [line_across, diagonal, theirs[3], theirs[4]]
-    table = np.array([[x[d] for x in order] for d in range(16)], np.int32)
     for d in range(16):
-        assert len({tuple(sorted(ab)) for ab in table[d].tolist()}) == 10
-    return table.reshape(16, 20)
-
-
-def purify_kernel(where, *refs):
-    blocks, patterns, out = refs[:10], refs[10:14], refs[14]
-    full, mask, square, low, sems = refs[15:]
+        assert len({tuple(sorted(names[d])) for names in order}) == 10
+    return order
+
+
+def spots(first, count, me):
+    order = whose_blocks()[first : first + count]
+    codes = [sum((4 * names[d][0] + names[d][1]) << 4 * k for k, names in enumerate(order)) for d in range(16)]
+    code = jnp.int32(codes[0])
+    for d in range(1, 16):
+        code = jnp.where(me == d, codes[d], code)
+    places = [jnp.bitwise_and(jnp.right_shift(code, 4 * k), 15) for k in range(count)]
+    return [(jnp.right_shift(p, 2), jnp.bitwise_and(p, 3)) for p in places]
+
+
+def block_at(edge, k):
+    return pl.ds(pl.multiple_of(k * edge, 128), edge)
+
+
+def place(first, blocks, full, sems):
+    edge = blocks[0].shape[0]
+    me = number(lax.axis_index("wide"), lax.axis_index("narrow"))
+    copies = []
+    for k, (a, b) in enumerate(spots(first, len(blocks), me)):
+        spot, image = (block_at(edge, a), block_at(edge, b)), (block_at(edge, b), block_at(edge, a))
+        copy = pltpu.make_async_copy(blocks[k], full.at[spot], sems.at[k])
+        copies.append((copy, a != b, spot, image))
+    for copy, *_ in copies:
+        copy.start()
+    return copies
+
+
+def mirror(copies, full):
+    for copy, off_diagonal, spot, image in copies:
+        copy.wait()
+
+        @pl.when(off_diagonal)
+        def _():
+            full[image] = full[spot].T
+
+
+def early_kernel(*refs):
+    blocks, full, sems = refs[:6], *refs[6:]
+    mirror(place(0, blocks, full, sems), full)
+
+
+def purify_kernel(full_in, *refs):
+    blocks, patterns = refs[:4], refs[4:8]
+    out, full, square, low, small, rows, sems = refs[8:]
     edge = out.shape[0]
     order = full.shape[0]
-    n = patterns[0].shape[0]
+    n = small.shape[1]
     step = edge // n
-    i, j = where[20], where[21]
-
-    def at(k):
-        return pl.ds(pl.multiple_of(k * edge, 128), edge)
-
-    def copy(k):
-        a, b = where[2 * k], where[2 * k + 1]
-        return pltpu.make_async_copy(blocks[k], full.at[at(a), at(b)], sems.at[k])
-
-    for k in range(10):
-        copy(k).start()
+    loads = [pltpu.make_async_copy(p, small.at[k], sems.at[4 + k]) for k, p in enumerate(patterns)]
+    for load in loads:
+        load.start()
+    copies = place(6, blocks, full, sems)
+    i, j = lax.axis_index("wide"), lax.axis_index("narrow")
     r = lax.broadcasted_iota(jnp.int32, (n, edge), 0)
     c = lax.broadcasted_iota(jnp.int32, (n, edge), 1)
     widen = jnp.where(r == c // step, 1.0, 0.0).astype(BF16)
-    for k, ref in enumerate(patterns):
-        rows = jnp.dot(ref[...].astype(BF16), widen, preferred_element_type=F32)
-        tall = jnp.broadcast_to(rows[:, None, :], (n, step, edge)).reshape(edge, edge)
-        mask[:, at(jnp.bitwise_xor(j, k))] = tall
-    for k in range(10):
-        a, b = where[2 * k], where[2 * k + 1]
-        copy(k).wait()
-
-        @pl.when(a != b)
-        def _():
-            full[at(b), at(a)] = full[at(a), at(b)].T
-
-    panel = full[at(i)]
+    for k, load in enumerate(loads):
+        load.wait()
+        wide = jnp.dot(small[k].astype(BF16), widen, preferred_element_type=F32)
+        rows[:, block_at(edge, jnp.bitwise_xor(j, k))] = wide
+    mirror(copies, full)
+
+    def masked(x, cols):
+        tall = x.reshape(n, step, x.shape[1]) * rows[:, cols][:, None, :]
+        return tall.reshape(x.shape)
+
+    panel = full[block_at(edge, i)]
     width = 256
     for t in range(order // width):
         cols = slice(t * width, (t + 1) * width)
-        s = jnp.dot(panel, full[:, cols], preferred_element_type=F32) * mask[:, cols]
+        s = masked(jnp.dot(panel, full[:, cols], preferred_element_type=F32), cols)
         square[:, cols] = s
         low[:, cols] = s.astype(BF16)
-    cube = jnp.dot(low[...], full[:, at(j)], preferred_element_type=F32) * mask[:, at(j)]
-    out[...] = (3.0 * square[:, at(j)] - 2.0 * cube).astype(BF16)
+    mine = block_at(edge, j)
+    cube = masked(jnp.dot(low[...], full[:, mine], preferred_element_type=F32), mine)
+    out[...] = (3.0 * square[:, mine] - 2.0 * cube).astype(BF16)
+
+
+VMEM = pl.BlockSpec(memory_space=pltpu.VMEM)
+HBM = pl.BlockSpec(memory_space=pl.ANY)
+PARAMS = pltpu.CompilerParams(vmem_limit_bytes=24 << 20)
+
+
+def in_hbm(array):
+    return pltpu.with_memory_space_constraint(array, pltpu.HBM)
+
+
+def early(blocks):
+    order = 4 * blocks[0].shape[0]
+    return pl.pallas_call(
+        early_kernel,
+        out_shape=pltpu.VMEM((order, order), BF16),
+        in_specs=[HBM] * 6,
+        out_specs=VMEM,
+        scratch_shapes=[pltpu.SemaphoreType.DMA((6,))],
+        compiler_params=PARAMS,
+        name="early",
+    )(*blocks)
+
+
+def purify(full, blocks, patterns):
+    order = full.shape[0]
+    edge = order // 4
+    n = patterns[0].shape[0]
+    full = pltpu.with_memory_space_constraint(full, pltpu.VMEM)
+    return pl.pallas_call(
+        purify_kernel,
+        out_shape=(jax.ShapeDtypeStruct((edge, edge), BF16), pltpu.VMEM((order, order), BF16)),
+        in_specs=[VMEM] + [HBM] * 8,
+        out_specs=(VMEM, VMEM),
+        input_output_aliases={0: 1},
+        scratch_shapes=[
+            pltpu.VMEM((edge, order), F32),
+            pltpu.VMEM((edge, order), BF16),
+            pltpu.VMEM((4, n, n), jnp.int32),
+            pltpu.VMEM((n, order), F32),
+            pltpu.SemaphoreType.DMA((8,)),
+        ],
+        compiler_params=PARAMS,
+        name="purify",
+    )(full, *blocks, *patterns)[0]
 
 
 def block_body(own, pattern):
-    edge = own.shape[0]
-    order = 4 * edge
     i, j = lax.axis_index("wide"), lax.axis_index("narrow")
     kind = jnp.bitwise_xor(i, j)
     hold = lax.optimization_barrier
@@ -149,40 +224,19 @@
     near = send(jnp.where(kind == 0, own, across), NEAR_DIAGONAL)
     far = send(across, FAR_DIAGONAL)
     own_c, across_c = send(own, CORES), send(across, CORES)
-    line, near, own_c, across_c = hold((line, near, own_c, across_c))
+    own_c, across_c, line = hold((own_c, across_c, line))
     line_across, last = send(line, ACROSS), send(line, LAST_DIAGONAL)
+    line_c = send(line, CORES)
     pattern, line = hold((pattern, line))
     patterns = [pattern]
     for k in (1, 2, 3):
         patterns.append(lax.ppermute(pattern, "narrow", [(c, c ^ k) for c in range(4)]))
-    line_across, last, far, patterns = hold((line_across, last, far, patterns))
+    full = early((own, own_c, across, across_c, line, line_c))
+    patterns, near, far, last, line_across, full = hold((patterns, near, far, last, line_across, full))
     diagonal = jnp.where(kind == 3, last, jnp.where(kind == 1, far, near))
-    line_c = send(line, CORES)
     line_across_c, diagonal_c = send(line_across, CORES), send(diagonal, CORES)
-    table = jnp.asarray(whose_blocks())
-    where = jnp.concatenate([table[number(i, j)], jnp.stack([i, j]).astype(jnp.int32)])
-    vmem = pl.BlockSpec(memory_space=pltpu.VMEM)
-    anywhere = pl.BlockSpec(memory_space=pl.ANY)
-    return pl.pallas_call(
-        purify_kernel,
-        out_shape=jax.ShapeDtypeStruct((edge, edge), BF16),
-        in_specs=[pl.BlockSpec(memory_space=pltpu.SMEM)] + [anywhere] * 10 + [vmem] * 4,
-        out_specs=vmem,
-        scratch_shapes=[
-            pltpu.VMEM((order, order), BF16),
-            pltpu.VMEM((edge, order), F32),
-            pltpu.VMEM((edge, order), F32),
-            pltpu.VMEM((edge, order), BF16),
-            pltpu.SemaphoreType.DMA((10,)),
-        ],
-        compiler_params=pltpu.CompilerParams(vmem_limit_bytes=40 << 20),
-        name="purify",
-    )(
-        where,
-        *(own, own_c, across, across_c, line, line_c),
-        *(line_across, diagonal, line_across_c, diagonal_c),
-        *patterns,
-    )
+    blocks = (line_across, diagonal, line_across_c, diagonal_c)
+    return purify(full, blocks, patterns)
 
 
 def solution(mesh):

time: 37.6 us -> 36.2 us (0.963)
  waiting for transfers between devices: 15.6 us -> 11.9 us
  starting transfers between devices: 14.4 us -> 16.8 us
    ppermute x3, waiting for transfers between devices: 3.96 us -> 1.35 us  [block_body(): lax.ppermute(pattern, 'narrow', [(c, c ^ k) for c in range(4)])]
    ppermute x11, starting transfers between devices: 10.8 us -> 12.4 us  [send(): return lax.ppermute(array, AXES, moves)]
    ppermute x11, waiting for transfers between devices: 11.7 us -> 10.6 us  [send(): return lax.ppermute(array, AXES, moves)]
    unnamed x4, local copies, waits for them, and re-layouts: 0.01 us -> 0.96 us
    ppermute x3, starting transfers between devices: 3.55 us -> 4.39 us  [block_body(): lax.ppermute(pattern, 'narrow', [(c, c ^ k) for c in range(4)])]
    squeeze x1 -> x0, local copies, waits for them, and re-layouts: 0.69 us -> none  [block_body(): table[number(i, j)]]
    pallas_call x1 -> x2, Pallas kernels: 5.49 us -> 5.16 us  [the longest x1 4.2 us: purify(): pl.pallas_call(purify_kernel, out_shape=(jax.ShapeDtypeStruct((edge, edge...]
  transfers between devices with their start and end apart: 14 -> 14, of which waited for: 7 -> 7; matrix products, arithmetic and copies ran while one was open for 5% -> 3% of each run, Pallas kernels for 0% -> 3%
where the time goes in v3:
time: 36.2 us; the launch traced here: 35.9 us
  starting transfers between devices  16.8 us (46%)
  waiting for transfers between devices  11.9 us (33%)
  Pallas kernels  5.16 us (14%)
  other arithmetic  1.05 us (3%)
  local copies, waits for them, and re-layouts  0.96 us (3%)
    ppermute x11, starting transfers between devices, send(): return lax.ppermute(array, AXES, moves)  12.4 us
    ppermute x11, waiting for transfers between devices, send(): return lax.ppermute(array, AXES, moves)  10.6 us
    ppermute x3, starting transfers between devices, block_body(): lax.ppermute(pattern, 'narrow', [(c, c ^ k) for c in range(4)])  4.39 us
    pallas_call x1, Pallas kernels, purify(): pl.pallas_call(purify_kernel, out_shape=(jax.ShapeDtypeStruct((edge, edge...  4.2 us
    ppermute x3, waiting for transfers between devices, block_body(): lax.ppermute(pattern, 'narrow', [(c, c ^ k) for c in range(4)])  1.35 us
    select_n x1, other arithmetic, block_body(): near = send(jnp.where(kind == 0, own, across), NEAR_DIAGONAL)  1 us
    unnamed x4, local copies, waits for them, and re-layouts  0.96 us
    pallas_call x1, Pallas kernels, early(): pl.pallas_call(early_kernel, out_shape=pltpu.VMEM((order, order), BF16),...  0.96 us
  transfers between devices with their start and end apart: 14, of which 7 were waited for; matrix products, arithmetic and copies ran while one was open for 3% of the time, Pallas kernels for 3%

profile of v3, /device:TPU:0, one launch (start us, length us, event | category | flops | bytes accessed | tf_op | source)
XLA Modules:
  0.0 35.9 jit_solution(4613753713354993992)
XLA Ops:
  0.0 3.0 %collective-permute-start.1 = (bf16[384,384]{1,0:T(8,128)(2,1)}, bf16[384,384]{1,0:T(8,128)(2,1)S(1)}, u32[]{:S(2)}, u32[]{:S(2)}) collective-permute-start(bf16[384,384]{1,0:T(8,128)(2,1)} %refs_0_.1), channel_id=1, source_target_pairs={{0,8},{1,9},{2,10},{3,11},{4,12},{5,13},{6,14},{7,15},{8,0},{9,1},... | collective-permute-start | bytes 884744 | tf_op jit(solution)/shard_map/ppermute | solution.py:67
  3.0 3.6 %collective-permute-start.3 = (bf16[384,384]{1,0:T(8,128)(2,1)}, bf16[384,384]{1,0:T(8,128)(2,1)S(1)}, u32[]{:S(2)}, u32[]{:S(2)}) collective-permute-start(bf16[384,384]{1,0:T(8,128)(2,1)} %refs_0_.1), channel_id=1, source_target_pairs={{8,11},{9,15},{12,10},{13,14},{10,9},{14,13},{11,8},{15,12},{7,4},... | collective-permute-start | bytes 884744 | tf_op jit(solution)/shard_map/ppermute | solution.py:67
  6.6 0.0 collective-permute-start
  6.6 3.6 %collective-permute-done.1.refs_2_ = bf16[384,384]{1,0:T(8,128)(2,1)S(1)} collective-permute-done((bf16[384,384]{1,0:T(8,128)(2,1)}, bf16[384,384]{1,0:T(8,128)(2,1)S(1)}, u32[]{:S(2)}, u32[]{:S(2)}) %collective-permute-start.1) | collective-permute-done | bytes 294944 | tf_op jit(solution)/shard_map/ppermute | solution.py:67
  10.2 0.0 collective-permute-start.2
  10.2 1.0 %broadcast_select_fusion = bf16[384,384]{1,0:T(8,128)(2,1)S(1)} fusion(bf16[384,384]{1,0:T(8,128)(2,1)} %refs_0_.1, bf16[384,384]{1,0:T(8,128)(2,1)S(1)} %collective-permute-done.1.refs_2_, pred[]{:T(512)S(6)} %eq.9), kind=kLoop, calls=%fused_computation.1 | loop fusion | flops 147456 | bytes 884737 | tf_op jit(solution)/shard_map/jit(_where)/select_n | solution.py:224
  11.2 3.8 %collective-permute-start.7 = (bf16[384,384]{1,0:T(8,128)(2,1)S(1)}, bf16[384,384]{1,0:T(8,128)(2,1)S(1)}, u32[]{:S(2)}, u32[]{:S(2)}) collective-permute-start(bf16[384,384]{1,0:T(8,128)(2,1)S(1)} %broadcast_select_fusion), channel_id=1, source_target_pairs={{0,5},{2,7},{5,0},{7,2},{8,13},{10,15},{13,8},{15,10},{16,21},{18,... | collective-permute-start | bytes 884744 | tf_op jit(solution)/shard_map/ppermute | solution.py:67
  15.0 0.7 %collective-permute-start.8 = (bf16[384,384]{1,0:T(8,128)(2,1)S(1)}, bf16[384,384]{1,0:T(8,128)(2,1)S(1)}, u32[]{:S(2)}, u32[]{:S(2)}) collective-permute-start(bf16[384,384]{1,0:T(8,128)(2,1)S(1)} %collective-permute-done.1.refs_2_), channel_id=1, source_target_pairs={{2,4},{7,1},{8,14},{13,11},{18,20},{23,17},{24,30},{29,27}} | collective-permute-start | bytes 884744 | tf_op jit(solution)/shard_map/ppermute | solution.py:67
  15.7 3.7 %collective-permute-done.3.refs_4_ = bf16[384,384]{1,0:T(8,128)(2,1)S(1)} collective-permute-done((bf16[384,384]{1,0:T(8,128)(2,1)}, bf16[384,384]{1,0:T(8,128)(2,1)S(1)}, u32[]{:S(2)}, u32[]{:S(2)}) %collective-permute-start.3) | collective-permute-done | bytes 294944 | tf_op jit(solution)/shard_map/ppermute | solution.py:67
  19.5 0.0 collective-permute-done.refs_1_
  19.5 0.0 collective-permute-done.2.refs_3_
  19.5 0.0 collective-permute-start.11
  19.5 0.1 collective-permute-start.10
  19.6 0.7 %collective-permute-start.9 = (bf16[384,384]{1,0:T(8,128)(2,1)S(1)}, bf16[384,384]{1,0:T(8,128)(2,1)S(1)}, u32[]{:S(2)}, u32[]{:S(2)}) collective-permute-start(bf16[384,384]{1,0:T(8,128)(2,1)S(1)} %collective-permute-done.3.refs_4_), channel_id=1, source_target_pairs={{3,6},{6,3},{9,12},{12,9},{19,22},{22,19},{25,28},{28,25}} | collective-permute-start | bytes 884744 | tf_op jit(solution)/shard_map/ppermute | solution.py:67
  20.2 1.7 %collective-permute-done.7 = bf16[384,384]{1,0:T(8,128)(2,1)S(1)} collective-permute-done((bf16[384,384]{1,0:T(8,128)(2,1)S(1)}, bf16[384,384]{1,0:T(8,128)(2,1)S(1)}, u32[]{:S(2)}, u32[]{:S(2)}) %collective-permute-start.7) | collective-permute-done | bytes 294944 | tf_op jit(solution)/shard_map/ppermute | solution.py:67
  21.9 2.2 %collective-permute-start.6 = (s32[12,12]{1,0:T(8,128)}, s32[12,12]{1,0:T(8,128)S(1)}, u32[]{:S(2)}, u32[]{:S(2)}) collective-permute-start(s32[12,12]{1,0:T(8,128)} %refs_4_), channel_id=1, source_target_pairs={{0,3},{1,2},{2,1},{3,0},{4,7},{5,6},{6,5},{7,4},{8,11},{9,10},{10,... | collective-permute-start | bytes 1736 | tf_op jit(solution)/shard_map/ppermute | solution.py:233
  24.1 0.0 collective-permute-done.8
  24.1 1.6 %collective-permute-start.5 = (s32[12,12]{1,0:T(8,128)}, s32[12,12]{1,0:T(8,128)S(1)}, u32[]{:S(2)}, u32[]{:S(2)}) collective-permute-start(s32[12,12]{1,0:T(8,128)} %refs_4_), channel_id=1, source_target_pairs={{0,2},{1,3},{2,0},{3,1},{4,6},{5,7},{6,4},{7,5},{8,10},{9,11},{10,... | collective-permute-start | bytes 1736 | tf_op jit(solution)/shard_map/ppermute | solution.py:233
  25.7 0.0 collective-permute-done.11.refs_5_
  25.8 0.6 %collective-permute-start.4 = (s32[12,12]{1,0:T(8,128)}, s32[12,12]{1,0:T(8,128)S(1)}, u32[]{:S(2)}, u32[]{:S(2)}) collective-permute-start(s32[12,12]{1,0:T(8,128)} %refs_4_), channel_id=1, source_target_pairs={{0,1},{1,0},{2,3},{3,2},{4,5},{5,4},{6,7},{7,6},{8,9},{9,8},{10,11... | collective-permute-start | bytes 1736 | tf_op jit(solution)/shard_map/ppermute | solution.py:233
  26.3 1.0 %copy-done = bf16[384,384]{1,0:T(8,128)(2,1)S(1)} copy-done((bf16[384,384]{1,0:T(8,128)(2,1)S(1)}, bf16[384,384]{1,0:T(8,128)(2,1)}, u32[]{:S(2)}) %copy-start) | copy-done | bytes 294936
  27.3 1.0 %early.1.full_in = bf16[1536,1536]{1,0:T(8,128)(2,1)S(1)} custom-call(bf16[384,384]{1,0:T(8,128)(2,1)S(1)} %copy-done, bf16[384,384]{1,0:T(8,128)(2,1)S(1)} %collective-permute-done.refs_1_, bf16[384,384]{1,0:T(8,128)(2,1)S(1)} %collective-permute-done.1.refs_2_, bf16[384,384]{1,0:T(8,128)(2,1)S(1)} %collective-permute-done.2.refs_3_, ...), custom_call_target="tpu_custom_call" | custom-call | tf_op jit(solution)/shard_map/early/pallas_call | solution.py:185
  28.3 0.7 %collective-permute-done.6.refs_7_ = s32[12,12]{1,0:T(8,128)S(1)} collective-permute-done((s32[12,12]{1,0:T(8,128)}, s32[12,12]{1,0:T(8,128)S(1)}, u32[]{:S(2)}, u32[]{:S(2)}) %collective-permute-start.6) | collective-permute-done | bytes 608 | tf_op jit(solution)/shard_map/ppermute | solution.py:233
  29.0 0.0 collective-permute-done.5.refs_6_
  29.0 0.6 %collective-permute-done.4.refs_5_ = s32[12,12]{1,0:T(8,128)S(1)} collective-permute-done((s32[12,12]{1,0:T(8,128)}, s32[12,12]{1,0:T(8,128)S(1)}, u32[]{:S(2)}, u32[]{:S(2)}) %collective-permute-start.4) | collective-permute-done | bytes 608 | tf_op jit(solution)/shard_map/ppermute | solution.py:233
  29.6 0.0 collective-permute-done.10.refs_0_
  29.6 0.0 collective-permute-done.9
  29.7 0.1 collective-permute-start.13
  29.8 0.5 %collective-permute-start.12 = (bf16[384,384]{1,0:T(8,128)(2,1)S(1)}, bf16[384,384]{1,0:T(8,128)(2,1)S(1)}, u32[]{:S(2)}, u32[]{:S(2)}) collective-permute-start(bf16[384,384]{1,0:T(8,128)(2,1)S(1)} %collective-permute-done.10.refs_0_), channel_id=1, source_target_pairs={{0,4},{1,5},{2,6},{3,7},{4,0},{5,1},{6,2},{7,3},{8,12},{9,13},{10,... | collective-permute-start | bytes 884744 | tf_op jit(solution)/shard_map/ppermute | solution.py:67
  30.3 1.1 %collective-permute-done.13.refs_3_ = bf16[384,384]{1,0:T(8,128)(2,1)S(1)} collective-permute-done((bf16[384,384]{1,0:T(8,128)(2,1)S(1)}, bf16[384,384]{1,0:T(8,128)(2,1)S(1)}, u32[]{:S(2)}, u32[]{:S(2)}) %collective-permute-start.13) | collective-permute-done | bytes 294944 | tf_op jit(solution)/shard_map/ppermute | solution.py:67
  31.3 0.4 %collective-permute-done.12.refs_2_ = bf16[384,384]{1,0:T(8,128)(2,1)S(1)} collective-permute-done((bf16[384,384]{1,0:T(8,128)(2,1)S(1)}, bf16[384,384]{1,0:T(8,128)(2,1)S(1)}, u32[]{:S(2)}, u32[]{:S(2)}) %collective-permute-start.12) | collective-permute-done | bytes 294944 | tf_op jit(solution)/shard_map/ppermute | solution.py:67
  31.7 4.2 %purify.1 = (bf16[384,384]{1,0:T(8,128)(2,1)}, bf16[1536,1536]{1,0:T(8,128)(2,1)S(1)}) custom-call(bf16[1536,1536]{1,0:T(8,128)(2,1)S(1)} %early.1.full_in, bf16[384,384]{1,0:T(8,128)(2,1)S(1)} %collective-permute-done.10.refs_0_, bf16[384,384]{1,0:T(8,128)(2,1)S(1)} %select_select_fusion.refs_1_, ...), custom_call_target="tpu_custom_call", output_to_operand_aliasing={{1}: (0, {})} | custom-call | tf_op jit(solution)/shard_map/purify/pallas_call | solution.py:201
  (4 shorter events, 0.1 us)
Async XLA Ops:
  0.0 31.7 %copy-start.1 = (s32[12,12]{1,0:T(8,128)S(1)}, s32[12,12]{1,0:T(8,128)}, u32[]{:S(2)}) copy-start(s32[12,12]{1,0:T(8,128)} %refs_4_) | copy-start | bytes 1732
  0.0 10.2 %collective-permute-start.1 = (bf16[384,384]{1,0:T(8,128)(2,1)}, bf16[384,384]{1,0:T(8,128)(2,1)S(1)}, u32[]{:S(2)}, u32[]{:S(2)}) collective-permute-start(bf16[384,384]{1,0:T(8,128)(2,1)} %refs_0_.1), channel_id=1, source_target_pairs={{0,8},{1,9},{2,10},{3,11},{4,12},{5,13},{6,14},{7,15},{8,0},{9,1},... | collective-permute-start | bytes 884744 | tf_op jit(solution)/shard_map/ppermute | solution.py:67
  3.0 16.5 %collective-permute-start.3 = (bf16[384,384]{1,0:T(8,128)(2,1)}, bf16[384,384]{1,0:T(8,128)(2,1)S(1)}, u32[]{:S(2)}, u32[]{:S(2)}) collective-permute-start(bf16[384,384]{1,0:T(8,128)(2,1)} %refs_0_.1), channel_id=1, source_target_pairs={{8,11},{9,15},{12,10},{13,14},{10,9},{14,13},{11,8},{15,12},{7,4},... | collective-permute-start | bytes 884744 | tf_op jit(solution)/shard_map/ppermute | solution.py:67
  6.6 12.9 %collective-permute-start = (bf16[384,384]{1,0:T(8,128)(2,1)}, bf16[384,384]{1,0:T(8,128)(2,1)S(1)}, u32[]{:S(2)}, u32[]{:S(2)}) collective-permute-start(bf16[384,384]{1,0:T(8,128)(2,1)} %refs_0_.1), channel_id=1, source_target_pairs={{0,4},{1,5},{2,6},{3,7},{4,0},{5,1},{6,2},{7,3},{8,12},{9,13},{10,... | collective-permute-start | bytes 884744 | tf_op jit(solution)/shard_map/ppermute | solution.py:67
  10.2 9.3 %collective-permute-start.2 = (bf16[384,384]{1,0:T(8,128)(2,1)S(1)}, bf16[384,384]{1,0:T(8,128)(2,1)S(1)}, u32[]{:S(2)}, u32[]{:S(2)}) collective-permute-start(bf16[384,384]{1,0:T(8,128)(2,1)S(1)} %collective-permute-done.1.refs_2_), channel_id=1, source_target_pairs={{0,4},{1,5},{2,6},{3,7},{4,0},{5,1},{6,2},{7,3},{8,12},{9,13},{10,... | collective-permute-start | bytes 884744 | tf_op jit(solution)/shard_map/ppermute | solution.py:67
  11.2 10.7 %collective-permute-start.7 = (bf16[384,384]{1,0:T(8,128)(2,1)S(1)}, bf16[384,384]{1,0:T(8,128)(2,1)S(1)}, u32[]{:S(2)}, u32[]{:S(2)}) collective-permute-start(bf16[384,384]{1,0:T(8,128)(2,1)S(1)} %broadcast_select_fusion), channel_id=1, source_target_pairs={{0,5},{2,7},{5,0},{7,2},{8,13},{10,15},{13,8},{15,10},{16,21},{18,... | collective-permute-start | bytes 884744 | tf_op jit(solution)/shard_map/ppermute | solution.py:67
  15.0 9.1 %collective-permute-start.8 = (bf16[384,384]{1,0:T(8,128)(2,1)S(1)}, bf16[384,384]{1,0:T(8,128)(2,1)S(1)}, u32[]{:S(2)}, u32[]{:S(2)}) collective-permute-start(bf16[384,384]{1,0:T(8,128)(2,1)S(1)} %collective-permute-done.1.refs_2_), channel_id=1, source_target_pairs={{2,4},{7,1},{8,14},{13,11},{18,20},{23,17},{24,30},{29,27}} | collective-permute-start | bytes 884744 | tf_op jit(solution)/shard_map/ppermute | solution.py:67
  19.5 6.3 %collective-permute-start.11 = (bf16[384,384]{1,0:T(8,128)(2,1)S(1)}, bf16[384,384]{1,0:T(8,128)(2,1)S(1)}, u32[]{:S(2)}, u32[]{:S(2)}) collective-permute-start(bf16[384,384]{1,0:T(8,128)(2,1)S(1)} %collective-permute-done.3.refs_4_), channel_id=1, source_target_pairs={{0,4},{1,5},{2,6},{3,7},{4,0},{5,1},{6,2},{7,3},{8,12},{9,13},{10,... | collective-permute-start | bytes 884744 | tf_op jit(solution)/shard_map/ppermute | solution.py:67
  19.5 10.1 %collective-permute-start.10 = (bf16[384,384]{1,0:T(8,128)(2,1)S(1)}, bf16[384,384]{1,0:T(8,128)(2,1)S(1)}, u32[]{:S(2)}, u32[]{:S(2)}) collective-permute-start(bf16[384,384]{1,0:T(8,128)(2,1)S(1)} %collective-permute-done.3.refs_4_), channel_id=1, source_target_pairs={{0,8},{1,9},{2,10},{3,11},{4,12},{5,13},{6,14},{7,15},{8,0},{9,1},... | collective-permute-start | bytes 884744 | tf_op jit(solution)/shard_map/ppermute | solution.py:67
  19.6 10.1 %collective-permute-start.9 = (bf16[384,384]{1,0:T(8,128)(2,1)S(1)}, bf16[384,384]{1,0:T(8,128)(2,1)S(1)}, u32[]{:S(2)}, u32[]{:S(2)}) collective-permute-start(bf16[384,384]{1,0:T(8,128)(2,1)S(1)} %collective-permute-done.3.refs_4_), channel_id=1, source_target_pairs={{3,6},{6,3},{9,12},{12,9},{19,22},{22,19},{25,28},{28,25}} | collective-permute-start | bytes 884744 | tf_op jit(solution)/shard_map/ppermute | solution.py:67
  21.9 7.1 %collective-permute-start.6 = (s32[12,12]{1,0:T(8,128)}, s32[12,12]{1,0:T(8,128)S(1)}, u32[]{:S(2)}, u32[]{:S(2)}) collective-permute-start(s32[12,12]{1,0:T(8,128)} %refs_4_), channel_id=1, source_target_pairs={{0,3},{1,2},{2,1},{3,0},{4,7},{5,6},{6,5},{7,4},{8,11},{9,10},{10,... | collective-permute-start | bytes 1736 | tf_op jit(solution)/shard_map/ppermute | solution.py:233
  24.1 4.9 %collective-permute-start.5 = (s32[12,12]{1,0:T(8,128)}, s32[12,12]{1,0:T(8,128)S(1)}, u32[]{:S(2)}, u32[]{:S(2)}) collective-permute-start(s32[12,12]{1,0:T(8,128)} %refs_4_), channel_id=1, source_target_pairs={{0,2},{1,3},{2,0},{3,1},{4,6},{5,7},{6,4},{7,5},{8,10},{9,11},{10,... | collective-permute-start | bytes 1736 | tf_op jit(solution)/shard_map/ppermute | solution.py:233
  25.8 3.9 %collective-permute-start.4 = (s32[12,12]{1,0:T(8,128)}, s32[12,12]{1,0:T(8,128)S(1)}, u32[]{:S(2)}, u32[]{:S(2)}) collective-permute-start(s32[12,12]{1,0:T(8,128)} %refs_4_), channel_id=1, source_target_pairs={{0,1},{1,0},{2,3},{3,2},{4,5},{5,4},{6,7},{7,6},{8,9},{9,8},{10,11... | collective-permute-start | bytes 1736 | tf_op jit(solution)/shard_map/ppermute | solution.py:233
  26.3 1.0 %copy-start = (bf16[384,384]{1,0:T(8,128)(2,1)S(1)}, bf16[384,384]{1,0:T(8,128)(2,1)}, u32[]{:S(2)}) copy-start(bf16[384,384]{1,0:T(8,128)(2,1)} %refs_0_.1) | copy-start | bytes 884740
  29.7 1.6 %collective-permute-start.13 = (bf16[384,384]{1,0:T(8,128)(2,1)S(1)}, bf16[384,384]{1,0:T(8,128)(2,1)S(1)}, u32[]{:S(2)}, u32[]{:S(2)}) collective-permute-start(bf16[384,384]{1,0:T(8,128)(2,1)S(1)} %select_select_fusion.refs_1_), channel_id=1, source_target_pairs={{0,4},{1,5},{2,6},{3,7},{4,0},{5,1},{6,2},{7,3},{8,12},{9,13},{10,... | collective-permute-start | bytes 884744 | tf_op jit(solution)/shard_map/ppermute | solution.py:67
  29.8 2.0 %collective-permute-start.12 = (bf16[384,384]{1,0:T(8,128)(2,1)S(1)}, bf16[384,384]{1,0:T(8,128)(2,1)S(1)}, u32[]{:S(2)}, u32[]{:S(2)}) collective-permute-start(bf16[384,384]{1,0:T(8,128)(2,1)S(1)} %collective-permute-done.10.refs_0_), channel_id=1, source_target_pairs={{0,4},{1,5},{2,6},{3,7},{4,0},{5,1},{6,2},{7,3},{8,12},{9,13},{10,... | collective-permute-start | bytes 884744 | tf_op jit(solution)/shard_map/ppermute | solution.py:67

commit v4 on v3

--- a/solution.py
+++ b/solution.py
@@ -86,8 +86,7 @@
     diagonal = [(near, far, near, last)[kind[d]][d] for d in range(16)]
     mine = [own, across, line, line_across, diagonal]
     theirs = [moved(names, CORES) for names in mine]
-    order = [own, theirs[0], across, theirs[1], line, theirs[2]]
-    order += [line_across, diagonal, theirs[3], theirs[4]]
+    order = [own, theirs[0], across, theirs[1], line, theirs[2], line_across, diagonal, theirs[3], theirs[4]]
     for d in range(16):
         assert len({tuple(sorted(names[d])) for names in order}) == 10
     return order
@@ -130,21 +129,22 @@
 
 
 def early_kernel(*refs):
-    blocks, full, sems = refs[:6], *refs[6:]
+    blocks, full, sems = refs[:-2], *refs[-2:]
     mirror(place(0, blocks, full, sems), full)
 
 
 def purify_kernel(full_in, *refs):
-    blocks, patterns = refs[:4], refs[4:8]
-    out, full, square, low, small, rows, sems = refs[8:]
+    blocks, patterns = refs[:-11], refs[-11:-7]
+    out, full, square, low, small, rows, sems = refs[-7:]
+    late = len(blocks)
     edge = out.shape[0]
     order = full.shape[0]
     n = small.shape[1]
     step = edge // n
-    loads = [pltpu.make_async_copy(p, small.at[k], sems.at[4 + k]) for k, p in enumerate(patterns)]
+    loads = [pltpu.make_async_copy(p, small.at[k], sems.at[late + k]) for k, p in enumerate(patterns)]
     for load in loads:
         load.start()
-    copies = place(6, blocks, full, sems)
+    copies = place(10 - late, blocks, full, sems)
     i, j = lax.axis_index("wide"), lax.axis_index("narrow")
     r = lax.broadcasted_iota(jnp.int32, (n, edge), 0)
     c = lax.broadcasted_iota(jnp.int32, (n, edge), 1)
@@ -185,9 +185,9 @@
     return pl.pallas_call(
         early_kernel,
         out_shape=pltpu.VMEM((order, order), BF16),
-        in_specs=[HBM] * 6,
+        in_specs=[HBM] * len(blocks),
         out_specs=VMEM,
-        scratch_shapes=[pltpu.SemaphoreType.DMA((6,))],
+        scratch_shapes=[pltpu.SemaphoreType.DMA((len(blocks),))],
         compiler_params=PARAMS,
         name="early",
     )(*blocks)
@@ -201,7 +201,7 @@
     return pl.pallas_call(
         purify_kernel,
         out_shape=(jax.ShapeDtypeStruct((edge, edge), BF16), pltpu.VMEM((order, order), BF16)),
-        in_specs=[VMEM] + [HBM] * 8,
+        in_specs=[VMEM] + [HBM] * (len(blocks) + 4),
         out_specs=(VMEM, VMEM),
         input_output_aliases={0: 1},
         scratch_shapes=[
@@ -209,7 +209,7 @@
             pltpu.VMEM((edge, order), BF16),
             pltpu.VMEM((4, n, n), jnp.int32),
             pltpu.VMEM((n, order), F32),
-            pltpu.SemaphoreType.DMA((8,)),
+            pltpu.SemaphoreType.DMA((len(blocks) + 4,)),
         ],
         compiler_params=PARAMS,
         name="purify",
@@ -228,13 +228,14 @@
     line_across, last = send(line, ACROSS), send(line, LAST_DIAGONAL)
     line_c = send(line, CORES)
     pattern, line = hold((pattern, line))
-    patterns = [pattern]
-    for k in (1, 2, 3):
-        patterns.append(lax.ppermute(pattern, "narrow", [(c, c ^ k) for c in range(4)]))
-    full = early((own, own_c, across, across_c, line, line_c))
-    patterns, near, far, last, line_across, full = hold((patterns, near, far, last, line_across, full))
+    got = {k: lax.ppermute(pattern, "narrow", [(c, c ^ k) for c in range(4)]) for k in (1, 2, 3)}
+    patterns = [pattern, got[1], got[2], got[3]]
+    full = early((own, own_c, across, across_c, line, line_c,))
+    patterns, full = hold((patterns, full))
+    line_across, full = hold((line_across, full))
+    line_across_c = send(line_across, CORES)
     diagonal = jnp.where(kind == 3, last, jnp.where(kind == 1, far, near))
-    line_across_c, diagonal_c = send(line_across, CORES), send(diagonal, CORES)
+    diagonal_c = send(diagonal, CORES)
     blocks = (line_across, diagonal, line_across_c, diagonal_c)
     return purify(full, blocks, patterns)
 

time: 36.2 us -> 35.6 us (0.983)
  waiting for transfers between devices: 11.9 us -> 9.95 us
  starting transfers between devices: 16.8 us -> 18.2 us
    ppermute x11, waiting for transfers between devices: 10.6 us -> 9.07 us  [send(): return lax.ppermute(array, AXES, moves)]
    ppermute x11, starting transfers between devices: 12.4 us -> 13.8 us  [send(): return lax.ppermute(array, AXES, moves)]
    ppermute x3, waiting for transfers between devices: 1.35 us -> 0.89 us  [block_body(): lax.ppermute(pattern, 'narrow', [(c, c ^ k) for c in range(4)])]
  transfers between devices with their start and end apart: 14 -> 14, of which waited for: 7 -> 5; matrix products, arithmetic and copies ran while one was open for 3% -> 3% of each run, Pallas kernels for 3% -> 3%
where the time goes in v4:
time: 35.6 us; the launch traced here: 35.4 us
  starting transfers between devices  18.2 us (51%)
  waiting for transfers between devices  9.95 us (28%)
  Pallas kernels  5.16 us (14%)
  other arithmetic  1.05 us (3%)
  local copies, waits for them, and re-layouts  0.96 us (3%)
    ppermute x11, starting transfers between devices, send(): return lax.ppermute(array, AXES, moves)  13.8 us
    ppermute x11, waiting for transfers between devices, send(): return lax.ppermute(array, AXES, moves)  9.07 us
    ppermute x3, starting transfers between devices, block_body(): lax.ppermute(pattern, 'narrow', [(c, c ^ k) for c in range(4)])  4.39 us
    pallas_call x1, Pallas kernels, purify(): pl.pallas_call(purify_kernel, out_shape=(jax.ShapeDtypeStruct((edge, edge...  4.2 us
    select_n x1, other arithmetic, block_body(): near = send(jnp.where(kind == 0, own, across), NEAR_DIAGONAL)  1 us
    pallas_call x1, Pallas kernels, early(): pl.pallas_call(early_kernel, out_shape=pltpu.VMEM((order, order), BF16),...  0.96 us
    unnamed x4, local copies, waits for them, and re-layouts  0.96 us
    ppermute x3, waiting for transfers between devices, block_body(): lax.ppermute(pattern, 'narrow', [(c, c ^ k) for c in range(4)])  0.89 us
  transfers between devices with their start and end apart: 14, of which 5 were waited for; matrix products, arithmetic and copies ran while one was open for 3% of the time, Pallas kernels for 3%

profile of v4, /device:TPU:0, one launch (start us, length us, event | category | flops | bytes accessed | tf_op | source)
XLA Modules:
  0.0 35.4 jit_solution(6303647091814047179)
XLA Ops:
  0.0 3.0 %collective-permute-start.1 = (bf16[384,384]{1,0:T(8,128)(2,1)}, bf16[384,384]{1,0:T(8,128)(2,1)S(1)}, u32[]{:S(2)}, u32[]{:S(2)}) collective-permute-start(bf16[384,384]{1,0:T(8,128)(2,1)} %refs_0_.1), channel_id=1, source_target_pairs={{0,8},{1,9},{2,10},{3,11},{4,12},{5,13},{6,14},{7,15},{8,0},{9,1},... | collective-permute-start | bytes 884744 | tf_op jit(solution)/shard_map/ppermute | solution.py:67
  3.0 3.6 %collective-permute-start.3 = (bf16[384,384]{1,0:T(8,128)(2,1)}, bf16[384,384]{1,0:T(8,128)(2,1)S(1)}, u32[]{:S(2)}, u32[]{:S(2)}) collective-permute-start(bf16[384,384]{1,0:T(8,128)(2,1)} %refs_0_.1), channel_id=1, source_target_pairs={{8,11},{9,15},{12,10},{13,14},{10,9},{14,13},{11,8},{15,12},{7,4},... | collective-permute-start | bytes 884744 | tf_op jit(solution)/shard_map/ppermute | solution.py:67
  6.6 0.0 collective-permute-start
  6.6 3.6 %collective-permute-done.1.refs_2_ = bf16[384,384]{1,0:T(8,128)(2,1)S(1)} collective-permute-done((bf16[384,384]{1,0:T(8,128)(2,1)}, bf16[384,384]{1,0:T(8,128)(2,1)S(1)}, u32[]{:S(2)}, u32[]{:S(2)}) %collective-permute-start.1) | collective-permute-done | bytes 294944 | tf_op jit(solution)/shard_map/ppermute | solution.py:67
  10.2 0.0 collective-permute-start.2
  10.2 1.0 %broadcast_select_fusion = bf16[384,384]{1,0:T(8,128)(2,1)S(1)} fusion(bf16[384,384]{1,0:T(8,128)(2,1)} %refs_0_.1, bf16[384,384]{1,0:T(8,128)(2,1)S(1)} %collective-permute-done.1.refs_2_, pred[]{:T(512)S(6)} %eq.11), kind=kLoop, calls=%fused_computation.1 | loop fusion | flops 147456 | bytes 884737 | tf_op jit(solution)/shard_map/jit(_where)/select_n | solution.py:224
  11.2 3.8 %collective-permute-start.11 = (bf16[384,384]{1,0:T(8,128)(2,1)S(1)}, bf16[384,384]{1,0:T(8,128)(2,1)S(1)}, u32[]{:S(2)}, u32[]{:S(2)}) collective-permute-start(bf16[384,384]{1,0:T(8,128)(2,1)S(1)} %broadcast_select_fusion), channel_id=1, source_target_pairs={{0,5},{2,7},{5,0},{7,2},{8,13},{10,15},{13,8},{15,10},{16,21},{18,... | collective-permute-start | bytes 884744 | tf_op jit(solution)/shard_map/ppermute | solution.py:67
  15.0 0.7 %collective-permute-start.10 = (bf16[384,384]{1,0:T(8,128)(2,1)S(1)}, bf16[384,384]{1,0:T(8,128)(2,1)S(1)}, u32[]{:S(2)}, u32[]{:S(2)}) collective-permute-start(bf16[384,384]{1,0:T(8,128)(2,1)S(1)} %collective-permute-done.1.refs_2_), channel_id=1, source_target_pairs={{2,4},{7,1},{8,14},{13,11},{18,20},{23,17},{24,30},{29,27}} | collective-permute-start | bytes 884744 | tf_op jit(solution)/shard_map/ppermute | solution.py:67
  15.7 3.7 %collective-permute-done.3.refs_4_ = bf16[384,384]{1,0:T(8,128)(2,1)S(1)} collective-permute-done((bf16[384,384]{1,0:T(8,128)(2,1)}, bf16[384,384]{1,0:T(8,128)(2,1)S(1)}, u32[]{:S(2)}, u32[]{:S(2)}) %collective-permute-start.3) | collective-permute-done | bytes 294944 | tf_op jit(solution)/shard_map/ppermute | solution.py:67
  19.5 0.0 collective-permute-done.refs_1_
  19.5 0.0 collective-permute-done.2.refs_3_
  19.5 0.7 %collective-permute-start.9 = (bf16[384,384]{1,0:T(8,128)(2,1)S(1)}, bf16[384,384]{1,0:T(8,128)(2,1)S(1)}, u32[]{:S(2)}, u32[]{:S(2)}) collective-permute-start(bf16[384,384]{1,0:T(8,128)(2,1)S(1)} %collective-permute-done.3.refs_4_), channel_id=1, source_target_pairs={{3,6},{6,3},{9,12},{12,9},{19,22},{22,19},{25,28},{28,25}} | collective-permute-start | bytes 884744 | tf_op jit(solution)/shard_map/ppermute | solution.py:67
  20.1 0.1 collective-permute-start.8
  20.2 1.9 %collective-permute-start.4 = (bf16[384,384]{1,0:T(8,128)(2,1)S(1)}, bf16[384,384]{1,0:T(8,128)(2,1)S(1)}, u32[]{:S(2)}, u32[]{:S(2)}) collective-permute-start(bf16[384,384]{1,0:T(8,128)(2,1)S(1)} %collective-permute-done.3.refs_4_), channel_id=1, source_target_pairs={{0,8},{1,9},{2,10},{3,11},{4,12},{5,13},{6,14},{7,15},{8,0},{9,1},... | collective-permute-start | bytes 884744 | tf_op jit(solution)/shard_map/ppermute | solution.py:67
  22.1 0.0 collective-permute-done.11
  22.1 0.4 %collective-permute-start.7 = (s32[12,12]{1,0:T(8,128)}, s32[12,12]{1,0:T(8,128)S(1)}, u32[]{:S(2)}, u32[]{:S(2)}) collective-permute-start(s32[12,12]{1,0:T(8,128)} %refs_4_), channel_id=1, source_target_pairs={{0,3},{1,2},{2,1},{3,0},{4,7},{5,6},{6,5},{7,4},{8,11},{9,10},{10,... | collective-permute-start | bytes 1736 | tf_op jit(solution)/shard_map/ppermute | solution.py:231
  22.5 0.0 collective-permute-done.10
  22.5 3.1 %collective-permute-start.6 = (s32[12,12]{1,0:T(8,128)}, s32[12,12]{1,0:T(8,128)S(1)}, u32[]{:S(2)}, u32[]{:S(2)}) collective-permute-start(s32[12,12]{1,0:T(8,128)} %refs_4_), channel_id=1, source_target_pairs={{0,2},{1,3},{2,0},{3,1},{4,6},{5,7},{6,4},{7,5},{8,10},{9,11},{10,... | collective-permute-start | bytes 1736 | tf_op jit(solution)/shard_map/ppermute | solution.py:231
  25.7 0.0 collective-permute-done.9
  25.7 0.9 %collective-permute-start.5 = (s32[12,12]{1,0:T(8,128)}, s32[12,12]{1,0:T(8,128)S(1)}, u32[]{:S(2)}, u32[]{:S(2)}) collective-permute-start(s32[12,12]{1,0:T(8,128)} %refs_4_), channel_id=1, source_target_pairs={{0,1},{1,0},{2,3},{3,2},{4,5},{5,4},{6,7},{7,6},{8,9},{9,8},{10,11... | collective-permute-start | bytes 1736 | tf_op jit(solution)/shard_map/ppermute | solution.py:231
  26.6 0.0 collective-permute-done.8.refs_5_
  26.6 0.1 collective-permute-start.13
  26.7 0.0 copy-start
  26.7 1.0 %copy-done = bf16[384,384]{1,0:T(8,128)(2,1)S(1)} copy-done((bf16[384,384]{1,0:T(8,128)(2,1)S(1)}, bf16[384,384]{1,0:T(8,128)(2,1)}, u32[]{:S(2)}) %copy-start) | copy-done | bytes 294936
  27.7 1.0 %early.1.full_in = bf16[1536,1536]{1,0:T(8,128)(2,1)S(1)} custom-call(bf16[384,384]{1,0:T(8,128)(2,1)S(1)} %copy-done, bf16[384,384]{1,0:T(8,128)(2,1)S(1)} %collective-permute-done.refs_1_, bf16[384,384]{1,0:T(8,128)(2,1)S(1)} %collective-permute-done.1.refs_2_, bf16[384,384]{1,0:T(8,128)(2,1)S(1)} %collective-permute-done.2.refs_3_, ...), custom_call_target="tpu_custom_call" | custom-call | tf_op jit(solution)/shard_map/early/pallas_call | solution.py:185
  28.6 0.0 collective-permute-done.7.refs_7_
  28.6 0.0 collective-permute-done.6.refs_6_
  28.6 0.9 %collective-permute-done.5.refs_5_ = s32[12,12]{1,0:T(8,128)S(1)} collective-permute-done((s32[12,12]{1,0:T(8,128)}, s32[12,12]{1,0:T(8,128)S(1)}, u32[]{:S(2)}, u32[]{:S(2)}) %collective-permute-start.5) | collective-permute-done | bytes 608 | tf_op jit(solution)/shard_map/ppermute | solution.py:231
  29.5 0.1 collective-permute-done.4.refs_0_
  29.6 0.0 collective-permute-start.12
  29.7 1.6 %collective-permute-done.12.refs_2_ = bf16[384,384]{1,0:T(8,128)(2,1)S(1)} collective-permute-done((bf16[384,384]{1,0:T(8,128)(2,1)S(1)}, bf16[384,384]{1,0:T(8,128)(2,1)S(1)}, u32[]{:S(2)}, u32[]{:S(2)}) %collective-permute-start.12) | collective-permute-done | bytes 294944 | tf_op jit(solution)/shard_map/ppermute | solution.py:67
  31.2 4.2 %purify.1 = (bf16[384,384]{1,0:T(8,128)(2,1)}, bf16[1536,1536]{1,0:T(8,128)(2,1)S(1)}) custom-call(bf16[1536,1536]{1,0:T(8,128)(2,1)S(1)} %early.1.full_in, bf16[384,384]{1,0:T(8,128)(2,1)S(1)} %collective-permute-done.4.refs_0_, bf16[384,384]{1,0:T(8,128)(2,1)S(1)} %select_select_fusion.refs_1_, ...), custom_call_target="tpu_custom_call", output_to_operand_aliasing={{1}: (0, {})} | custom-call | tf_op jit(solution)/shard_map/purify/pallas_call | solution.py:201
  (4 shorter events, 0.1 us)
Async XLA Ops:
  0.0 31.2 %copy-start.1 = (s32[12,12]{1,0:T(8,128)S(1)}, s32[12,12]{1,0:T(8,128)}, u32[]{:S(2)}) copy-start(s32[12,12]{1,0:T(8,128)} %refs_4_) | copy-start | bytes 1732
  0.0 10.2 %collective-permute-start.1 = (bf16[384,384]{1,0:T(8,128)(2,1)}, bf16[384,384]{1,0:T(8,128)(2,1)S(1)}, u32[]{:S(2)}, u32[]{:S(2)}) collective-permute-start(bf16[384,384]{1,0:T(8,128)(2,1)} %refs_0_.1), channel_id=1, source_target_pairs={{0,8},{1,9},{2,10},{3,11},{4,12},{5,13},{6,14},{7,15},{8,0},{9,1},... | collective-permute-start | bytes 884744 | tf_op jit(solution)/shard_map/ppermute | solution.py:67
  3.0 16.5 %collective-permute-start.3 = (bf16[384,384]{1,0:T(8,128)(2,1)}, bf16[384,384]{1,0:T(8,128)(2,1)S(1)}, u32[]{:S(2)}, u32[]{:S(2)}) collective-permute-start(bf16[384,384]{1,0:T(8,128)(2,1)} %refs_0_.1), channel_id=1, source_target_pairs={{8,11},{9,15},{12,10},{13,14},{10,9},{14,13},{11,8},{15,12},{7,4},... | collective-permute-start | bytes 884744 | tf_op jit(solution)/shard_map/ppermute | solution.py:67
  6.6 12.9 %collective-permute-start = (bf16[384,384]{1,0:T(8,128)(2,1)}, bf16[384,384]{1,0:T(8,128)(2,1)S(1)}, u32[]{:S(2)}, u32[]{:S(2)}) collective-permute-start(bf16[384,384]{1,0:T(8,128)(2,1)} %refs_0_.1), channel_id=1, source_target_pairs={{0,4},{1,5},{2,6},{3,7},{4,0},{5,1},{6,2},{7,3},{8,12},{9,13},{10,... | collective-permute-start | bytes 884744 | tf_op jit(solution)/shard_map/ppermute | solution.py:67
  10.2 9.3 %collective-permute-start.2 = (bf16[384,384]{1,0:T(8,128)(2,1)S(1)}, bf16[384,384]{1,0:T(8,128)(2,1)S(1)}, u32[]{:S(2)}, u32[]{:S(2)}) collective-permute-start(bf16[384,384]{1,0:T(8,128)(2,1)S(1)} %collective-permute-done.1.refs_2_), channel_id=1, source_target_pairs={{0,4},{1,5},{2,6},{3,7},{4,0},{5,1},{6,2},{7,3},{8,12},{9,13},{10,... | collective-permute-start | bytes 884744 | tf_op jit(solution)/shard_map/ppermute | solution.py:67
  11.2 11.0 %collective-permute-start.11 = (bf16[384,384]{1,0:T(8,128)(2,1)S(1)}, bf16[384,384]{1,0:T(8,128)(2,1)S(1)}, u32[]{:S(2)}, u32[]{:S(2)}) collective-permute-start(bf16[384,384]{1,0:T(8,128)(2,1)S(1)} %broadcast_select_fusion), channel_id=1, source_target_pairs={{0,5},{2,7},{5,0},{7,2},{8,13},{10,15},{13,8},{15,10},{16,21},{18,... | collective-permute-start | bytes 884744 | tf_op jit(solution)/shard_map/ppermute | solution.py:67
  15.0 7.5 %collective-permute-start.10 = (bf16[384,384]{1,0:T(8,128)(2,1)S(1)}, bf16[384,384]{1,0:T(8,128)(2,1)S(1)}, u32[]{:S(2)}, u32[]{:S(2)}) collective-permute-start(bf16[384,384]{1,0:T(8,128)(2,1)S(1)} %collective-permute-done.1.refs_2_), channel_id=1, source_target_pairs={{2,4},{7,1},{8,14},{13,11},{18,20},{23,17},{24,30},{29,27}} | collective-permute-start | bytes 884744 | tf_op jit(solution)/shard_map/ppermute | solution.py:67
  19.5 6.2 %collective-permute-start.9 = (bf16[384,384]{1,0:T(8,128)(2,1)S(1)}, bf16[384,384]{1,0:T(8,128)(2,1)S(1)}, u32[]{:S(2)}, u32[]{:S(2)}) collective-permute-start(bf16[384,384]{1,0:T(8,128)(2,1)S(1)} %collective-permute-done.3.refs_4_), channel_id=1, source_target_pairs={{3,6},{6,3},{9,12},{12,9},{19,22},{22,19},{25,28},{28,25}} | collective-permute-start | bytes 884744 | tf_op jit(solution)/shard_map/ppermute | solution.py:67
  20.1 6.5 %collective-permute-start.8 = (bf16[384,384]{1,0:T(8,128)(2,1)S(1)}, bf16[384,384]{1,0:T(8,128)(2,1)S(1)}, u32[]{:S(2)}, u32[]{:S(2)}) collective-permute-start(bf16[384,384]{1,0:T(8,128)(2,1)S(1)} %collective-permute-done.3.refs_4_), channel_id=1, source_target_pairs={{0,4},{1,5},{2,6},{3,7},{4,0},{5,1},{6,2},{7,3},{8,12},{9,13},{10,... | collective-permute-start | bytes 884744 | tf_op jit(solution)/shard_map/ppermute | solution.py:67
  20.2 9.4 %collective-permute-start.4 = (bf16[384,384]{1,0:T(8,128)(2,1)S(1)}, bf16[384,384]{1,0:T(8,128)(2,1)S(1)}, u32[]{:S(2)}, u32[]{:S(2)}) collective-permute-start(bf16[384,384]{1,0:T(8,128)(2,1)S(1)} %collective-permute-done.3.refs_4_), channel_id=1, source_target_pairs={{0,8},{1,9},{2,10},{3,11},{4,12},{5,13},{6,14},{7,15},{8,0},{9,1},... | collective-permute-start | bytes 884744 | tf_op jit(solution)/shard_map/ppermute | solution.py:67
  22.1 6.5 %collective-permute-start.7 = (s32[12,12]{1,0:T(8,128)}, s32[12,12]{1,0:T(8,128)S(1)}, u32[]{:S(2)}, u32[]{:S(2)}) collective-permute-start(s32[12,12]{1,0:T(8,128)} %refs_4_), channel_id=1, source_target_pairs={{0,3},{1,2},{2,1},{3,0},{4,7},{5,6},{6,5},{7,4},{8,11},{9,10},{10,... | collective-permute-start | bytes 1736 | tf_op jit(solution)/shard_map/ppermute | solution.py:231
  22.5 6.1 %collective-permute-start.6 = (s32[12,12]{1,0:T(8,128)}, s32[12,12]{1,0:T(8,128)S(1)}, u32[]{:S(2)}, u32[]{:S(2)}) collective-permute-start(s32[12,12]{1,0:T(8,128)} %refs_4_), channel_id=1, source_target_pairs={{0,2},{1,3},{2,0},{3,1},{4,6},{5,7},{6,4},{7,5},{8,10},{9,11},{10,... | collective-permute-start | bytes 1736 | tf_op jit(solution)/shard_map/ppermute | solution.py:231
  25.7 3.9 %collective-permute-start.5 = (s32[12,12]{1,0:T(8,128)}, s32[12,12]{1,0:T(8,128)S(1)}, u32[]{:S(2)}, u32[]{:S(2)}) collective-permute-start(s32[12,12]{1,0:T(8,128)} %refs_4_), channel_id=1, source_target_pairs={{0,1},{1,0},{2,3},{3,2},{4,5},{5,4},{6,7},{7,6},{8,9},{9,8},{10,11... | collective-permute-start | bytes 1736 | tf_op jit(solution)/shard_map/ppermute | solution.py:231
  26.6 3.0 %collective-permute-start.13 = (bf16[384,384]{1,0:T(8,128)(2,1)S(1)}, bf16[384,384]{1,0:T(8,128)(2,1)S(1)}, u32[]{:S(2)}, u32[]{:S(2)}) collective-permute-start(bf16[384,384]{1,0:T(8,128)(2,1)S(1)} %select_select_fusion.refs_1_), channel_id=1, source_target_pairs={{0,4},{1,5},{2,6},{3,7},{4,0},{5,1},{6,2},{7,3},{8,12},{9,13},{10,... | collective-permute-start | bytes 884744 | tf_op jit(solution)/shard_map/ppermute | solution.py:67
  26.7 1.0 %copy-start = (bf16[384,384]{1,0:T(8,128)(2,1)S(1)}, bf16[384,384]{1,0:T(8,128)(2,1)}, u32[]{:S(2)}) copy-start(bf16[384,384]{1,0:T(8,128)(2,1)} %refs_0_.1) | copy-start | bytes 884740
  29.6 1.6 %collective-permute-start.12 = (bf16[384,384]{1,0:T(8,128)(2,1)S(1)}, bf16[384,384]{1,0:T(8,128)(2,1)S(1)}, u32[]{:S(2)}, u32[]{:S(2)}) collective-permute-start(bf16[384,384]{1,0:T(8,128)(2,1)S(1)} %collective-permute-done.4.refs_0_), channel_id=1, source_target_pairs={{0,4},{1,5},{2,6},{3,7},{4,0},{5,1},{6,2},{7,3},{8,12},{9,13},{10,... | collective-permute-start | bytes 884744 | tf_op jit(solution)/shard_map/ppermute | solution.py:67

commit v5 on v4

--- a/solution.py
+++ b/solution.py
@@ -86,7 +86,8 @@
     diagonal = [(near, far, near, last)[kind[d]][d] for d in range(16)]
     mine = [own, across, line, line_across, diagonal]
     theirs = [moved(names, CORES) for names in mine]
-    order = [own, theirs[0], across, theirs[1], line, theirs[2], line_across, diagonal, theirs[3], theirs[4]]
+    order = [own, theirs[0], across, theirs[1], line, theirs[2]]
+    order += [line_across, diagonal, theirs[4], theirs[3]]
     for d in range(16):
         assert len({tuple(sorted(names[d])) for names in order}) == 10
     return order
@@ -133,19 +134,17 @@
     mirror(place(0, blocks, full, sems), full)
 
 
-def purify_kernel(full_in, *refs):
-    blocks, patterns = refs[:-11], refs[-11:-7]
-    out, full, square, low, small, rows, sems = refs[-7:]
-    late = len(blocks)
-    edge = out.shape[0]
-    order = full.shape[0]
+def middle_kernel(full_in, *refs):
+    blocks, patterns, (full, rows, small, sems) = refs[:-8], refs[-8:-4], refs[-4:]
+    edge = blocks[0].shape[0]
     n = small.shape[1]
     step = edge // n
-    loads = [pltpu.make_async_copy(p, small.at[k], sems.at[late + k]) for k, p in enumerate(patterns)]
+    count = len(blocks)
+    loads = [pltpu.make_async_copy(p, small.at[k], sems.at[count + k]) for k, p in enumerate(patterns)]
     for load in loads:
         load.start()
-    copies = place(10 - late, blocks, full, sems)
-    i, j = lax.axis_index("wide"), lax.axis_index("narrow")
+    copies = place(6, blocks, full, sems)
+    j = lax.axis_index("narrow")
     r = lax.broadcasted_iota(jnp.int32, (n, edge), 0)
     c = lax.broadcasted_iota(jnp.int32, (n, edge), 1)
     widen = jnp.where(r == c // step, 1.0, 0.0).astype(BF16)
@@ -154,6 +153,16 @@
         wide = jnp.dot(small[k].astype(BF16), widen, preferred_element_type=F32)
         rows[:, block_at(edge, jnp.bitwise_xor(j, k))] = wide
     mirror(copies, full)
+
+
+def purify_kernel(full_in, rows, *refs):
+    blocks, (out, full, square, low, sems) = refs[:-5], refs[-5:]
+    edge = out.shape[0]
+    order = full.shape[0]
+    n = rows.shape[0]
+    step = edge // n
+    mirror(place(10 - len(blocks), blocks, full, sems), full)
+    i, j = lax.axis_index("wide"), lax.axis_index("narrow")
 
     def masked(x, cols):
         tall = x.reshape(n, step, x.shape[1]) * rows[:, cols][:, None, :]
@@ -176,8 +185,8 @@
 PARAMS = pltpu.CompilerParams(vmem_limit_bytes=24 << 20)
 
 
-def in_hbm(array):
-    return pltpu.with_memory_space_constraint(array, pltpu.HBM)
+def in_vmem(array):
+    return pltpu.with_memory_space_constraint(array, pltpu.VMEM)
 
 
 def early(blocks):
@@ -193,27 +202,41 @@
     )(*blocks)
 
 
-def purify(full, blocks, patterns):
+def middle(full, blocks, patterns):
+    order = full.shape[0]
+    n = patterns[0].shape[0]
+    return pl.pallas_call(
+        middle_kernel,
+        out_shape=(pltpu.VMEM((order, order), BF16), pltpu.VMEM((n, order), F32)),
+        in_specs=[VMEM] + [HBM] * (len(blocks) + 4),
+        out_specs=(VMEM, VMEM),
+        input_output_aliases={0: 0},
+        scratch_shapes=[
+            pltpu.VMEM((4, n, n), jnp.int32),
+            pltpu.SemaphoreType.DMA((len(blocks) + 4,)),
+        ],
+        compiler_params=PARAMS,
+        name="middle",
+    )(in_vmem(full), *blocks, *patterns)
+
+
+def purify(full, rows, blocks):
     order = full.shape[0]
     edge = order // 4
-    n = patterns[0].shape[0]
-    full = pltpu.with_memory_space_constraint(full, pltpu.VMEM)
     return pl.pallas_call(
         purify_kernel,
         out_shape=(jax.ShapeDtypeStruct((edge, edge), BF16), pltpu.VMEM((order, order), BF16)),
-        in_specs=[VMEM] + [HBM] * (len(blocks) + 4),
+        in_specs=[VMEM, VMEM] + [HBM] * len(blocks),
         out_specs=(VMEM, VMEM),
         input_output_aliases={0: 1},
         scratch_shapes=[
             pltpu.VMEM((edge, order), F32),
             pltpu.VMEM((edge, order), BF16),
-            pltpu.VMEM((4, n, n), jnp.int32),
-            pltpu.VMEM((n, order), F32),
-            pltpu.SemaphoreType.DMA((len(blocks) + 4,)),
+            pltpu.SemaphoreType.DMA((len(blocks),)),
         ],
         compiler_params=PARAMS,
         name="purify",
-    )(full, *blocks, *patterns)[0]
+    )(in_vmem(full), in_vmem(rows), *blocks)[0]
 
 
 def block_body(own, pattern):
@@ -236,8 +259,8 @@
     line_across_c = send(line_across, CORES)
     diagonal = jnp.where(kind == 3, last, jnp.where(kind == 1, far, near))
     diagonal_c = send(diagonal, CORES)
-    blocks = (line_across, diagonal, line_across_c, diagonal_c)
-    return purify(full, blocks, patterns)
+    full, rows = middle(full, (line_across, diagonal, diagonal_c), patterns)
+    return purify(full, rows, (line_across_c,))
 
 
 def solution(mesh):

time: 35.6 us -> 34.8 us (0.978)
  waiting for transfers between devices: 9.95 us -> 9.1 us
    ppermute x11, waiting for transfers between devices: 9.07 us -> 8.21 us  [send(): return lax.ppermute(array, AXES, moves)]
    pallas_call x1, Pallas kernels: 4.2 us -> 3.36 us  [purify(): pl.pallas_call(purify_kernel, out_shape=(jax.ShapeDtypeStruct((edge, edge...]
    pallas_call x0 -> x1, Pallas kernels: none -> 0.84 us  [middle(): pl.pallas_call(middle_kernel, out_shape=(pltpu.VMEM((order, order), BF16)...]
  transfers between devices with their start and end apart: 14 -> 14, of which waited for: 5 -> 5; matrix products, arithmetic and copies ran while one was open for 3% -> 3% of each run, Pallas kernels for 3% -> 5%
where the time goes in v5:
time: 34.8 us; the launch traced here: 34.6 us
  starting transfers between devices  18.2 us (52%)
  waiting for transfers between devices  9.1 us (26%)
  Pallas kernels  5.16 us (15%)
  other arithmetic  1.05 us (3%)
  local copies, waits for them, and re-layouts  0.96 us (3%)
    ppermute x11, starting transfers between devices, send(): return lax.ppermute(array, AXES, moves)  13.8 us
    ppermute x11, waiting for transfers between devices, send(): return lax.ppermute(array, AXES, moves)  8.21 us
    ppermute x3, starting transfers between devices, block_body(): lax.ppermute(pattern, 'narrow', [(c, c ^ k) for c in range(4)])  4.39 us
    pallas_call x1, Pallas kernels, purify(): pl.pallas_call(purify_kernel, out_shape=(jax.ShapeDtypeStruct((edge, edge...  3.36 us
    select_n x1, other arithmetic, block_body(): near = send(jnp.where(kind == 0, own, across), NEAR_DIAGONAL)  1 us
    pallas_call x1, Pallas kernels, early(): pl.pallas_call(early_kernel, out_shape=pltpu.VMEM((order, order), BF16),...  0.96 us
    unnamed x4, local copies, waits for them, and re-layouts  0.96 us
    ppermute x3, waiting for transfers between devices, block_body(): lax.ppermute(pattern, 'narrow', [(c, c ^ k) for c in range(4)])  0.89 us
  transfers between devices with their start and end apart: 14, of which 5 were waited for; matrix products, arithmetic and copies ran while one was open for 3% of the time, Pallas kernels for 5%

profile of v5, /device:TPU:0, one launch (start us, length us, event | category | flops | bytes accessed | tf_op | source)
XLA Modules:
  0.0 34.6 jit_solution(1624758716149079386)
XLA Ops:
  0.0 3.0 %collective-permute-start.1 = (bf16[384,384]{1,0:T(8,128)(2,1)}, bf16[384,384]{1,0:T(8,128)(2,1)S(1)}, u32[]{:S(2)}, u32[]{:S(2)}) collective-permute-start(bf16[384,384]{1,0:T(8,128)(2,1)} %refs_0_.1), channel_id=1, source_target_pairs={{0,8},{1,9},{2,10},{3,11},{4,12},{5,13},{6,14},{7,15},{8,0},{9,1},... | collective-permute-start | bytes 884744 | tf_op jit(solution)/shard_map/ppermute | solution.py:67
  3.0 3.6 %collective-permute-start.3 = (bf16[384,384]{1,0:T(8,128)(2,1)}, bf16[384,384]{1,0:T(8,128)(2,1)S(1)}, u32[]{:S(2)}, u32[]{:S(2)}) collective-permute-start(bf16[384,384]{1,0:T(8,128)(2,1)} %refs_0_.1), channel_id=1, source_target_pairs={{8,11},{9,15},{12,10},{13,14},{10,9},{14,13},{11,8},{15,12},{7,4},... | collective-permute-start | bytes 884744 | tf_op jit(solution)/shard_map/ppermute | solution.py:67
  6.6 0.0 collective-permute-start
  6.6 3.6 %collective-permute-done.1.refs_2_ = bf16[384,384]{1,0:T(8,128)(2,1)S(1)} collective-permute-done((bf16[384,384]{1,0:T(8,128)(2,1)}, bf16[384,384]{1,0:T(8,128)(2,1)S(1)}, u32[]{:S(2)}, u32[]{:S(2)}) %collective-permute-start.1) | collective-permute-done | bytes 294944 | tf_op jit(solution)/shard_map/ppermute | solution.py:67
  10.2 0.0 collective-permute-start.2
  10.2 1.0 %broadcast_select_fusion = bf16[384,384]{1,0:T(8,128)(2,1)S(1)} fusion(bf16[384,384]{1,0:T(8,128)(2,1)} %refs_0_.1, bf16[384,384]{1,0:T(8,128)(2,1)S(1)} %collective-permute-done.1.refs_2_, pred[]{:T(512)S(6)} %eq.11), kind=kLoop, calls=%fused_computation.1 | loop fusion | flops 147456 | bytes 884737 | tf_op jit(solution)/shard_map/jit(_where)/select_n | solution.py:247
  11.2 3.8 %collective-permute-start.11 = (bf16[384,384]{1,0:T(8,128)(2,1)S(1)}, bf16[384,384]{1,0:T(8,128)(2,1)S(1)}, u32[]{:S(2)}, u32[]{:S(2)}) collective-permute-start(bf16[384,384]{1,0:T(8,128)(2,1)S(1)} %broadcast_select_fusion), channel_id=1, source_target_pairs={{0,5},{2,7},{5,0},{7,2},{8,13},{10,15},{13,8},{15,10},{16,21},{18,... | collective-permute-start | bytes 884744 | tf_op jit(solution)/shard_map/ppermute | solution.py:67
  15.0 0.7 %collective-permute-start.10 = (bf16[384,384]{1,0:T(8,128)(2,1)S(1)}, bf16[384,384]{1,0:T(8,128)(2,1)S(1)}, u32[]{:S(2)}, u32[]{:S(2)}) collective-permute-start(bf16[384,384]{1,0:T(8,128)(2,1)S(1)} %collective-permute-done.1.refs_2_), channel_id=1, source_target_pairs={{2,4},{7,1},{8,14},{13,11},{18,20},{23,17},{24,30},{29,27}} | collective-permute-start | bytes 884744 | tf_op jit(solution)/shard_map/ppermute | solution.py:67
  15.7 3.7 %collective-permute-done.3.refs_4_ = bf16[384,384]{1,0:T(8,128)(2,1)S(1)} collective-permute-done((bf16[384,384]{1,0:T(8,128)(2,1)}, bf16[384,384]{1,0:T(8,128)(2,1)S(1)}, u32[]{:S(2)}, u32[]{:S(2)}) %collective-permute-start.3) | collective-permute-done | bytes 294944 | tf_op jit(solution)/shard_map/ppermute | solution.py:67
  19.5 0.0 collective-permute-done.refs_1_
  19.5 0.0 collective-permute-done.2.refs_3_
  19.5 0.7 %collective-permute-start.9 = (bf16[384,384]{1,0:T(8,128)(2,1)S(1)}, bf16[384,384]{1,0:T(8,128)(2,1)S(1)}, u32[]{:S(2)}, u32[]{:S(2)}) collective-permute-start(bf16[384,384]{1,0:T(8,128)(2,1)S(1)} %collective-permute-done.3.refs_4_), channel_id=1, source_target_pairs={{3,6},{6,3},{9,12},{12,9},{19,22},{22,19},{25,28},{28,25}} | collective-permute-start | bytes 884744 | tf_op jit(solution)/shard_map/ppermute | solution.py:67
  20.1 0.1 collective-permute-start.8
  20.2 1.9 %collective-permute-start.4 = (bf16[384,384]{1,0:T(8,128)(2,1)S(1)}, bf16[384,384]{1,0:T(8,128)(2,1)S(1)}, u32[]{:S(2)}, u32[]{:S(2)}) collective-permute-start(bf16[384,384]{1,0:T(8,128)(2,1)S(1)} %collective-permute-done.3.refs_4_), channel_id=1, source_target_pairs={{0,8},{1,9},{2,10},{3,11},{4,12},{5,13},{6,14},{7,15},{8,0},{9,1},... | collective-permute-start | bytes 884744 | tf_op jit(solution)/shard_map/ppermute | solution.py:67
  22.1 0.0 collective-permute-done.11
  22.1 0.4 %collective-permute-start.7 = (s32[12,12]{1,0:T(8,128)}, s32[12,12]{1,0:T(8,128)S(1)}, u32[]{:S(2)}, u32[]{:S(2)}) collective-permute-start(s32[12,12]{1,0:T(8,128)} %refs_3_), channel_id=1, source_target_pairs={{0,3},{1,2},{2,1},{3,0},{4,7},{5,6},{6,5},{7,4},{8,11},{9,10},{10,... | collective-permute-start | bytes 1736 | tf_op jit(solution)/shard_map/ppermute | solution.py:254
  22.5 0.0 collective-permute-done.10
  22.5 3.1 %collective-permute-start.6 = (s32[12,12]{1,0:T(8,128)}, s32[12,12]{1,0:T(8,128)S(1)}, u32[]{:S(2)}, u32[]{:S(2)}) collective-permute-start(s32[12,12]{1,0:T(8,128)} %refs_3_), channel_id=1, source_target_pairs={{0,2},{1,3},{2,0},{3,1},{4,6},{5,7},{6,4},{7,5},{8,10},{9,11},{10,... | collective-permute-start | bytes 1736 | tf_op jit(solution)/shard_map/ppermute | solution.py:254
  25.7 0.0 collective-permute-done.9
  25.7 0.9 %collective-permute-start.5 = (s32[12,12]{1,0:T(8,128)}, s32[12,12]{1,0:T(8,128)S(1)}, u32[]{:S(2)}, u32[]{:S(2)}) collective-permute-start(s32[12,12]{1,0:T(8,128)} %refs_3_), channel_id=1, source_target_pairs={{0,1},{1,0},{2,3},{3,2},{4,5},{5,4},{6,7},{7,6},{8,9},{9,8},{10,11... | collective-permute-start | bytes 1736 | tf_op jit(solution)/shard_map/ppermute | solution.py:254
  26.6 0.1 collective-permute-start.12
  26.7 0.0 copy-start
  26.7 1.0 %copy-done = bf16[384,384]{1,0:T(8,128)(2,1)S(1)} copy-done((bf16[384,384]{1,0:T(8,128)(2,1)S(1)}, bf16[384,384]{1,0:T(8,128)(2,1)}, u32[]{:S(2)}) %copy-start) | copy-done | bytes 294936
  27.7 1.0 %early.1.full_in = bf16[1536,1536]{1,0:T(8,128)(2,1)S(1)} custom-call(bf16[384,384]{1,0:T(8,128)(2,1)S(1)} %copy-done, bf16[384,384]{1,0:T(8,128)(2,1)S(1)} %collective-permute-done.refs_1_, bf16[384,384]{1,0:T(8,128)(2,1)S(1)} %collective-permute-done.1.refs_2_, bf16[384,384]{1,0:T(8,128)(2,1)S(1)} %collective-permute-done.2.refs_3_, ...), custom_call_target="tpu_custom_call" | custom-call | tf_op jit(solution)/shard_map/early/pallas_call | solution.py:194
  28.6 0.0 collective-permute-done.7.refs_6_
  28.6 0.9 %collective-permute-done.5.refs_4_ = s32[12,12]{1,0:T(8,128)S(1)} collective-permute-done((s32[12,12]{1,0:T(8,128)}, s32[12,12]{1,0:T(8,128)S(1)}, u32[]{:S(2)}, u32[]{:S(2)}) %collective-permute-start.5) | collective-permute-done | bytes 608 | tf_op jit(solution)/shard_map/ppermute | solution.py:254
  29.5 0.1 collective-permute-done.4.refs_0_
  29.6 0.0 collective-permute-start.13
  29.6 0.0 collective-permute-done.12.refs_2_
  29.7 0.8 %middle.1 = (bf16[1536,1536]{1,0:T(8,128)(2,1)S(1)}, f32[12,1536]{1,0:T(8,128)S(1)}) custom-call(bf16[1536,1536]{1,0:T(8,128)(2,1)S(1)} %early.1.full_in, bf16[384,384]{1,0:T(8,128)(2,1)S(1)} %collective-permute-done.4.refs_0_, bf16[384,384]{1,0:T(8,128)(2,1)S(1)} %select_select_fusion.refs_1_, ...), custom_call_target="tpu_custom_call", output_to_operand_aliasing={{0}: (0, {})} | custom-call | tf_op jit(solution)/shard_map/middle/pallas_call | solution.py:208
  30.5 0.7 %collective-permute-done.13.refs_0_ = bf16[384,384]{1,0:T(8,128)(2,1)S(1)} collective-permute-done((bf16[384,384]{1,0:T(8,128)(2,1)S(1)}, bf16[384,384]{1,0:T(8,128)(2,1)S(1)}, u32[]{:S(2)}, u32[]{:S(2)}) %collective-permute-start.13) | collective-permute-done | bytes 294944 | tf_op jit(solution)/shard_map/ppermute | solution.py:67
  31.2 3.4 %purify.1 = (bf16[384,384]{1,0:T(8,128)(2,1)}, bf16[1536,1536]{1,0:T(8,128)(2,1)S(1)}) custom-call(bf16[1536,1536]{1,0:T(8,128)(2,1)S(1)} %get-tuple-element.32.full_in, f32[12,1536]{1,0:T(8,128)S(1)} %get-tuple-element.33.rows, bf16[384,384]{1,0:T(8,128)(2,1)S(1)} %collective-permute-done.13.refs_0_), custom_call_target="tpu_custom_call", output_to_operand_aliasing={{1}: (0, {})} | custom-call | tf_op jit(solution)/shard_map/purify/pallas_call | solution.py:226
  (5 shorter events, 0.1 us)
Async XLA Ops:
  0.0 29.7 %copy-start.1 = (s32[12,12]{1,0:T(8,128)S(1)}, s32[12,12]{1,0:T(8,128)}, u32[]{:S(2)}) copy-start(s32[12,12]{1,0:T(8,128)} %refs_3_) | copy-start | bytes 1732
  0.0 10.2 %collective-permute-start.1 = (bf16[384,384]{1,0:T(8,128)(2,1)}, bf16[384,384]{1,0:T(8,128)(2,1)S(1)}, u32[]{:S(2)}, u32[]{:S(2)}) collective-permute-start(bf16[384,384]{1,0:T(8,128)(2,1)} %refs_0_.1), channel_id=1, source_target_pairs={{0,8},{1,9},{2,10},{3,11},{4,12},{5,13},{6,14},{7,15},{8,0},{9,1},... | collective-permute-start | bytes 884744 | tf_op jit(solution)/shard_map/ppermute | solution.py:67
  3.0 16.5 %collective-permute-start.3 = (bf16[384,384]{1,0:T(8,128)(2,1)}, bf16[384,384]{1,0:T(8,128)(2,1)S(1)}, u32[]{:S(2)}, u32[]{:S(2)}) collective-permute-start(bf16[384,384]{1,0:T(8,128)(2,1)} %refs_0_.1), channel_id=1, source_target_pairs={{8,11},{9,15},{12,10},{13,14},{10,9},{14,13},{11,8},{15,12},{7,4},... | collective-permute-start | bytes 884744 | tf_op jit(solution)/shard_map/ppermute | solution.py:67
  6.6 12.9 %collective-permute-start = (bf16[384,384]{1,0:T(8,128)(2,1)}, bf16[384,384]{1,0:T(8,128)(2,1)S(1)}, u32[]{:S(2)}, u32[]{:S(2)}) collective-permute-start(bf16[384,384]{1,0:T(8,128)(2,1)} %refs_0_.1), channel_id=1, source_target_pairs={{0,4},{1,5},{2,6},{3,7},{4,0},{5,1},{6,2},{7,3},{8,12},{9,13},{10,... | collective-permute-start | bytes 884744 | tf_op jit(solution)/shard_map/ppermute | solution.py:67
  10.2 9.3 %collective-permute-start.2 = (bf16[384,384]{1,0:T(8,128)(2,1)S(1)}, bf16[384,384]{1,0:T(8,128)(2,1)S(1)}, u32[]{:S(2)}, u32[]{:S(2)}) collective-permute-start(bf16[384,384]{1,0:T(8,128)(2,1)S(1)} %collective-permute-done.1.refs_2_), channel_id=1, source_target_pairs={{0,4},{1,5},{2,6},{3,7},{4,0},{5,1},{6,2},{7,3},{8,12},{9,13},{10,... | collective-permute-start | bytes 884744 | tf_op jit(solution)/shard_map/ppermute | solution.py:67
  11.2 11.0 %collective-permute-start.11 = (bf16[384,384]{1,0:T(8,128)(2,1)S(1)}, bf16[384,384]{1,0:T(8,128)(2,1)S(1)}, u32[]{:S(2)}, u32[]{:S(2)}) collective-permute-start(bf16[384,384]{1,0:T(8,128)(2,1)S(1)} %broadcast_select_fusion), channel_id=1, source_target_pairs={{0,5},{2,7},{5,0},{7,2},{8,13},{10,15},{13,8},{15,10},{16,21},{18,... | collective-permute-start | bytes 884744 | tf_op jit(solution)/shard_map/ppermute | solution.py:67
  15.0 7.5 %collective-permute-start.10 = (bf16[384,384]{1,0:T(8,128)(2,1)S(1)}, bf16[384,384]{1,0:T(8,128)(2,1)S(1)}, u32[]{:S(2)}, u32[]{:S(2)}) collective-permute-start(bf16[384,384]{1,0:T(8,128)(2,1)S(1)} %collective-permute-done.1.refs_2_), channel_id=1, source_target_pairs={{2,4},{7,1},{8,14},{13,11},{18,20},{23,17},{24,30},{29,27}} | collective-permute-start | bytes 884744 | tf_op jit(solution)/shard_map/ppermute | solution.py:67
  19.5 6.2 %collective-permute-start.9 = (bf16[384,384]{1,0:T(8,128)(2,1)S(1)}, bf16[384,384]{1,0:T(8,128)(2,1)S(1)}, u32[]{:S(2)}, u32[]{:S(2)}) collective-permute-start(bf16[384,384]{1,0:T(8,128)(2,1)S(1)} %collective-permute-done.3.refs_4_), channel_id=1, source_target_pairs={{3,6},{6,3},{9,12},{12,9},{19,22},{22,19},{25,28},{28,25}} | collective-permute-start | bytes 884744 | tf_op jit(solution)/shard_map/ppermute | solution.py:67
  20.1 6.5 %collective-permute-start.8 = (bf16[384,384]{1,0:T(8,128)(2,1)S(1)}, bf16[384,384]{1,0:T(8,128)(2,1)S(1)}, u32[]{:S(2)}, u32[]{:S(2)}) collective-permute-start(bf16[384,384]{1,0:T(8,128)(2,1)S(1)} %collective-permute-done.3.refs_4_), channel_id=1, source_target_pairs={{0,4},{1,5},{2,6},{3,7},{4,0},{5,1},{6,2},{7,3},{8,12},{9,13},{10,... | collective-permute-start | bytes 884744 | tf_op jit(solution)/shard_map/ppermute | solution.py:67
  20.2 9.4 %collective-permute-start.4 = (bf16[384,384]{1,0:T(8,128)(2,1)S(1)}, bf16[384,384]{1,0:T(8,128)(2,1)S(1)}, u32[]{:S(2)}, u32[]{:S(2)}) collective-permute-start(bf16[384,384]{1,0:T(8,128)(2,1)S(1)} %collective-permute-done.3.refs_4_), channel_id=1, source_target_pairs={{0,8},{1,9},{2,10},{3,11},{4,12},{5,13},{6,14},{7,15},{8,0},{9,1},... | collective-permute-start | bytes 884744 | tf_op jit(solution)/shard_map/ppermute | solution.py:67
  22.1 6.5 %collective-permute-start.7 = (s32[12,12]{1,0:T(8,128)}, s32[12,12]{1,0:T(8,128)S(1)}, u32[]{:S(2)}, u32[]{:S(2)}) collective-permute-start(s32[12,12]{1,0:T(8,128)} %refs_3_), channel_id=1, source_target_pairs={{0,3},{1,2},{2,1},{3,0},{4,7},{5,6},{6,5},{7,4},{8,11},{9,10},{10,... | collective-permute-start | bytes 1736 | tf_op jit(solution)/shard_map/ppermute | solution.py:254
  22.5 6.1 %collective-permute-start.6 = (s32[12,12]{1,0:T(8,128)}, s32[12,12]{1,0:T(8,128)S(1)}, u32[]{:S(2)}, u32[]{:S(2)}) collective-permute-start(s32[12,12]{1,0:T(8,128)} %refs_3_), channel_id=1, source_target_pairs={{0,2},{1,3},{2,0},{3,1},{4,6},{5,7},{6,4},{7,5},{8,10},{9,11},{10,... | collective-permute-start | bytes 1736 | tf_op jit(solution)/shard_map/ppermute | solution.py:254
  25.7 3.9 %collective-permute-start.5 = (s32[12,12]{1,0:T(8,128)}, s32[12,12]{1,0:T(8,128)S(1)}, u32[]{:S(2)}, u32[]{:S(2)}) collective-permute-start(s32[12,12]{1,0:T(8,128)} %refs_3_), channel_id=1, source_target_pairs={{0,1},{1,0},{2,3},{3,2},{4,5},{5,4},{6,7},{7,6},{8,9},{9,8},{10,11... | collective-permute-start | bytes 1736 | tf_op jit(solution)/shard_map/ppermute | solution.py:254
  26.6 3.0 %collective-permute-start.12 = (bf16[384,384]{1,0:T(8,128)(2,1)S(1)}, bf16[384,384]{1,0:T(8,128)(2,1)S(1)}, u32[]{:S(2)}, u32[]{:S(2)}) collective-permute-start(bf16[384,384]{1,0:T(8,128)(2,1)S(1)} %select_select_fusion.refs_1_), channel_id=1, source_target_pairs={{0,4},{1,5},{2,6},{3,7},{4,0},{5,1},{6,2},{7,3},{8,12},{9,13},{10,... | collective-permute-start | bytes 884744 | tf_op jit(solution)/shard_map/ppermute | solution.py:67
  26.7 1.0 %copy-start = (bf16[384,384]{1,0:T(8,128)(2,1)S(1)}, bf16[384,384]{1,0:T(8,128)(2,1)}, u32[]{:S(2)}) copy-start(bf16[384,384]{1,0:T(8,128)(2,1)} %refs_0_.1) | copy-start | bytes 884740
  29.6 1.6 %collective-permute-start.13 = (bf16[384,384]{1,0:T(8,128)(2,1)S(1)}, bf16[384,384]{1,0:T(8,128)(2,1)S(1)}, u32[]{:S(2)}, u32[]{:S(2)}) collective-permute-start(bf16[384,384]{1,0:T(8,128)(2,1)S(1)} %collective-permute-done.4.refs_0_), channel_id=1, source_target_pairs={{0,4},{1,5},{2,6},{3,7},{4,0},{5,1},{6,2},{7,3},{8,12},{9,13},{10,... | collective-permute-start | bytes 884744 | tf_op jit(solution)/shard_map/ppermute | solution.py:67

commit v6 on v5

--- a/solution.py
+++ b/solution.py
@@ -134,9 +134,26 @@
     mirror(place(0, blocks, full, sems), full)
 
 
+def square_columns(first, count, full, rows, square, low):
+    n, edge = rows.shape[0], square.shape[0]
+    panel = full[block_at(edge, lax.axis_index("wide"))]
+    for t in range(count):
+        cols = pl.ds(pl.multiple_of(first + 256 * t, 128), 256)
+        s = jnp.dot(panel, full[:, cols], preferred_element_type=F32)
+        s = masked(s, rows[:, cols])
+        square[:, cols] = s
+        low[:, cols] = s.astype(BF16)
+
+
+def masked(x, rows):
+    n = rows.shape[0]
+    tall = x.reshape(n, x.shape[0] // n, x.shape[1]) * rows[:, None, :]
+    return tall.reshape(x.shape)
+
+
 def middle_kernel(full_in, *refs):
-    blocks, patterns, (full, rows, small, sems) = refs[:-8], refs[-8:-4], refs[-4:]
-    edge = blocks[0].shape[0]
+    blocks, patterns, (full, rows, square, low, small, sems) = refs[:-10], refs[-10:-6], refs[-6:]
+    edge, order = square.shape
     n = small.shape[1]
     step = edge // n
     count = len(blocks)
@@ -144,7 +161,7 @@
     for load in loads:
         load.start()
     copies = place(6, blocks, full, sems)
-    j = lax.axis_index("narrow")
+    i, j = lax.axis_index("wide"), lax.axis_index("narrow")
     r = lax.broadcasted_iota(jnp.int32, (n, edge), 0)
     c = lax.broadcasted_iota(jnp.int32, (n, edge), 1)
     widen = jnp.where(r == c // step, 1.0, 0.0).astype(BF16)
@@ -154,29 +171,29 @@
         rows[:, block_at(edge, jnp.bitwise_xor(j, k))] = wide
     mirror(copies, full)
 
-
-def purify_kernel(full_in, rows, *refs):
+    @pl.when(jnp.right_shift(i, 1) == jnp.right_shift(j, 1))
+    def _():
+        square_columns(jnp.right_shift(i, 1) * (order // 2), order // 512, full, rows, square, low)
+
+
+def purify_kernel(full_in, rows, square_in, low_in, *refs):
     blocks, (out, full, square, low, sems) = refs[:-5], refs[-5:]
-    edge = out.shape[0]
-    order = full.shape[0]
-    n = rows.shape[0]
-    step = edge // n
+    edge, order = square.shape
     mirror(place(10 - len(blocks), blocks, full, sems), full)
     i, j = lax.axis_index("wide"), lax.axis_index("narrow")
-
-    def masked(x, cols):
-        tall = x.reshape(n, step, x.shape[1]) * rows[:, cols][:, None, :]
-        return tall.reshape(x.shape)
-
-    panel = full[block_at(edge, i)]
-    width = 256
-    for t in range(order // width):
-        cols = slice(t * width, (t + 1) * width)
-        s = masked(jnp.dot(panel, full[:, cols], preferred_element_type=F32), cols)
-        square[:, cols] = s
-        low[:, cols] = s.astype(BF16)
+    half = jnp.right_shift(i, 1)
+
+    @pl.when(half == jnp.right_shift(j, 1))
+    def _():
+        square_columns((1 - half) * (order // 2), order // 512, full, rows, square, low)
+
+    @pl.when(half != jnp.right_shift(j, 1))
+    def _():
+        square_columns(0, order // 256, full, rows, square, low)
+
     mine = block_at(edge, j)
-    cube = masked(jnp.dot(low[...], full[:, mine], preferred_element_type=F32), mine)
+    cube = jnp.dot(low[...], full[:, mine], preferred_element_type=F32)
+    cube = masked(cube, rows[:, mine])
     out[...] = (3.0 * square[:, mine] - 2.0 * cube).astype(BF16)
 
 
@@ -204,12 +221,18 @@
 
 def middle(full, blocks, patterns):
     order = full.shape[0]
+    edge = order // 4
     n = patterns[0].shape[0]
     return pl.pallas_call(
         middle_kernel,
-        out_shape=(pltpu.VMEM((order, order), BF16), pltpu.VMEM((n, order), F32)),
+        out_shape=(
+            pltpu.VMEM((order, order), BF16),
+            pltpu.VMEM((n, order), F32),
+            pltpu.VMEM((edge, order), F32),
+            pltpu.VMEM((edge, order), BF16),
+        ),
         in_specs=[VMEM] + [HBM] * (len(blocks) + 4),
-        out_specs=(VMEM, VMEM),
+        out_specs=(VMEM,) * 4,
         input_output_aliases={0: 0},
         scratch_shapes=[
             pltpu.VMEM((4, n, n), jnp.int32),
@@ -220,23 +243,23 @@
     )(in_vmem(full), *blocks, *patterns)
 
 
-def purify(full, rows, blocks):
-    order = full.shape[0]
-    edge = order // 4
+def purify(full, rows, square, low, blocks):
+    edge, order = square.shape
     return pl.pallas_call(
         purify_kernel,
-        out_shape=(jax.ShapeDtypeStruct((edge, edge), BF16), pltpu.VMEM((order, order), BF16)),
-        in_specs=[VMEM, VMEM] + [HBM] * len(blocks),
-        out_specs=(VMEM, VMEM),
-        input_output_aliases={0: 1},
-        scratch_shapes=[
+        out_shape=(
+            jax.ShapeDtypeStruct((edge, edge), BF16),
+            pltpu.VMEM((order, order), BF16),
             pltpu.VMEM((edge, order), F32),
             pltpu.VMEM((edge, order), BF16),
-            pltpu.SemaphoreType.DMA((len(blocks),)),
-        ],
+        ),
+        in_specs=[VMEM] * 4 + [HBM] * len(blocks),
+        out_specs=(VMEM,) * 4,
+        input_output_aliases={0: 1, 2: 2, 3: 3},
+        scratch_shapes=[pltpu.SemaphoreType.DMA((len(blocks),))],
         compiler_params=PARAMS,
         name="purify",
-    )(in_vmem(full), in_vmem(rows), *blocks)[0]
+    )(*map(in_vmem, (full, rows, square, low)), *blocks)[0]
 
 
 def block_body(own, pattern):
@@ -253,14 +276,14 @@
     pattern, line = hold((pattern, line))
     got = {k: lax.ppermute(pattern, "narrow", [(c, c ^ k) for c in range(4)]) for k in (1, 2, 3)}
     patterns = [pattern, got[1], got[2], got[3]]
-    full = early((own, own_c, across, across_c, line, line_c,))
+    full = early((own, own_c, across, across_c, line, line_c))
     patterns, full = hold((patterns, full))
     line_across, full = hold((line_across, full))
     line_across_c = send(line_across, CORES)
     diagonal = jnp.where(kind == 3, last, jnp.where(kind == 1, far, near))
     diagonal_c = send(diagonal, CORES)
-    full, rows = middle(full, (line_across, diagonal, diagonal_c), patterns)
-    return purify(full, rows, (line_across_c,))
+    full, rows, square, low = middle(full, (line_across, diagonal, diagonal_c), patterns)
+    return purify(full, rows, square, low, (line_across_c,))
 
 
 def solution(mesh):

time: 34.8 us -> 34.5 us (level)
  waiting for transfers between devices: 9.1 us -> 8.38 us
  Pallas kernels: 5.16 us -> 5.56 us
    pallas_call x1, Pallas kernels: 0.84 us -> 1.93 us  [middle(): pl.pallas_call(middle_kernel, out_shape=(pltpu.VMEM((order, order), BF16)...]
    ppermute x11, waiting for transfers between devices: 8.21 us -> 7.5 us  [send(): return lax.ppermute(array, AXES, moves)]
    pallas_call x1, Pallas kernels: 3.36 us -> 2.67 us  [purify(): pl.pallas_call(purify_kernel, out_shape=(jax.ShapeDtypeStruct((edge, edge...]
  transfers between devices with their start and end apart: 14 -> 14, of which waited for: 5 -> 4; matrix products, arithmetic and copies ran while one was open for 3% -> 3% of each run, Pallas kernels for 5% -> 8%
where the time goes in v6:
time: 34.5 us; the launch traced here: 34.3 us
  starting transfers between devices  18.2 us (53%)
  waiting for transfers between devices  8.38 us (24%)
  Pallas kernels  5.56 us (16%)
  other arithmetic  1.05 us (3%)
  local copies, waits for them, and re-layouts  0.96 us (3%)
    ppermute x11, starting transfers between devices, send(): return lax.ppermute(array, AXES, moves)  13.8 us
    ppermute x11, waiting for transfers between devices, send(): return lax.ppermute(array, AXES, moves)  7.5 us
    ppermute x3, starting transfers between devices, block_body(): lax.ppermute(pattern, 'narrow', [(c, c ^ k) for c in range(4)])  4.39 us
    pallas_call x1, Pallas kernels, purify(): pl.pallas_call(purify_kernel, out_shape=(jax.ShapeDtypeStruct((edge, edge...  2.67 us
    pallas_call x1, Pallas kernels, middle(): pl.pallas_call(middle_kernel, out_shape=(pltpu.VMEM((order, order), BF16)...  1.93 us
    select_n x1, other arithmetic, block_body(): near = send(jnp.where(kind == 0, own, across), NEAR_DIAGONAL)  1 us
    pallas_call x1, Pallas kernels, early(): pl.pallas_call(early_kernel, out_shape=pltpu.VMEM((order, order), BF16),...  0.96 us
    unnamed x4, local copies, waits for them, and re-layouts  0.96 us
  transfers between devices with their start and end apart: 14, of which 4 were waited for; matrix products, arithmetic and copies ran while one was open for 3% of the time, Pallas kernels for 8%

profile of v6, /device:TPU:0, one launch (start us, length us, event | category | flops | bytes accessed | tf_op | source)
XLA Modules:
  0.0 34.3 jit_solution(15179994821187949073)
XLA Ops:
  0.0 3.0 %collective-permute-start.1 = (bf16[384,384]{1,0:T(8,128)(2,1)}, bf16[384,384]{1,0:T(8,128)(2,1)S(1)}, u32[]{:S(2)}, u32[]{:S(2)}) collective-permute-start(bf16[384,384]{1,0:T(8,128)(2,1)} %refs_0_.1), channel_id=1, source_target_pairs={{0,8},{1,9},{2,10},{3,11},{4,12},{5,13},{6,14},{7,15},{8,0},{9,1},... | collective-permute-start | bytes 884744 | tf_op jit(solution)/shard_map/ppermute | solution.py:67
  3.0 3.6 %collective-permute-start.3 = (bf16[384,384]{1,0:T(8,128)(2,1)}, bf16[384,384]{1,0:T(8,128)(2,1)S(1)}, u32[]{:S(2)}, u32[]{:S(2)}) collective-permute-start(bf16[384,384]{1,0:T(8,128)(2,1)} %refs_0_.1), channel_id=1, source_target_pairs={{8,11},{9,15},{12,10},{13,14},{10,9},{14,13},{11,8},{15,12},{7,4},... | collective-permute-start | bytes 884744 | tf_op jit(solution)/shard_map/ppermute | solution.py:67
  6.6 0.0 collective-permute-start
  6.6 3.6 %collective-permute-done.1.refs_2_ = bf16[384,384]{1,0:T(8,128)(2,1)S(1)} collective-permute-done((bf16[384,384]{1,0:T(8,128)(2,1)}, bf16[384,384]{1,0:T(8,128)(2,1)S(1)}, u32[]{:S(2)}, u32[]{:S(2)}) %collective-permute-start.1) | collective-permute-done | bytes 294944 | tf_op jit(solution)/shard_map/ppermute | solution.py:67
  10.2 0.0 collective-permute-start.2
  10.2 1.0 %broadcast_select_fusion = bf16[384,384]{1,0:T(8,128)(2,1)S(1)} fusion(bf16[384,384]{1,0:T(8,128)(2,1)} %refs_0_.1, bf16[384,384]{1,0:T(8,128)(2,1)S(1)} %collective-permute-done.1.refs_2_, pred[]{:T(512)S(6)} %eq.11), kind=kLoop, calls=%fused_computation.1 | loop fusion | flops 147456 | bytes 884737 | tf_op jit(solution)/shard_map/jit(_where)/select_n | solution.py:270
  11.2 3.8 %collective-permute-start.11 = (bf16[384,384]{1,0:T(8,128)(2,1)S(1)}, bf16[384,384]{1,0:T(8,128)(2,1)S(1)}, u32[]{:S(2)}, u32[]{:S(2)}) collective-permute-start(bf16[384,384]{1,0:T(8,128)(2,1)S(1)} %broadcast_select_fusion), channel_id=1, source_target_pairs={{0,5},{2,7},{5,0},{7,2},{8,13},{10,15},{13,8},{15,10},{16,21},{18,... | collective-permute-start | bytes 884744 | tf_op jit(solution)/shard_map/ppermute | solution.py:67
  15.0 0.7 %collective-permute-start.10 = (bf16[384,384]{1,0:T(8,128)(2,1)S(1)}, bf16[384,384]{1,0:T(8,128)(2,1)S(1)}, u32[]{:S(2)}, u32[]{:S(2)}) collective-permute-start(bf16[384,384]{1,0:T(8,128)(2,1)S(1)} %collective-permute-done.1.refs_2_), channel_id=1, source_target_pairs={{2,4},{7,1},{8,14},{13,11},{18,20},{23,17},{24,30},{29,27}} | collective-permute-start | bytes 884744 | tf_op jit(solution)/shard_map/ppermute | solution.py:67
  15.7 3.7 %collective-permute-done.3.refs_4_ = bf16[384,384]{1,0:T(8,128)(2,1)S(1)} collective-permute-done((bf16[384,384]{1,0:T(8,128)(2,1)}, bf16[384,384]{1,0:T(8,128)(2,1)S(1)}, u32[]{:S(2)}, u32[]{:S(2)}) %collective-permute-start.3) | collective-permute-done | bytes 294944 | tf_op jit(solution)/shard_map/ppermute | solution.py:67
  19.5 0.0 collective-permute-done.refs_1_
  19.5 0.0 collective-permute-done.2.refs_3_
  19.5 0.7 %collective-permute-start.9 = (bf16[384,384]{1,0:T(8,128)(2,1)S(1)}, bf16[384,384]{1,0:T(8,128)(2,1)S(1)}, u32[]{:S(2)}, u32[]{:S(2)}) collective-permute-start(bf16[384,384]{1,0:T(8,128)(2,1)S(1)} %collective-permute-done.3.refs_4_), channel_id=1, source_target_pairs={{3,6},{6,3},{9,12},{12,9},{19,22},{22,19},{25,28},{28,25}} | collective-permute-start | bytes 884744 | tf_op jit(solution)/shard_map/ppermute | solution.py:67
  20.1 0.1 collective-permute-start.8
  20.2 1.9 %collective-permute-start.4 = (bf16[384,384]{1,0:T(8,128)(2,1)S(1)}, bf16[384,384]{1,0:T(8,128)(2,1)S(1)}, u32[]{:S(2)}, u32[]{:S(2)}) collective-permute-start(bf16[384,384]{1,0:T(8,128)(2,1)S(1)} %collective-permute-done.3.refs_4_), channel_id=1, source_target_pairs={{0,8},{1,9},{2,10},{3,11},{4,12},{5,13},{6,14},{7,15},{8,0},{9,1},... | collective-permute-start | bytes 884744 | tf_op jit(solution)/shard_map/ppermute | solution.py:67
  22.1 0.0 collective-permute-done.11
  22.1 0.4 %collective-permute-start.7 = (s32[12,12]{1,0:T(8,128)}, s32[12,12]{1,0:T(8,128)S(1)}, u32[]{:S(2)}, u32[]{:S(2)}) collective-permute-start(s32[12,12]{1,0:T(8,128)} %refs_3_), channel_id=1, source_target_pairs={{0,3},{1,2},{2,1},{3,0},{4,7},{5,6},{6,5},{7,4},{8,11},{9,10},{10,... | collective-permute-start | bytes 1736 | tf_op jit(solution)/shard_map/ppermute | solution.py:277
  22.5 0.0 collective-permute-done.10
  22.5 3.1 %collective-permute-start.6 = (s32[12,12]{1,0:T(8,128)}, s32[12,12]{1,0:T(8,128)S(1)}, u32[]{:S(2)}, u32[]{:S(2)}) collective-permute-start(s32[12,12]{1,0:T(8,128)} %refs_3_), channel_id=1, source_target_pairs={{0,2},{1,3},{2,0},{3,1},{4,6},{5,7},{6,4},{7,5},{8,10},{9,11},{10,... | collective-permute-start | bytes 1736 | tf_op jit(solution)/shard_map/ppermute | solution.py:277
  25.7 0.0 collective-permute-done.9
  25.7 0.9 %collective-permute-start.5 = (s32[12,12]{1,0:T(8,128)}, s32[12,12]{1,0:T(8,128)S(1)}, u32[]{:S(2)}, u32[]{:S(2)}) collective-permute-start(s32[12,12]{1,0:T(8,128)} %refs_3_), channel_id=1, source_target_pairs={{0,1},{1,0},{2,3},{3,2},{4,5},{5,4},{6,7},{7,6},{8,9},{9,8},{10,11... | collective-permute-start | bytes 1736 | tf_op jit(solution)/shard_map/ppermute | solution.py:277
  26.6 0.0 collective-permute-done.8.refs_5_
  26.6 0.1 collective-permute-start.12
  26.7 0.0 copy-start
  26.7 1.0 %copy-done = bf16[384,384]{1,0:T(8,128)(2,1)S(1)} copy-done((bf16[384,384]{1,0:T(8,128)(2,1)S(1)}, bf16[384,384]{1,0:T(8,128)(2,1)}, u32[]{:S(2)}) %copy-start) | copy-done | bytes 294936
  27.7 1.0 %early.1.full_in = bf16[1536,1536]{1,0:T(8,128)(2,1)S(1)} custom-call(bf16[384,384]{1,0:T(8,128)(2,1)S(1)} %copy-done, bf16[384,384]{1,0:T(8,128)(2,1)S(1)} %collective-permute-done.refs_1_, bf16[384,384]{1,0:T(8,128)(2,1)S(1)} %collective-permute-done.1.refs_2_, bf16[384,384]{1,0:T(8,128)(2,1)S(1)} %collective-permute-done.2.refs_3_, ...), custom_call_target="tpu_custom_call" | custom-call | tf_op jit(solution)/shard_map/early/pallas_call | solution.py:211
  28.6 0.0 collective-permute-done.7.refs_6_
  28.6 0.9 %collective-permute-done.5.refs_4_ = s32[12,12]{1,0:T(8,128)S(1)} collective-permute-done((s32[12,12]{1,0:T(8,128)}, s32[12,12]{1,0:T(8,128)S(1)}, u32[]{:S(2)}, u32[]{:S(2)}) %collective-permute-start.5) | collective-permute-done | bytes 608 | tf_op jit(solution)/shard_map/ppermute | solution.py:277
  29.5 0.1 collective-permute-done.4.refs_0_
  29.6 0.0 collective-permute-start.13
  29.6 0.0 collective-permute-done.12.refs_2_
  29.7 1.9 %middle.1 = (bf16[1536,1536]{1,0:T(8,128)(2,1)S(1)}, f32[12,1536]{1,0:T(8,128)S(1)}, f32[384,1536]{1,0:T(8,128)S(1)}, bf16[384,1536]{1,0:T(8,128)(2,1)S(1)}) custom-call(bf16[1536,1536]{1,0:T(8,128)(2,1)S(1)} %early.1.full_in, bf16[384,384]{1,0:T(8,128)(2,1)S(1)} %collective-permute-done.4.refs_0_, ...), custom_call_target="tpu_custom_call", output_to_operand_aliasing={{0}: (0, {})} | custom-call | tf_op jit(solution)/shard_map/middle/pallas_call | solution.py:226
  31.6 2.7 %purify.1 = (bf16[384,384]{1,0:T(8,128)(2,1)}, bf16[1536,1536]{1,0:T(8,128)(2,1)S(1)}, f32[384,1536]{1,0:T(8,128)S(1)}, bf16[384,1536]{1,0:T(8,128)(2,1)S(1)}) custom-call(bf16[1536,1536]{1,0:T(8,128)(2,1)S(1)} %get-tuple-element.34.full_in, f32[12,1536]{1,0:T(8,128)S(1)} %get-tuple-element.35.rows, ...), custom_call_target="tpu_custom_call", output_to_operand_aliasing={{1}: (0, {}), {2}: (2, {}), {3}: (3, {})} | custom-call | tf_op jit(solution)/shard_map/purify/pallas_call | solution.py:248
  (5 shorter events, 0.1 us)
Async XLA Ops:
  0.0 10.2 %collective-permute-start.1 = (bf16[384,384]{1,0:T(8,128)(2,1)}, bf16[384,384]{1,0:T(8,128)(2,1)S(1)}, u32[]{:S(2)}, u32[]{:S(2)}) collective-permute-start(bf16[384,384]{1,0:T(8,128)(2,1)} %refs_0_.1), channel_id=1, source_target_pairs={{0,8},{1,9},{2,10},{3,11},{4,12},{5,13},{6,14},{7,15},{8,0},{9,1},... | collective-permute-start | bytes 884744 | tf_op jit(solution)/shard_map/ppermute | solution.py:67
  3.0 16.5 %collective-permute-start.3 = (bf16[384,384]{1,0:T(8,128)(2,1)}, bf16[384,384]{1,0:T(8,128)(2,1)S(1)}, u32[]{:S(2)}, u32[]{:S(2)}) collective-permute-start(bf16[384,384]{1,0:T(8,128)(2,1)} %refs_0_.1), channel_id=1, source_target_pairs={{8,11},{9,15},{12,10},{13,14},{10,9},{14,13},{11,8},{15,12},{7,4},... | collective-permute-start | bytes 884744 | tf_op jit(solution)/shard_map/ppermute | solution.py:67
  6.6 12.9 %collective-permute-start = (bf16[384,384]{1,0:T(8,128)(2,1)}, bf16[384,384]{1,0:T(8,128)(2,1)S(1)}, u32[]{:S(2)}, u32[]{:S(2)}) collective-permute-start(bf16[384,384]{1,0:T(8,128)(2,1)} %refs_0_.1), channel_id=1, source_target_pairs={{0,4},{1,5},{2,6},{3,7},{4,0},{5,1},{6,2},{7,3},{8,12},{9,13},{10,... | collective-permute-start | bytes 884744 | tf_op jit(solution)/shard_map/ppermute | solution.py:67
  10.2 9.3 %collective-permute-start.2 = (bf16[384,384]{1,0:T(8,128)(2,1)S(1)}, bf16[384,384]{1,0:T(8,128)(2,1)S(1)}, u32[]{:S(2)}, u32[]{:S(2)}) collective-permute-start(bf16[384,384]{1,0:T(8,128)(2,1)S(1)} %collective-permute-done.1.refs_2_), channel_id=1, source_target_pairs={{0,4},{1,5},{2,6},{3,7},{4,0},{5,1},{6,2},{7,3},{8,12},{9,13},{10,... | collective-permute-start | bytes 884744 | tf_op jit(solution)/shard_map/ppermute | solution.py:67
  11.2 11.0 %collective-permute-start.11 = (bf16[384,384]{1,0:T(8,128)(2,1)S(1)}, bf16[384,384]{1,0:T(8,128)(2,1)S(1)}, u32[]{:S(2)}, u32[]{:S(2)}) collective-permute-start(bf16[384,384]{1,0:T(8,128)(2,1)S(1)} %broadcast_select_fusion), channel_id=1, source_target_pairs={{0,5},{2,7},{5,0},{7,2},{8,13},{10,15},{13,8},{15,10},{16,21},{18,... | collective-permute-start | bytes 884744 | tf_op jit(solution)/shard_map/ppermute | solution.py:67
  15.0 7.5 %collective-permute-start.10 = (bf16[384,384]{1,0:T(8,128)(2,1)S(1)}, bf16[384,384]{1,0:T(8,128)(2,1)S(1)}, u32[]{:S(2)}, u32[]{:S(2)}) collective-permute-start(bf16[384,384]{1,0:T(8,128)(2,1)S(1)} %collective-permute-done.1.refs_2_), channel_id=1, source_target_pairs={{2,4},{7,1},{8,14},{13,11},{18,20},{23,17},{24,30},{29,27}} | collective-permute-start | bytes 884744 | tf_op jit(solution)/shard_map/ppermute | solution.py:67
  19.5 6.2 %collective-permute-start.9 = (bf16[384,384]{1,0:T(8,128)(2,1)S(1)}, bf16[384,384]{1,0:T(8,128)(2,1)S(1)}, u32[]{:S(2)}, u32[]{:S(2)}) collective-permute-start(bf16[384,384]{1,0:T(8,128)(2,1)S(1)} %collective-permute-done.3.refs_4_), channel_id=1, source_target_pairs={{3,6},{6,3},{9,12},{12,9},{19,22},{22,19},{25,28},{28,25}} | collective-permute-start | bytes 884744 | tf_op jit(solution)/shard_map/ppermute | solution.py:67
  20.1 6.5 %collective-permute-start.8 = (bf16[384,384]{1,0:T(8,128)(2,1)S(1)}, bf16[384,384]{1,0:T(8,128)(2,1)S(1)}, u32[]{:S(2)}, u32[]{:S(2)}) collective-permute-start(bf16[384,384]{1,0:T(8,128)(2,1)S(1)} %collective-permute-done.3.refs_4_), channel_id=1, source_target_pairs={{0,4},{1,5},{2,6},{3,7},{4,0},{5,1},{6,2},{7,3},{8,12},{9,13},{10,... | collective-permute-start | bytes 884744 | tf_op jit(solution)/shard_map/ppermute | solution.py:67
  20.2 9.4 %collective-permute-start.4 = (bf16[384,384]{1,0:T(8,128)(2,1)S(1)}, bf16[384,384]{1,0:T(8,128)(2,1)S(1)}, u32[]{:S(2)}, u32[]{:S(2)}) collective-permute-start(bf16[384,384]{1,0:T(8,128)(2,1)S(1)} %collective-permute-done.3.refs_4_), channel_id=1, source_target_pairs={{0,8},{1,9},{2,10},{3,11},{4,12},{5,13},{6,14},{7,15},{8,0},{9,1},... | collective-permute-start | bytes 884744 | tf_op jit(solution)/shard_map/ppermute | solution.py:67
  22.1 6.5 %collective-permute-start.7 = (s32[12,12]{1,0:T(8,128)}, s32[12,12]{1,0:T(8,128)S(1)}, u32[]{:S(2)}, u32[]{:S(2)}) collective-permute-start(s32[12,12]{1,0:T(8,128)} %refs_3_), channel_id=1, source_target_pairs={{0,3},{1,2},{2,1},{3,0},{4,7},{5,6},{6,5},{7,4},{8,11},{9,10},{10,... | collective-permute-start | bytes 1736 | tf_op jit(solution)/shard_map/ppermute | solution.py:277
  22.5 6.1 %collective-permute-start.6 = (s32[12,12]{1,0:T(8,128)}, s32[12,12]{1,0:T(8,128)S(1)}, u32[]{:S(2)}, u32[]{:S(2)}) collective-permute-start(s32[12,12]{1,0:T(8,128)} %refs_3_), channel_id=1, source_target_pairs={{0,2},{1,3},{2,0},{3,1},{4,6},{5,7},{6,4},{7,5},{8,10},{9,11},{10,... | collective-permute-start | bytes 1736 | tf_op jit(solution)/shard_map/ppermute | solution.py:277
  25.7 3.9 %collective-permute-start.5 = (s32[12,12]{1,0:T(8,128)}, s32[12,12]{1,0:T(8,128)S(1)}, u32[]{:S(2)}, u32[]{:S(2)}) collective-permute-start(s32[12,12]{1,0:T(8,128)} %refs_3_), channel_id=1, source_target_pairs={{0,1},{1,0},{2,3},{3,2},{4,5},{5,4},{6,7},{7,6},{8,9},{9,8},{10,11... | collective-permute-start | bytes 1736 | tf_op jit(solution)/shard_map/ppermute | solution.py:277
  26.5 3.1 %copy-start.1 = (s32[12,12]{1,0:T(8,128)S(1)}, s32[12,12]{1,0:T(8,128)}, u32[]{:S(2)}) copy-start(s32[12,12]{1,0:T(8,128)} %refs_3_) | copy-start | bytes 1732
  26.6 3.0 %collective-permute-start.12 = (bf16[384,384]{1,0:T(8,128)(2,1)S(1)}, bf16[384,384]{1,0:T(8,128)(2,1)S(1)}, u32[]{:S(2)}, u32[]{:S(2)}) collective-permute-start(bf16[384,384]{1,0:T(8,128)(2,1)S(1)} %select_select_fusion.refs_1_), channel_id=1, source_target_pairs={{0,4},{1,5},{2,6},{3,7},{4,0},{5,1},{6,2},{7,3},{8,12},{9,13},{10,... | collective-permute-start | bytes 884744 | tf_op jit(solution)/shard_map/ppermute | solution.py:67
  26.7 1.0 %copy-start = (bf16[384,384]{1,0:T(8,128)(2,1)S(1)}, bf16[384,384]{1,0:T(8,128)(2,1)}, u32[]{:S(2)}) copy-start(bf16[384,384]{1,0:T(8,128)(2,1)} %refs_0_.1) | copy-start | bytes 884740
  29.6 2.0 %collective-permute-start.13 = (bf16[384,384]{1,0:T(8,128)(2,1)S(1)}, bf16[384,384]{1,0:T(8,128)(2,1)S(1)}, u32[]{:S(2)}, u32[]{:S(2)}) collective-permute-start(bf16[384,384]{1,0:T(8,128)(2,1)S(1)} %collective-permute-done.4.refs_0_), channel_id=1, source_target_pairs={{0,4},{1,5},{2,6},{3,7},{4,0},{5,1},{6,2},{7,3},{8,12},{9,13},{10,... | collective-permute-start | bytes 884744 | tf_op jit(solution)/shard_map/ppermute | solution.py:67

commit v7 on v6

--- a/solution.py
+++ b/solution.py
@@ -46,8 +46,8 @@
 
 LINE = turned(
     [
-        ((2, 0), (2, 3)),
-        ((2, 1), (3, 3)),
+        ((2, 0), (3, 3)),
+        ((2, 1), (2, 3)),
         ((3, 0), (2, 2)),
         ((3, 1), (3, 2)),
         ((2, 2), (2, 1)),

time: 34.5 us -> 34.3 us (level)
  waiting for transfers between devices: 8.38 us -> 4.39 us
  starting transfers between devices: 18.2 us -> 21.9 us
    ppermute x11, waiting for transfers between devices: 7.5 us -> 3.7 us  [send(): return lax.ppermute(array, AXES, moves)]
    ppermute x11, starting transfers between devices: 13.8 us -> 17.5 us  [send(): return lax.ppermute(array, AXES, moves)]
  transfers between devices with their start and end apart: 14 -> 14, of which waited for: 4 -> 3; matrix products, arithmetic and copies ran while one was open for 3% -> 3% of each run, Pallas kernels for 8% -> 9%
where the time goes in v7:
time: 34.3 us; the launch traced here: 34 us
  starting transfers between devices  21.9 us (64%)
  Pallas kernels  5.57 us (16%)
  waiting for transfers between devices  4.39 us (13%)
  other arithmetic  1.05 us (3%)
  local copies, waits for them, and re-layouts  0.96 us (3%)
    ppermute x11, starting transfers between devices, send(): return lax.ppermute(array, AXES, moves)  17.5 us
    ppermute x3, starting transfers between devices, block_body(): lax.ppermute(pattern, 'narrow', [(c, c ^ k) for c in range(4)])  4.39 us
    ppermute x11, waiting for transfers between devices, send(): return lax.ppermute(array, AXES, moves)  3.7 us
    pallas_call x1, Pallas kernels, purify(): pl.pallas_call(purify_kernel, out_shape=(jax.ShapeDtypeStruct((edge, edge...  2.67 us
    pallas_call x1, Pallas kernels, middle(): pl.pallas_call(middle_kernel, out_shape=(pltpu.VMEM((order, order), BF16)...  1.93 us
    select_n x1, other arithmetic, block_body(): near = send(jnp.where(kind == 0, own, across), NEAR_DIAGONAL)  1 us
    pallas_call x1, Pallas kernels, early(): pl.pallas_call(early_kernel, out_shape=pltpu.VMEM((order, order), BF16),...  0.96 us
    unnamed x4, local copies, waits for them, and re-layouts  0.96 us
  transfers between devices with their start and end apart: 14, of which 3 were waited for; matrix products, arithmetic and copies ran while one was open for 3% of the time, Pallas kernels for 9%

profile of v7, /device:TPU:0, one launch (start us, length us, event | category | flops | bytes accessed | tf_op | source)
XLA Modules:
  0.0 34.0 jit_solution(11546008750852793490)
XLA Ops:
  0.0 3.0 %collective-permute-start.1 = (bf16[384,384]{1,0:T(8,128)(2,1)}, bf16[384,384]{1,0:T(8,128)(2,1)S(1)}, u32[]{:S(2)}, u32[]{:S(2)}) collective-permute-start(bf16[384,384]{1,0:T(8,128)(2,1)} %refs_0_.1), channel_id=1, source_target_pairs={{0,8},{1,9},{2,10},{3,11},{4,12},{5,13},{6,14},{7,15},{8,0},{9,1},... | collective-permute-start | bytes 884744 | tf_op jit(solution)/shard_map/ppermute | solution.py:67
  3.0 3.6 %collective-permute-start.3 = (bf16[384,384]{1,0:T(8,128)(2,1)}, bf16[384,384]{1,0:T(8,128)(2,1)S(1)}, u32[]{:S(2)}, u32[]{:S(2)}) collective-permute-start(bf16[384,384]{1,0:T(8,128)(2,1)} %refs_0_.1), channel_id=1, source_target_pairs={{8,15},{9,11},{12,10},{13,14},{10,9},{14,13},{11,8},{15,12},{7,0},... | collective-permute-start | bytes 884744 | tf_op jit(solution)/shard_map/ppermute | solution.py:67
  6.6 0.0 collective-permute-start
  6.6 3.6 %collective-permute-done.1.refs_2_ = bf16[384,384]{1,0:T(8,128)(2,1)S(1)} collective-permute-done((bf16[384,384]{1,0:T(8,128)(2,1)}, bf16[384,384]{1,0:T(8,128)(2,1)S(1)}, u32[]{:S(2)}, u32[]{:S(2)}) %collective-permute-start.1) | collective-permute-done | bytes 294944 | tf_op jit(solution)/shard_map/ppermute | solution.py:67
  10.2 0.0 collective-permute-start.2
  10.2 1.0 %broadcast_select_fusion = bf16[384,384]{1,0:T(8,128)(2,1)S(1)} fusion(bf16[384,384]{1,0:T(8,128)(2,1)} %refs_0_.1, bf16[384,384]{1,0:T(8,128)(2,1)S(1)} %collective-permute-done.1.refs_2_, pred[]{:T(512)S(6)} %eq.11), kind=kLoop, calls=%fused_computation.1 | loop fusion | flops 147456 | bytes 884737 | tf_op jit(solution)/shard_map/jit(_where)/select_n | solution.py:270
  11.2 3.8 %collective-permute-start.11 = (bf16[384,384]{1,0:T(8,128)(2,1)S(1)}, bf16[384,384]{1,0:T(8,128)(2,1)S(1)}, u32[]{:S(2)}, u32[]{:S(2)}) collective-permute-start(bf16[384,384]{1,0:T(8,128)(2,1)S(1)} %broadcast_select_fusion), channel_id=1, source_target_pairs={{0,5},{2,7},{5,0},{7,2},{8,13},{10,15},{13,8},{15,10},{16,21},{18,... | collective-permute-start | bytes 884744 | tf_op jit(solution)/shard_map/ppermute | solution.py:67
  15.0 0.7 %collective-permute-start.10 = (bf16[384,384]{1,0:T(8,128)(2,1)S(1)}, bf16[384,384]{1,0:T(8,128)(2,1)S(1)}, u32[]{:S(2)}, u32[]{:S(2)}) collective-permute-start(bf16[384,384]{1,0:T(8,128)(2,1)S(1)} %collective-permute-done.1.refs_2_), channel_id=1, source_target_pairs={{2,4},{7,1},{8,14},{13,11},{18,20},{23,17},{24,30},{29,27}} | collective-permute-start | bytes 884744 | tf_op jit(solution)/shard_map/ppermute | solution.py:67
  15.7 0.0 collective-permute-done.3.refs_4_
  15.7 0.0 collective-permute-done.refs_1_
  15.7 0.0 collective-permute-done.2.refs_3_
  15.7 0.7 %collective-permute-start.9 = (bf16[384,384]{1,0:T(8,128)(2,1)S(1)}, bf16[384,384]{1,0:T(8,128)(2,1)S(1)}, u32[]{:S(2)}, u32[]{:S(2)}) collective-permute-start(bf16[384,384]{1,0:T(8,128)(2,1)S(1)} %collective-permute-done.3.refs_4_), channel_id=1, source_target_pairs={{3,6},{6,3},{9,12},{12,9},{19,22},{22,19},{25,28},{28,25}} | collective-permute-start | bytes 884744 | tf_op jit(solution)/shard_map/ppermute | solution.py:67
  16.4 1.4 %collective-permute-start.8 = (bf16[384,384]{1,0:T(8,128)(2,1)S(1)}, bf16[384,384]{1,0:T(8,128)(2,1)S(1)}, u32[]{:S(2)}, u32[]{:S(2)}) collective-permute-start(bf16[384,384]{1,0:T(8,128)(2,1)S(1)} %collective-permute-done.3.refs_4_), channel_id=1, source_target_pairs={{0,4},{1,5},{2,6},{3,7},{4,0},{5,1},{6,2},{7,3},{8,12},{9,13},{10,... | collective-permute-start | bytes 884744 | tf_op jit(solution)/shard_map/ppermute | solution.py:67
  17.9 4.3 %collective-permute-start.4 = (bf16[384,384]{1,0:T(8,128)(2,1)S(1)}, bf16[384,384]{1,0:T(8,128)(2,1)S(1)}, u32[]{:S(2)}, u32[]{:S(2)}) collective-permute-start(bf16[384,384]{1,0:T(8,128)(2,1)S(1)} %collective-permute-done.3.refs_4_), channel_id=1, source_target_pairs={{0,8},{1,9},{2,10},{3,11},{4,12},{5,13},{6,14},{7,15},{8,0},{9,1},... | collective-permute-start | bytes 884744 | tf_op jit(solution)/shard_map/ppermute | solution.py:67
  22.1 0.0 collective-permute-done.11
  22.1 0.6 %collective-permute-start.7 = (s32[12,12]{1,0:T(8,128)}, s32[12,12]{1,0:T(8,128)S(1)}, u32[]{:S(2)}, u32[]{:S(2)}) collective-permute-start(s32[12,12]{1,0:T(8,128)} %refs_3_), channel_id=1, source_target_pairs={{0,3},{1,2},{2,1},{3,0},{4,7},{5,6},{6,5},{7,4},{8,11},{9,10},{10,... | collective-permute-start | bytes 1736 | tf_op jit(solution)/shard_map/ppermute | solution.py:277
  22.8 0.0 collective-permute-done.10
  22.8 2.7 %collective-permute-start.6 = (s32[12,12]{1,0:T(8,128)}, s32[12,12]{1,0:T(8,128)S(1)}, u32[]{:S(2)}, u32[]{:S(2)}) collective-permute-start(s32[12,12]{1,0:T(8,128)} %refs_3_), channel_id=1, source_target_pairs={{0,2},{1,3},{2,0},{3,1},{4,6},{5,7},{6,4},{7,5},{8,10},{9,11},{10,... | collective-permute-start | bytes 1736 | tf_op jit(solution)/shard_map/ppermute | solution.py:277
  25.5 0.0 collective-permute-done.9
  25.5 1.1 %collective-permute-start.5 = (s32[12,12]{1,0:T(8,128)}, s32[12,12]{1,0:T(8,128)S(1)}, u32[]{:S(2)}, u32[]{:S(2)}) collective-permute-start(s32[12,12]{1,0:T(8,128)} %refs_3_), channel_id=1, source_target_pairs={{0,1},{1,0},{2,3},{3,2},{4,5},{5,4},{6,7},{7,6},{8,9},{9,8},{10,11... | collective-permute-start | bytes 1736 | tf_op jit(solution)/shard_map/ppermute | solution.py:277
  26.6 0.0 collective-permute-done.8.refs_5_
  26.6 0.1 collective-permute-start.12
  26.7 0.0 copy-start
  26.7 1.0 %copy-done = bf16[384,384]{1,0:T(8,128)(2,1)S(1)} copy-done((bf16[384,384]{1,0:T(8,128)(2,1)S(1)}, bf16[384,384]{1,0:T(8,128)(2,1)}, u32[]{:S(2)}) %copy-start) | copy-done | bytes 294936
  27.7 1.0 %early.1.full_in = bf16[1536,1536]{1,0:T(8,128)(2,1)S(1)} custom-call(bf16[384,384]{1,0:T(8,128)(2,1)S(1)} %copy-done, bf16[384,384]{1,0:T(8,128)(2,1)S(1)} %collective-permute-done.refs_1_, bf16[384,384]{1,0:T(8,128)(2,1)S(1)} %collective-permute-done.1.refs_2_, bf16[384,384]{1,0:T(8,128)(2,1)S(1)} %collective-permute-done.2.refs_3_, ...), custom_call_target="tpu_custom_call" | custom-call | tf_op jit(solution)/shard_map/early/pallas_call | solution.py:211
  28.6 0.0 collective-permute-done.7.refs_6_
  28.6 0.0 collective-permute-done.6.refs_5_
  28.6 0.7 %collective-permute-done.5.refs_4_ = s32[12,12]{1,0:T(8,128)S(1)} collective-permute-done((s32[12,12]{1,0:T(8,128)}, s32[12,12]{1,0:T(8,128)S(1)}, u32[]{:S(2)}, u32[]{:S(2)}) %collective-permute-start.5) | collective-permute-done | bytes 608 | tf_op jit(solution)/shard_map/ppermute | solution.py:277
  29.3 0.1 collective-permute-done.4.refs_0_
  29.4 0.0 collective-permute-start.13
  29.4 1.9 %middle.1 = (bf16[1536,1536]{1,0:T(8,128)(2,1)S(1)}, f32[12,1536]{1,0:T(8,128)S(1)}, f32[384,1536]{1,0:T(8,128)S(1)}, bf16[384,1536]{1,0:T(8,128)(2,1)S(1)}) custom-call(bf16[1536,1536]{1,0:T(8,128)(2,1)S(1)} %early.1.full_in, bf16[384,384]{1,0:T(8,128)(2,1)S(1)} %collective-permute-done.4.refs_0_, ...), custom_call_target="tpu_custom_call", output_to_operand_aliasing={{0}: (0, {})} | custom-call | tf_op jit(solution)/shard_map/middle/pallas_call | solution.py:226
  31.4 2.7 %purify.1 = (bf16[384,384]{1,0:T(8,128)(2,1)}, bf16[1536,1536]{1,0:T(8,128)(2,1)S(1)}, f32[384,1536]{1,0:T(8,128)S(1)}, bf16[384,1536]{1,0:T(8,128)(2,1)S(1)}) custom-call(bf16[1536,1536]{1,0:T(8,128)(2,1)S(1)} %get-tuple-element.34.full_in, f32[12,1536]{1,0:T(8,128)S(1)} %get-tuple-element.35.rows, ...), custom_call_target="tpu_custom_call", output_to_operand_aliasing={{1}: (0, {}), {2}: (2, {}), {3}: (3, {})} | custom-call | tf_op jit(solution)/shard_map/purify/pallas_call | solution.py:248
  (5 shorter events, 0.1 us)
Async XLA Ops:
  0.0 10.2 %collective-permute-start.1 = (bf16[384,384]{1,0:T(8,128)(2,1)}, bf16[384,384]{1,0:T(8,128)(2,1)S(1)}, u32[]{:S(2)}, u32[]{:S(2)}) collective-permute-start(bf16[384,384]{1,0:T(8,128)(2,1)} %refs_0_.1), channel_id=1, source_target_pairs={{0,8},{1,9},{2,10},{3,11},{4,12},{5,13},{6,14},{7,15},{8,0},{9,1},... | collective-permute-start | bytes 884744 | tf_op jit(solution)/shard_map/ppermute | solution.py:67
  3.0 12.7 %collective-permute-start.3 = (bf16[384,384]{1,0:T(8,128)(2,1)}, bf16[384,384]{1,0:T(8,128)(2,1)S(1)}, u32[]{:S(2)}, u32[]{:S(2)}) collective-permute-start(bf16[384,384]{1,0:T(8,128)(2,1)} %refs_0_.1), channel_id=1, source_target_pairs={{8,15},{9,11},{12,10},{13,14},{10,9},{14,13},{11,8},{15,12},{7,0},... | collective-permute-start | bytes 884744 | tf_op jit(solution)/shard_map/ppermute | solution.py:67
  6.6 9.1 %collective-permute-start = (bf16[384,384]{1,0:T(8,128)(2,1)}, bf16[384,384]{1,0:T(8,128)(2,1)S(1)}, u32[]{:S(2)}, u32[]{:S(2)}) collective-permute-start(bf16[384,384]{1,0:T(8,128)(2,1)} %refs_0_.1), channel_id=1, source_target_pairs={{0,4},{1,5},{2,6},{3,7},{4,0},{5,1},{6,2},{7,3},{8,12},{9,13},{10,... | collective-permute-start | bytes 884744 | tf_op jit(solution)/shard_map/ppermute | solution.py:67
  10.2 5.5 %collective-permute-start.2 = (bf16[384,384]{1,0:T(8,128)(2,1)S(1)}, bf16[384,384]{1,0:T(8,128)(2,1)S(1)}, u32[]{:S(2)}, u32[]{:S(2)}) collective-permute-start(bf16[384,384]{1,0:T(8,128)(2,1)S(1)} %collective-permute-done.1.refs_2_), channel_id=1, source_target_pairs={{0,4},{1,5},{2,6},{3,7},{4,0},{5,1},{6,2},{7,3},{8,12},{9,13},{10,... | collective-permute-start | bytes 884744 | tf_op jit(solution)/shard_map/ppermute | solution.py:67
  11.2 11.0 %collective-permute-start.11 = (bf16[384,384]{1,0:T(8,128)(2,1)S(1)}, bf16[384,384]{1,0:T(8,128)(2,1)S(1)}, u32[]{:S(2)}, u32[]{:S(2)}) collective-permute-start(bf16[384,384]{1,0:T(8,128)(2,1)S(1)} %broadcast_select_fusion), channel_id=1, source_target_pairs={{0,5},{2,7},{5,0},{7,2},{8,13},{10,15},{13,8},{15,10},{16,21},{18,... | collective-permute-start | bytes 884744 | tf_op jit(solution)/shard_map/ppermute | solution.py:67
  15.0 7.8 %collective-permute-start.10 = (bf16[384,384]{1,0:T(8,128)(2,1)S(1)}, bf16[384,384]{1,0:T(8,128)(2,1)S(1)}, u32[]{:S(2)}, u32[]{:S(2)}) collective-permute-start(bf16[384,384]{1,0:T(8,128)(2,1)S(1)} %collective-permute-done.1.refs_2_), channel_id=1, source_target_pairs={{2,4},{7,1},{8,14},{13,11},{18,20},{23,17},{24,30},{29,27}} | collective-permute-start | bytes 884744 | tf_op jit(solution)/shard_map/ppermute | solution.py:67
  15.7 9.7 %collective-permute-start.9 = (bf16[384,384]{1,0:T(8,128)(2,1)S(1)}, bf16[384,384]{1,0:T(8,128)(2,1)S(1)}, u32[]{:S(2)}, u32[]{:S(2)}) collective-permute-start(bf16[384,384]{1,0:T(8,128)(2,1)S(1)} %collective-permute-done.3.refs_4_), channel_id=1, source_target_pairs={{3,6},{6,3},{9,12},{12,9},{19,22},{22,19},{25,28},{28,25}} | collective-permute-start | bytes 884744 | tf_op jit(solution)/shard_map/ppermute | solution.py:67
  16.4 10.2 %collective-permute-start.8 = (bf16[384,384]{1,0:T(8,128)(2,1)S(1)}, bf16[384,384]{1,0:T(8,128)(2,1)S(1)}, u32[]{:S(2)}, u32[]{:S(2)}) collective-permute-start(bf16[384,384]{1,0:T(8,128)(2,1)S(1)} %collective-permute-done.3.refs_4_), channel_id=1, source_target_pairs={{0,4},{1,5},{2,6},{3,7},{4,0},{5,1},{6,2},{7,3},{8,12},{9,13},{10,... | collective-permute-start | bytes 884744 | tf_op jit(solution)/shard_map/ppermute | solution.py:67
  17.9 11.5 %collective-permute-start.4 = (bf16[384,384]{1,0:T(8,128)(2,1)S(1)}, bf16[384,384]{1,0:T(8,128)(2,1)S(1)}, u32[]{:S(2)}, u32[]{:S(2)}) collective-permute-start(bf16[384,384]{1,0:T(8,128)(2,1)S(1)} %collective-permute-done.3.refs_4_), channel_id=1, source_target_pairs={{0,8},{1,9},{2,10},{3,11},{4,12},{5,13},{6,14},{7,15},{8,0},{9,1},... | collective-permute-start | bytes 884744 | tf_op jit(solution)/shard_map/ppermute | solution.py:67
  22.1 6.5 %collective-permute-start.7 = (s32[12,12]{1,0:T(8,128)}, s32[12,12]{1,0:T(8,128)S(1)}, u32[]{:S(2)}, u32[]{:S(2)}) collective-permute-start(s32[12,12]{1,0:T(8,128)} %refs_3_), channel_id=1, source_target_pairs={{0,3},{1,2},{2,1},{3,0},{4,7},{5,6},{6,5},{7,4},{8,11},{9,10},{10,... | collective-permute-start | bytes 1736 | tf_op jit(solution)/shard_map/ppermute | solution.py:277
  22.8 5.8 %collective-permute-start.6 = (s32[12,12]{1,0:T(8,128)}, s32[12,12]{1,0:T(8,128)S(1)}, u32[]{:S(2)}, u32[]{:S(2)}) collective-permute-start(s32[12,12]{1,0:T(8,128)} %refs_3_), channel_id=1, source_target_pairs={{0,2},{1,3},{2,0},{3,1},{4,6},{5,7},{6,4},{7,5},{8,10},{9,11},{10,... | collective-permute-start | bytes 1736 | tf_op jit(solution)/shard_map/ppermute | solution.py:277
  25.5 3.9 %collective-permute-start.5 = (s32[12,12]{1,0:T(8,128)}, s32[12,12]{1,0:T(8,128)S(1)}, u32[]{:S(2)}, u32[]{:S(2)}) collective-permute-start(s32[12,12]{1,0:T(8,128)} %refs_3_), channel_id=1, source_target_pairs={{0,1},{1,0},{2,3},{3,2},{4,5},{5,4},{6,7},{7,6},{8,9},{9,8},{10,11... | collective-permute-start | bytes 1736 | tf_op jit(solution)/shard_map/ppermute | solution.py:277
  26.5 2.9 %copy-start.1 = (s32[12,12]{1,0:T(8,128)S(1)}, s32[12,12]{1,0:T(8,128)}, u32[]{:S(2)}) copy-start(s32[12,12]{1,0:T(8,128)} %refs_3_) | copy-start | bytes 1732
  26.6 2.8 %collective-permute-start.12 = (bf16[384,384]{1,0:T(8,128)(2,1)S(1)}, bf16[384,384]{1,0:T(8,128)(2,1)S(1)}, u32[]{:S(2)}, u32[]{:S(2)}) collective-permute-start(bf16[384,384]{1,0:T(8,128)(2,1)S(1)} %select_select_fusion.refs_1_), channel_id=1, source_target_pairs={{0,4},{1,5},{2,6},{3,7},{4,0},{5,1},{6,2},{7,3},{8,12},{9,13},{10,... | collective-permute-start | bytes 884744 | tf_op jit(solution)/shard_map/ppermute | solution.py:67
  26.7 1.0 %copy-start = (bf16[384,384]{1,0:T(8,128)(2,1)S(1)}, bf16[384,384]{1,0:T(8,128)(2,1)}, u32[]{:S(2)}) copy-start(bf16[384,384]{1,0:T(8,128)(2,1)} %refs_0_.1) | copy-start | bytes 884740
  29.4 2.0 %collective-permute-start.13 = (bf16[384,384]{1,0:T(8,128)(2,1)S(1)}, bf16[384,384]{1,0:T(8,128)(2,1)S(1)}, u32[]{:S(2)}, u32[]{:S(2)}) collective-permute-start(bf16[384,384]{1,0:T(8,128)(2,1)S(1)} %collective-permute-done.4.refs_0_), channel_id=1, source_target_pairs={{0,4},{1,5},{2,6},{3,7},{4,0},{5,1},{6,2},{7,3},{8,12},{9,13},{10,... | collective-permute-start | bytes 884744 | tf_op jit(solution)/shard_map/ppermute | solution.py:67

commit v8 on v7

--- a/solution.py
+++ b/solution.py
@@ -177,7 +177,7 @@
 
 
 def purify_kernel(full_in, rows, square_in, low_in, *refs):
-    blocks, (out, full, square, low, sems) = refs[:-5], refs[-5:]
+    blocks, (out, full, square, low, result, sems, done) = refs[:-7], refs[-7:]
     edge, order = square.shape
     mirror(place(10 - len(blocks), blocks, full, sems), full)
     i, j = lax.axis_index("wide"), lax.axis_index("narrow")
@@ -192,9 +192,17 @@
         square_columns(0, order // 256, full, rows, square, low)
 
     mine = block_at(edge, j)
-    cube = jnp.dot(low[...], full[:, mine], preferred_element_type=F32)
-    cube = masked(cube, rows[:, mine])
-    out[...] = (3.0 * square[:, mine] - 2.0 * cube).astype(BF16)
+    n = rows.shape[0]
+    writes = []
+    for part in range(2):
+        some = slice(part * edge // 2, (part + 1) * edge // 2)
+        cube = jnp.dot(low[some], full[:, mine], preferred_element_type=F32)
+        cube = masked(cube, rows[part * n // 2 : (part + 1) * n // 2, mine])
+        result[some] = (3.0 * square[some, mine] - 2.0 * cube).astype(BF16)
+        writes.append(pltpu.make_async_copy(result.at[some], out.at[some], done.at[part]))
+        writes[-1].start()
+    for write in writes:
+        write.wait()
 
 
 VMEM = pl.BlockSpec(memory_space=pltpu.VMEM)
@@ -254,9 +262,13 @@
             pltpu.VMEM((edge, order), BF16),
         ),
         in_specs=[VMEM] * 4 + [HBM] * len(blocks),
-        out_specs=(VMEM,) * 4,
+        out_specs=(HBM,) + (VMEM,) * 3,
         input_output_aliases={0: 1, 2: 2, 3: 3},
-        scratch_shapes=[pltpu.SemaphoreType.DMA((len(blocks),))],
+        scratch_shapes=[
+            pltpu.VMEM((edge, edge), BF16),
+            pltpu.SemaphoreType.DMA((len(blocks),)),
+            pltpu.SemaphoreType.DMA((2,)),
+        ],
         compiler_params=PARAMS,
         name="purify",
     )(*map(in_vmem, (full, rows, square, low)), *blocks)[0]
@@ -293,6 +305,7 @@
         rows, cols = density.shape
         fits = rows == cols and rows % 128 == 0 and rows <= 512
         fits = fits and pattern.shape[0] == pattern.shape[1] <= 16
+        fits = fits and pattern.shape[0] % 2 == 0
         return (block_body if four and fits else panel_body)(density, pattern)
 
     return jax.shard_map(

time: 34.3 us -> 34.2 us (level)
  no operation moved by 1% of the time
where the time goes in v8:
time: 34.2 us; the launch traced here: 34 us
  starting transfers between devices  21.9 us (64%)
  Pallas kernels  5.54 us (16%)
  waiting for transfers between devices  4.39 us (13%)
  other arithmetic  1.05 us (3%)
  local copies, waits for them, and re-layouts  0.96 us (3%)
    ppermute x11, starting transfers between devices, send(): return lax.ppermute(array, AXES, moves)  17.5 us
    ppermute x3, starting transfers between devices, block_body(): lax.ppermute(pattern, 'narrow', [(c, c ^ k) for c in range(4)])  4.39 us
    ppermute x11, waiting for transfers between devices, send(): return lax.ppermute(array, AXES, moves)  3.7 us
    pallas_call x1, Pallas kernels, purify(): pl.pallas_call(purify_kernel, out_shape=(jax.ShapeDtypeStruct((edge, edge...  2.64 us
    pallas_call x1, Pallas kernels, middle(): pl.pallas_call(middle_kernel, out_shape=(pltpu.VMEM((order, order), BF16)...  1.93 us
    select_n x1, other arithmetic, block_body(): near = send(jnp.where(kind == 0, own, across), NEAR_DIAGONAL)  1 us
    pallas_call x1, Pallas kernels, early(): pl.pallas_call(early_kernel, out_shape=pltpu.VMEM((order, order), BF16),...  0.96 us
    unnamed x4, local copies, waits for them, and re-layouts  0.96 us
  transfers between devices with their start and end apart: 14, of which 3 were waited for; matrix products, arithmetic and copies ran while one was open for 3% of the time, Pallas kernels for 9%

profile of v8, /device:TPU:0, one launch (start us, length us, event | category | flops | bytes accessed | tf_op | source)
XLA Modules:
  0.0 34.0 jit_solution(14699141604079915994)
XLA Ops:
  0.0 3.0 %collective-permute-start.1 = (bf16[384,384]{1,0:T(8,128)(2,1)}, bf16[384,384]{1,0:T(8,128)(2,1)S(1)}, u32[]{:S(2)}, u32[]{:S(2)}) collective-permute-start(bf16[384,384]{1,0:T(8,128)(2,1)} %refs_0_.1), channel_id=1, source_target_pairs={{0,8},{1,9},{2,10},{3,11},{4,12},{5,13},{6,14},{7,15},{8,0},{9,1},... | collective-permute-start | bytes 884744 | tf_op jit(solution)/shard_map/ppermute | solution.py:67
  3.0 3.6 %collective-permute-start.3 = (bf16[384,384]{1,0:T(8,128)(2,1)}, bf16[384,384]{1,0:T(8,128)(2,1)S(1)}, u32[]{:S(2)}, u32[]{:S(2)}) collective-permute-start(bf16[384,384]{1,0:T(8,128)(2,1)} %refs_0_.1), channel_id=1, source_target_pairs={{8,15},{9,11},{12,10},{13,14},{10,9},{14,13},{11,8},{15,12},{7,0},... | collective-permute-start | bytes 884744 | tf_op jit(solution)/shard_map/ppermute | solution.py:67
  6.6 0.0 collective-permute-start
  6.6 3.6 %collective-permute-done.1.refs_2_ = bf16[384,384]{1,0:T(8,128)(2,1)S(1)} collective-permute-done((bf16[384,384]{1,0:T(8,128)(2,1)}, bf16[384,384]{1,0:T(8,128)(2,1)S(1)}, u32[]{:S(2)}, u32[]{:S(2)}) %collective-permute-start.1) | collective-permute-done | bytes 294944 | tf_op jit(solution)/shard_map/ppermute | solution.py:67
  10.2 0.0 collective-permute-start.2
  10.2 1.0 %broadcast_select_fusion = bf16[384,384]{1,0:T(8,128)(2,1)S(1)} fusion(bf16[384,384]{1,0:T(8,128)(2,1)} %refs_0_.1, bf16[384,384]{1,0:T(8,128)(2,1)S(1)} %collective-permute-done.1.refs_2_, pred[]{:T(512)S(6)} %eq.11), kind=kLoop, calls=%fused_computation.1 | loop fusion | flops 147456 | bytes 884737 | tf_op jit(solution)/shard_map/jit(_where)/select_n | solution.py:282
  11.2 3.8 %collective-permute-start.11 = (bf16[384,384]{1,0:T(8,128)(2,1)S(1)}, bf16[384,384]{1,0:T(8,128)(2,1)S(1)}, u32[]{:S(2)}, u32[]{:S(2)}) collective-permute-start(bf16[384,384]{1,0:T(8,128)(2,1)S(1)} %broadcast_select_fusion), channel_id=1, source_target_pairs={{0,5},{2,7},{5,0},{7,2},{8,13},{10,15},{13,8},{15,10},{16,21},{18,... | collective-permute-start | bytes 884744 | tf_op jit(solution)/shard_map/ppermute | solution.py:67
  15.0 0.7 %collective-permute-start.10 = (bf16[384,384]{1,0:T(8,128)(2,1)S(1)}, bf16[384,384]{1,0:T(8,128)(2,1)S(1)}, u32[]{:S(2)}, u32[]{:S(2)}) collective-permute-start(bf16[384,384]{1,0:T(8,128)(2,1)S(1)} %collective-permute-done.1.refs_2_), channel_id=1, source_target_pairs={{2,4},{7,1},{8,14},{13,11},{18,20},{23,17},{24,30},{29,27}} | collective-permute-start | bytes 884744 | tf_op jit(solution)/shard_map/ppermute | solution.py:67
  15.7 0.0 collective-permute-done.3.refs_4_
  15.7 0.0 collective-permute-done.refs_1_
  15.7 0.0 collective-permute-done.2.refs_3_
  15.7 0.7 %collective-permute-start.9 = (bf16[384,384]{1,0:T(8,128)(2,1)S(1)}, bf16[384,384]{1,0:T(8,128)(2,1)S(1)}, u32[]{:S(2)}, u32[]{:S(2)}) collective-permute-start(bf16[384,384]{1,0:T(8,128)(2,1)S(1)} %collective-permute-done.3.refs_4_), channel_id=1, source_target_pairs={{3,6},{6,3},{9,12},{12,9},{19,22},{22,19},{25,28},{28,25}} | collective-permute-start | bytes 884744 | tf_op jit(solution)/shard_map/ppermute | solution.py:67
  16.4 1.4 %collective-permute-start.8 = (bf16[384,384]{1,0:T(8,128)(2,1)S(1)}, bf16[384,384]{1,0:T(8,128)(2,1)S(1)}, u32[]{:S(2)}, u32[]{:S(2)}) collective-permute-start(bf16[384,384]{1,0:T(8,128)(2,1)S(1)} %collective-permute-done.3.refs_4_), channel_id=1, source_target_pairs={{0,4},{1,5},{2,6},{3,7},{4,0},{5,1},{6,2},{7,3},{8,12},{9,13},{10,... | collective-permute-start | bytes 884744 | tf_op jit(solution)/shard_map/ppermute | solution.py:67
  17.9 4.3 %collective-permute-start.4 = (bf16[384,384]{1,0:T(8,128)(2,1)S(1)}, bf16[384,384]{1,0:T(8,128)(2,1)S(1)}, u32[]{:S(2)}, u32[]{:S(2)}) collective-permute-start(bf16[384,384]{1,0:T(8,128)(2,1)S(1)} %collective-permute-done.3.refs_4_), channel_id=1, source_target_pairs={{0,8},{1,9},{2,10},{3,11},{4,12},{5,13},{6,14},{7,15},{8,0},{9,1},... | collective-permute-start | bytes 884744 | tf_op jit(solution)/shard_map/ppermute | solution.py:67
  22.1 0.0 collective-permute-done.11
  22.1 0.6 %collective-permute-start.7 = (s32[12,12]{1,0:T(8,128)}, s32[12,12]{1,0:T(8,128)S(1)}, u32[]{:S(2)}, u32[]{:S(2)}) collective-permute-start(s32[12,12]{1,0:T(8,128)} %refs_3_), channel_id=1, source_target_pairs={{0,3},{1,2},{2,1},{3,0},{4,7},{5,6},{6,5},{7,4},{8,11},{9,10},{10,... | collective-permute-start | bytes 1736 | tf_op jit(solution)/shard_map/ppermute | solution.py:289
  22.8 0.0 collective-permute-done.10
  22.8 2.7 %collective-permute-start.6 = (s32[12,12]{1,0:T(8,128)}, s32[12,12]{1,0:T(8,128)S(1)}, u32[]{:S(2)}, u32[]{:S(2)}) collective-permute-start(s32[12,12]{1,0:T(8,128)} %refs_3_), channel_id=1, source_target_pairs={{0,2},{1,3},{2,0},{3,1},{4,6},{5,7},{6,4},{7,5},{8,10},{9,11},{10,... | collective-permute-start | bytes 1736 | tf_op jit(solution)/shard_map/ppermute | solution.py:289
  25.5 0.0 collective-permute-done.9
  25.5 1.1 %collective-permute-start.5 = (s32[12,12]{1,0:T(8,128)}, s32[12,12]{1,0:T(8,128)S(1)}, u32[]{:S(2)}, u32[]{:S(2)}) collective-permute-start(s32[12,12]{1,0:T(8,128)} %refs_3_), channel_id=1, source_target_pairs={{0,1},{1,0},{2,3},{3,2},{4,5},{5,4},{6,7},{7,6},{8,9},{9,8},{10,11... | collective-permute-start | bytes 1736 | tf_op jit(solution)/shard_map/ppermute | solution.py:289
  26.6 0.0 collective-permute-done.8.refs_5_
  26.6 0.1 collective-permute-start.12
  26.7 0.0 copy-start
  26.7 1.0 %copy-done = bf16[384,384]{1,0:T(8,128)(2,1)S(1)} copy-done((bf16[384,384]{1,0:T(8,128)(2,1)S(1)}, bf16[384,384]{1,0:T(8,128)(2,1)}, u32[]{:S(2)}) %copy-start) | copy-done | bytes 294936
  27.7 1.0 %early.1.full_in = bf16[1536,1536]{1,0:T(8,128)(2,1)S(1)} custom-call(bf16[384,384]{1,0:T(8,128)(2,1)S(1)} %copy-done, bf16[384,384]{1,0:T(8,128)(2,1)S(1)} %collective-permute-done.refs_1_, bf16[384,384]{1,0:T(8,128)(2,1)S(1)} %collective-permute-done.1.refs_2_, bf16[384,384]{1,0:T(8,128)(2,1)S(1)} %collective-permute-done.2.refs_3_, ...), custom_call_target="tpu_custom_call" | custom-call | tf_op jit(solution)/shard_map/early/pallas_call | solution.py:219
  28.6 0.0 collective-permute-done.7.refs_6_
  28.6 0.7 %collective-permute-done.5.refs_4_ = s32[12,12]{1,0:T(8,128)S(1)} collective-permute-done((s32[12,12]{1,0:T(8,128)}, s32[12,12]{1,0:T(8,128)S(1)}, u32[]{:S(2)}, u32[]{:S(2)}) %collective-permute-start.5) | collective-permute-done | bytes 608 | tf_op jit(solution)/shard_map/ppermute | solution.py:289
  29.3 0.1 collective-permute-done.4.refs_0_
  29.4 0.0 collective-permute-done.12.refs_2_
  29.4 1.9 %middle.1 = (bf16[1536,1536]{1,0:T(8,128)(2,1)S(1)}, f32[12,1536]{1,0:T(8,128)S(1)}, f32[384,1536]{1,0:T(8,128)S(1)}, bf16[384,1536]{1,0:T(8,128)(2,1)S(1)}) custom-call(bf16[1536,1536]{1,0:T(8,128)(2,1)S(1)} %early.1.full_in, bf16[384,384]{1,0:T(8,128)(2,1)S(1)} %collective-permute-done.4.refs_0_, ...), custom_call_target="tpu_custom_call", output_to_operand_aliasing={{0}: (0, {})} | custom-call | tf_op jit(solution)/shard_map/middle/pallas_call | solution.py:234
  31.4 0.0 collective-permute-done.13.refs_0_
  31.4 2.6 %purify.1 = (bf16[384,384]{1,0:T(8,128)(2,1)}, bf16[1536,1536]{1,0:T(8,128)(2,1)S(1)}, f32[384,1536]{1,0:T(8,128)S(1)}, bf16[384,1536]{1,0:T(8,128)(2,1)S(1)}) custom-call(bf16[1536,1536]{1,0:T(8,128)(2,1)S(1)} %get-tuple-element.34.full_in, f32[12,1536]{1,0:T(8,128)S(1)} %get-tuple-element.35.rows, ...), custom_call_target="tpu_custom_call", output_to_operand_aliasing={{1}: (0, {}), {2}: (2, {}), {3}: (3, {})} | custom-call | tf_op jit(solution)/shard_map/purify/pallas_call | solution.py:256
  (5 shorter events, 0.1 us)
Async XLA Ops:
  0.0 10.2 %collective-permute-start.1 = (bf16[384,384]{1,0:T(8,128)(2,1)}, bf16[384,384]{1,0:T(8,128)(2,1)S(1)}, u32[]{:S(2)}, u32[]{:S(2)}) collective-permute-start(bf16[384,384]{1,0:T(8,128)(2,1)} %refs_0_.1), channel_id=1, source_target_pairs={{0,8},{1,9},{2,10},{3,11},{4,12},{5,13},{6,14},{7,15},{8,0},{9,1},... | collective-permute-start | bytes 884744 | tf_op jit(solution)/shard_map/ppermute | solution.py:67
  3.0 12.7 %collective-permute-start.3 = (bf16[384,384]{1,0:T(8,128)(2,1)}, bf16[384,384]{1,0:T(8,128)(2,1)S(1)}, u32[]{:S(2)}, u32[]{:S(2)}) collective-permute-start(bf16[384,384]{1,0:T(8,128)(2,1)} %refs_0_.1), channel_id=1, source_target_pairs={{8,15},{9,11},{12,10},{13,14},{10,9},{14,13},{11,8},{15,12},{7,0},... | collective-permute-start | bytes 884744 | tf_op jit(solution)/shard_map/ppermute | solution.py:67
  6.6 9.1 %collective-permute-start = (bf16[384,384]{1,0:T(8,128)(2,1)}, bf16[384,384]{1,0:T(8,128)(2,1)S(1)}, u32[]{:S(2)}, u32[]{:S(2)}) collective-permute-start(bf16[384,384]{1,0:T(8,128)(2,1)} %refs_0_.1), channel_id=1, source_target_pairs={{0,4},{1,5},{2,6},{3,7},{4,0},{5,1},{6,2},{7,3},{8,12},{9,13},{10,... | collective-permute-start | bytes 884744 | tf_op jit(solution)/shard_map/ppermute | solution.py:67
  10.2 5.5 %collective-permute-start.2 = (bf16[384,384]{1,0:T(8,128)(2,1)S(1)}, bf16[384,384]{1,0:T(8,128)(2,1)S(1)}, u32[]{:S(2)}, u32[]{:S(2)}) collective-permute-start(bf16[384,384]{1,0:T(8,128)(2,1)S(1)} %collective-permute-done.1.refs_2_), channel_id=1, source_target_pairs={{0,4},{1,5},{2,6},{3,7},{4,0},{5,1},{6,2},{7,3},{8,12},{9,13},{10,... | collective-permute-start | bytes 884744 | tf_op jit(solution)/shard_map/ppermute | solution.py:67
  11.2 11.0 %collective-permute-start.11 = (bf16[384,384]{1,0:T(8,128)(2,1)S(1)}, bf16[384,384]{1,0:T(8,128)(2,1)S(1)}, u32[]{:S(2)}, u32[]{:S(2)}) collective-permute-start(bf16[384,384]{1,0:T(8,128)(2,1)S(1)} %broadcast_select_fusion), channel_id=1, source_target_pairs={{0,5},{2,7},{5,0},{7,2},{8,13},{10,15},{13,8},{15,10},{16,21},{18,... | collective-permute-start | bytes 884744 | tf_op jit(solution)/shard_map/ppermute | solution.py:67
  15.0 7.8 %collective-permute-start.10 = (bf16[384,384]{1,0:T(8,128)(2,1)S(1)}, bf16[384,384]{1,0:T(8,128)(2,1)S(1)}, u32[]{:S(2)}, u32[]{:S(2)}) collective-permute-start(bf16[384,384]{1,0:T(8,128)(2,1)S(1)} %collective-permute-done.1.refs_2_), channel_id=1, source_target_pairs={{2,4},{7,1},{8,14},{13,11},{18,20},{23,17},{24,30},{29,27}} | collective-permute-start | bytes 884744 | tf_op jit(solution)/shard_map/ppermute | solution.py:67
  15.7 9.7 %collective-permute-start.9 = (bf16[384,384]{1,0:T(8,128)(2,1)S(1)}, bf16[384,384]{1,0:T(8,128)(2,1)S(1)}, u32[]{:S(2)}, u32[]{:S(2)}) collective-permute-start(bf16[384,384]{1,0:T(8,128)(2,1)S(1)} %collective-permute-done.3.refs_4_), channel_id=1, source_target_pairs={{3,6},{6,3},{9,12},{12,9},{19,22},{22,19},{25,28},{28,25}} | collective-permute-start | bytes 884744 | tf_op jit(solution)/shard_map/ppermute | solution.py:67
  16.4 10.2 %collective-permute-start.8 = (bf16[384,384]{1,0:T(8,128)(2,1)S(1)}, bf16[384,384]{1,0:T(8,128)(2,1)S(1)}, u32[]{:S(2)}, u32[]{:S(2)}) collective-permute-start(bf16[384,384]{1,0:T(8,128)(2,1)S(1)} %collective-permute-done.3.refs_4_), channel_id=1, source_target_pairs={{0,4},{1,5},{2,6},{3,7},{4,0},{5,1},{6,2},{7,3},{8,12},{9,13},{10,... | collective-permute-start | bytes 884744 | tf_op jit(solution)/shard_map/ppermute | solution.py:67
  17.9 11.5 %collective-permute-start.4 = (bf16[384,384]{1,0:T(8,128)(2,1)S(1)}, bf16[384,384]{1,0:T(8,128)(2,1)S(1)}, u32[]{:S(2)}, u32[]{:S(2)}) collective-permute-start(bf16[384,384]{1,0:T(8,128)(2,1)S(1)} %collective-permute-done.3.refs_4_), channel_id=1, source_target_pairs={{0,8},{1,9},{2,10},{3,11},{4,12},{5,13},{6,14},{7,15},{8,0},{9,1},... | collective-permute-start | bytes 884744 | tf_op jit(solution)/shard_map/ppermute | solution.py:67
  22.1 6.5 %collective-permute-start.7 = (s32[12,12]{1,0:T(8,128)}, s32[12,12]{1,0:T(8,128)S(1)}, u32[]{:S(2)}, u32[]{:S(2)}) collective-permute-start(s32[12,12]{1,0:T(8,128)} %refs_3_), channel_id=1, source_target_pairs={{0,3},{1,2},{2,1},{3,0},{4,7},{5,6},{6,5},{7,4},{8,11},{9,10},{10,... | collective-permute-start | bytes 1736 | tf_op jit(solution)/shard_map/ppermute | solution.py:289
  22.8 5.8 %collective-permute-start.6 = (s32[12,12]{1,0:T(8,128)}, s32[12,12]{1,0:T(8,128)S(1)}, u32[]{:S(2)}, u32[]{:S(2)}) collective-permute-start(s32[12,12]{1,0:T(8,128)} %refs_3_), channel_id=1, source_target_pairs={{0,2},{1,3},{2,0},{3,1},{4,6},{5,7},{6,4},{7,5},{8,10},{9,11},{10,... | collective-permute-start | bytes 1736 | tf_op jit(solution)/shard_map/ppermute | solution.py:289
  25.5 3.9 %collective-permute-start.5 = (s32[12,12]{1,0:T(8,128)}, s32[12,12]{1,0:T(8,128)S(1)}, u32[]{:S(2)}, u32[]{:S(2)}) collective-permute-start(s32[12,12]{1,0:T(8,128)} %refs_3_), channel_id=1, source_target_pairs={{0,1},{1,0},{2,3},{3,2},{4,5},{5,4},{6,7},{7,6},{8,9},{9,8},{10,11... | collective-permute-start | bytes 1736 | tf_op jit(solution)/shard_map/ppermute | solution.py:289
  26.5 2.9 %copy-start.1 = (s32[12,12]{1,0:T(8,128)S(1)}, s32[12,12]{1,0:T(8,128)}, u32[]{:S(2)}) copy-start(s32[12,12]{1,0:T(8,128)} %refs_3_) | copy-start | bytes 1732
  26.6 2.8 %collective-permute-start.12 = (bf16[384,384]{1,0:T(8,128)(2,1)S(1)}, bf16[384,384]{1,0:T(8,128)(2,1)S(1)}, u32[]{:S(2)}, u32[]{:S(2)}) collective-permute-start(bf16[384,384]{1,0:T(8,128)(2,1)S(1)} %select_select_fusion.refs_1_), channel_id=1, source_target_pairs={{0,4},{1,5},{2,6},{3,7},{4,0},{5,1},{6,2},{7,3},{8,12},{9,13},{10,... | collective-permute-start | bytes 884744 | tf_op jit(solution)/shard_map/ppermute | solution.py:67
  26.7 1.0 %copy-start = (bf16[384,384]{1,0:T(8,128)(2,1)S(1)}, bf16[384,384]{1,0:T(8,128)(2,1)}, u32[]{:S(2)}) copy-start(bf16[384,384]{1,0:T(8,128)(2,1)} %refs_0_.1) | copy-start | bytes 884740
  29.4 2.0 %collective-permute-start.13 = (bf16[384,384]{1,0:T(8,128)(2,1)S(1)}, bf16[384,384]{1,0:T(8,128)(2,1)S(1)}, u32[]{:S(2)}, u32[]{:S(2)}) collective-permute-start(bf16[384,384]{1,0:T(8,128)(2,1)S(1)} %collective-permute-done.4.refs_0_), channel_id=1, source_target_pairs={{0,4},{1,5},{2,6},{3,7},{4,0},{5,1},{6,2},{7,3},{8,12},{9,13},{10,... | collective-permute-start | bytes 884744 | tf_op jit(solution)/shard_map/ppermute | solution.py:67

commit v9 on v7

--- a/solution.py
+++ b/solution.py
@@ -140,9 +140,8 @@
     for t in range(count):
         cols = pl.ds(pl.multiple_of(first + 256 * t, 128), 256)
         s = jnp.dot(panel, full[:, cols], preferred_element_type=F32)
-        s = masked(s, rows[:, cols])
         square[:, cols] = s
-        low[:, cols] = s.astype(BF16)
+        low[:, cols] = masked(s, rows[:, cols]).astype(BF16)
 
 
 def masked(x, rows):
@@ -193,8 +192,7 @@
 
     mine = block_at(edge, j)
     cube = jnp.dot(low[...], full[:, mine], preferred_element_type=F32)
-    cube = masked(cube, rows[:, mine])
-    out[...] = (3.0 * square[:, mine] - 2.0 * cube).astype(BF16)
+    out[...] = masked(3.0 * square[:, mine] - 2.0 * cube, rows[:, mine]).astype(BF16)
 
 
 VMEM = pl.BlockSpec(memory_space=pltpu.VMEM)

time: 34.3 us -> 34.3 us (level)
  no operation moved by 1% of the time
where the time goes in v9:
time: 34.3 us; the launch traced here: 34 us
  starting transfers between devices  21.9 us (64%)
  Pallas kernels  5.56 us (16%)
  waiting for transfers between devices  4.39 us (13%)
  other arithmetic  1.05 us (3%)
  local copies, waits for them, and re-layouts  0.96 us (3%)
    ppermute x11, starting transfers between devices, send(): return lax.ppermute(array, AXES, moves)  17.5 us
    ppermute x3, starting transfers between devices, block_body(): lax.ppermute(pattern, 'narrow', [(c, c ^ k) for c in range(4)])  4.39 us
    ppermute x11, waiting for transfers between devices, send(): return lax.ppermute(array, AXES, moves)  3.7 us
    pallas_call x1, Pallas kernels, purify(): pl.pallas_call(purify_kernel, out_shape=(jax.ShapeDtypeStruct((edge, edge...  2.67 us
    pallas_call x1, Pallas kernels, middle(): pl.pallas_call(middle_kernel, out_shape=(pltpu.VMEM((order, order), BF16)...  1.93 us
    select_n x1, other arithmetic, block_body(): near = send(jnp.where(kind == 0, own, across), NEAR_DIAGONAL)  1 us
    pallas_call x1, Pallas kernels, early(): pl.pallas_call(early_kernel, out_shape=pltpu.VMEM((order, order), BF16),...  0.96 us
    unnamed x4, local copies, waits for them, and re-layouts  0.96 us
  transfers between devices with their start and end apart: 14, of which 3 were waited for; matrix products, arithmetic and copies ran while one was open for 3% of the time, Pallas kernels for 9%

profile of v9, /device:TPU:0, one launch (start us, length us, event | category | flops | bytes accessed | tf_op | source)
XLA Modules:
  0.0 34.0 jit_solution(17634081868273263267)
XLA Ops:
  0.0 3.0 %collective-permute-start.1 = (bf16[384,384]{1,0:T(8,128)(2,1)}, bf16[384,384]{1,0:T(8,128)(2,1)S(1)}, u32[]{:S(2)}, u32[]{:S(2)}) collective-permute-start(bf16[384,384]{1,0:T(8,128)(2,1)} %refs_0_.1), channel_id=1, source_target_pairs={{0,8},{1,9},{2,10},{3,11},{4,12},{5,13},{6,14},{7,15},{8,0},{9,1},... | collective-permute-start | bytes 884744 | tf_op jit(solution)/shard_map/ppermute | solution.py:67
  3.0 3.6 %collective-permute-start.3 = (bf16[384,384]{1,0:T(8,128)(2,1)}, bf16[384,384]{1,0:T(8,128)(2,1)S(1)}, u32[]{:S(2)}, u32[]{:S(2)}) collective-permute-start(bf16[384,384]{1,0:T(8,128)(2,1)} %refs_0_.1), channel_id=1, source_target_pairs={{8,15},{9,11},{12,10},{13,14},{10,9},{14,13},{11,8},{15,12},{7,0},... | collective-permute-start | bytes 884744 | tf_op jit(solution)/shard_map/ppermute | solution.py:67
  6.6 0.0 collective-permute-start
  6.6 3.6 %collective-permute-done.1.refs_2_ = bf16[384,384]{1,0:T(8,128)(2,1)S(1)} collective-permute-done((bf16[384,384]{1,0:T(8,128)(2,1)}, bf16[384,384]{1,0:T(8,128)(2,1)S(1)}, u32[]{:S(2)}, u32[]{:S(2)}) %collective-permute-start.1) | collective-permute-done | bytes 294944 | tf_op jit(solution)/shard_map/ppermute | solution.py:67
  10.2 0.0 collective-permute-start.2
  10.2 1.0 %broadcast_select_fusion = bf16[384,384]{1,0:T(8,128)(2,1)S(1)} fusion(bf16[384,384]{1,0:T(8,128)(2,1)} %refs_0_.1, bf16[384,384]{1,0:T(8,128)(2,1)S(1)} %collective-permute-done.1.refs_2_, pred[]{:T(512)S(6)} %eq.11), kind=kLoop, calls=%fused_computation.1 | loop fusion | flops 147456 | bytes 884737 | tf_op jit(solution)/shard_map/jit(_where)/select_n | solution.py:268
  11.2 3.8 %collective-permute-start.11 = (bf16[384,384]{1,0:T(8,128)(2,1)S(1)}, bf16[384,384]{1,0:T(8,128)(2,1)S(1)}, u32[]{:S(2)}, u32[]{:S(2)}) collective-permute-start(bf16[384,384]{1,0:T(8,128)(2,1)S(1)} %broadcast_select_fusion), channel_id=1, source_target_pairs={{0,5},{2,7},{5,0},{7,2},{8,13},{10,15},{13,8},{15,10},{16,21},{18,... | collective-permute-start | bytes 884744 | tf_op jit(solution)/shard_map/ppermute | solution.py:67
  15.0 0.7 %collective-permute-start.10 = (bf16[384,384]{1,0:T(8,128)(2,1)S(1)}, bf16[384,384]{1,0:T(8,128)(2,1)S(1)}, u32[]{:S(2)}, u32[]{:S(2)}) collective-permute-start(bf16[384,384]{1,0:T(8,128)(2,1)S(1)} %collective-permute-done.1.refs_2_), channel_id=1, source_target_pairs={{2,4},{7,1},{8,14},{13,11},{18,20},{23,17},{24,30},{29,27}} | collective-permute-start | bytes 884744 | tf_op jit(solution)/shard_map/ppermute | solution.py:67
  15.7 0.0 collective-permute-done.3.refs_4_
  15.7 0.0 collective-permute-done.refs_1_
  15.7 0.0 collective-permute-done.2.refs_3_
  15.7 0.7 %collective-permute-start.9 = (bf16[384,384]{1,0:T(8,128)(2,1)S(1)}, bf16[384,384]{1,0:T(8,128)(2,1)S(1)}, u32[]{:S(2)}, u32[]{:S(2)}) collective-permute-start(bf16[384,384]{1,0:T(8,128)(2,1)S(1)} %collective-permute-done.3.refs_4_), channel_id=1, source_target_pairs={{3,6},{6,3},{9,12},{12,9},{19,22},{22,19},{25,28},{28,25}} | collective-permute-start | bytes 884744 | tf_op jit(solution)/shard_map/ppermute | solution.py:67
  16.4 1.4 %collective-permute-start.8 = (bf16[384,384]{1,0:T(8,128)(2,1)S(1)}, bf16[384,384]{1,0:T(8,128)(2,1)S(1)}, u32[]{:S(2)}, u32[]{:S(2)}) collective-permute-start(bf16[384,384]{1,0:T(8,128)(2,1)S(1)} %collective-permute-done.3.refs_4_), channel_id=1, source_target_pairs={{0,4},{1,5},{2,6},{3,7},{4,0},{5,1},{6,2},{7,3},{8,12},{9,13},{10,... | collective-permute-start | bytes 884744 | tf_op jit(solution)/shard_map/ppermute | solution.py:67
  17.9 4.3 %collective-permute-start.4 = (bf16[384,384]{1,0:T(8,128)(2,1)S(1)}, bf16[384,384]{1,0:T(8,128)(2,1)S(1)}, u32[]{:S(2)}, u32[]{:S(2)}) collective-permute-start(bf16[384,384]{1,0:T(8,128)(2,1)S(1)} %collective-permute-done.3.refs_4_), channel_id=1, source_target_pairs={{0,8},{1,9},{2,10},{3,11},{4,12},{5,13},{6,14},{7,15},{8,0},{9,1},... | collective-permute-start | bytes 884744 | tf_op jit(solution)/shard_map/ppermute | solution.py:67
  22.1 0.0 collective-permute-done.11
  22.1 0.6 %collective-permute-start.7 = (s32[12,12]{1,0:T(8,128)}, s32[12,12]{1,0:T(8,128)S(1)}, u32[]{:S(2)}, u32[]{:S(2)}) collective-permute-start(s32[12,12]{1,0:T(8,128)} %refs_3_), channel_id=1, source_target_pairs={{0,3},{1,2},{2,1},{3,0},{4,7},{5,6},{6,5},{7,4},{8,11},{9,10},{10,... | collective-permute-start | bytes 1736 | tf_op jit(solution)/shard_map/ppermute | solution.py:275
  22.8 0.0 collective-permute-done.10
  22.8 2.7 %collective-permute-start.6 = (s32[12,12]{1,0:T(8,128)}, s32[12,12]{1,0:T(8,128)S(1)}, u32[]{:S(2)}, u32[]{:S(2)}) collective-permute-start(s32[12,12]{1,0:T(8,128)} %refs_3_), channel_id=1, source_target_pairs={{0,2},{1,3},{2,0},{3,1},{4,6},{5,7},{6,4},{7,5},{8,10},{9,11},{10,... | collective-permute-start | bytes 1736 | tf_op jit(solution)/shard_map/ppermute | solution.py:275
  25.5 0.0 collective-permute-done.9
  25.5 1.1 %collective-permute-start.5 = (s32[12,12]{1,0:T(8,128)}, s32[12,12]{1,0:T(8,128)S(1)}, u32[]{:S(2)}, u32[]{:S(2)}) collective-permute-start(s32[12,12]{1,0:T(8,128)} %refs_3_), channel_id=1, source_target_pairs={{0,1},{1,0},{2,3},{3,2},{4,5},{5,4},{6,7},{7,6},{8,9},{9,8},{10,11... | collective-permute-start | bytes 1736 | tf_op jit(solution)/shard_map/ppermute | solution.py:275
  26.6 0.0 collective-permute-done.8.refs_5_
  26.6 0.1 collective-permute-start.12
  26.7 0.0 copy-start
  26.7 1.0 %copy-done = bf16[384,384]{1,0:T(8,128)(2,1)S(1)} copy-done((bf16[384,384]{1,0:T(8,128)(2,1)S(1)}, bf16[384,384]{1,0:T(8,128)(2,1)}, u32[]{:S(2)}) %copy-start) | copy-done | bytes 294936
  27.7 1.0 %early.1.full_in = bf16[1536,1536]{1,0:T(8,128)(2,1)S(1)} custom-call(bf16[384,384]{1,0:T(8,128)(2,1)S(1)} %copy-done, bf16[384,384]{1,0:T(8,128)(2,1)S(1)} %collective-permute-done.refs_1_, bf16[384,384]{1,0:T(8,128)(2,1)S(1)} %collective-permute-done.1.refs_2_, bf16[384,384]{1,0:T(8,128)(2,1)S(1)} %collective-permute-done.2.refs_3_, ...), custom_call_target="tpu_custom_call" | custom-call | tf_op jit(solution)/shard_map/early/pallas_call | solution.py:209
  28.6 0.0 collective-permute-done.7.refs_6_
  28.6 0.0 collective-permute-done.6.refs_5_
  28.6 0.7 %collective-permute-done.5.refs_4_ = s32[12,12]{1,0:T(8,128)S(1)} collective-permute-done((s32[12,12]{1,0:T(8,128)}, s32[12,12]{1,0:T(8,128)S(1)}, u32[]{:S(2)}, u32[]{:S(2)}) %collective-permute-start.5) | collective-permute-done | bytes 608 | tf_op jit(solution)/shard_map/ppermute | solution.py:275
  29.3 0.1 collective-permute-done.4.refs_0_
  29.4 0.0 collective-permute-start.13
  29.4 1.9 %middle.1 = (bf16[1536,1536]{1,0:T(8,128)(2,1)S(1)}, f32[12,1536]{1,0:T(8,128)S(1)}, f32[384,1536]{1,0:T(8,128)S(1)}, bf16[384,1536]{1,0:T(8,128)(2,1)S(1)}) custom-call(bf16[1536,1536]{1,0:T(8,128)(2,1)S(1)} %early.1.full_in, bf16[384,384]{1,0:T(8,128)(2,1)S(1)} %collective-permute-done.4.refs_0_, ...), custom_call_target="tpu_custom_call", output_to_operand_aliasing={{0}: (0, {})} | custom-call | tf_op jit(solution)/shard_map/middle/pallas_call | solution.py:224
  31.4 2.7 %purify.1 = (bf16[384,384]{1,0:T(8,128)(2,1)}, bf16[1536,1536]{1,0:T(8,128)(2,1)S(1)}, f32[384,1536]{1,0:T(8,128)S(1)}, bf16[384,1536]{1,0:T(8,128)(2,1)S(1)}) custom-call(bf16[1536,1536]{1,0:T(8,128)(2,1)S(1)} %get-tuple-element.34.full_in, f32[12,1536]{1,0:T(8,128)S(1)} %get-tuple-element.35.rows, ...), custom_call_target="tpu_custom_call", output_to_operand_aliasing={{1}: (0, {}), {2}: (2, {}), {3}: (3, {})} | custom-call | tf_op jit(solution)/shard_map/purify/pallas_call | solution.py:246
  (5 shorter events, 0.1 us)
Async XLA Ops:
  0.0 10.2 %collective-permute-start.1 = (bf16[384,384]{1,0:T(8,128)(2,1)}, bf16[384,384]{1,0:T(8,128)(2,1)S(1)}, u32[]{:S(2)}, u32[]{:S(2)}) collective-permute-start(bf16[384,384]{1,0:T(8,128)(2,1)} %refs_0_.1), channel_id=1, source_target_pairs={{0,8},{1,9},{2,10},{3,11},{4,12},{5,13},{6,14},{7,15},{8,0},{9,1},... | collective-permute-start | bytes 884744 | tf_op jit(solution)/shard_map/ppermute | solution.py:67
  3.0 12.7 %collective-permute-start.3 = (bf16[384,384]{1,0:T(8,128)(2,1)}, bf16[384,384]{1,0:T(8,128)(2,1)S(1)}, u32[]{:S(2)}, u32[]{:S(2)}) collective-permute-start(bf16[384,384]{1,0:T(8,128)(2,1)} %refs_0_.1), channel_id=1, source_target_pairs={{8,15},{9,11},{12,10},{13,14},{10,9},{14,13},{11,8},{15,12},{7,0},... | collective-permute-start | bytes 884744 | tf_op jit(solution)/shard_map/ppermute | solution.py:67
  6.6 9.1 %collective-permute-start = (bf16[384,384]{1,0:T(8,128)(2,1)}, bf16[384,384]{1,0:T(8,128)(2,1)S(1)}, u32[]{:S(2)}, u32[]{:S(2)}) collective-permute-start(bf16[384,384]{1,0:T(8,128)(2,1)} %refs_0_.1), channel_id=1, source_target_pairs={{0,4},{1,5},{2,6},{3,7},{4,0},{5,1},{6,2},{7,3},{8,12},{9,13},{10,... | collective-permute-start | bytes 884744 | tf_op jit(solution)/shard_map/ppermute | solution.py:67
  10.2 5.5 %collective-permute-start.2 = (bf16[384,384]{1,0:T(8,128)(2,1)S(1)}, bf16[384,384]{1,0:T(8,128)(2,1)S(1)}, u32[]{:S(2)}, u32[]{:S(2)}) collective-permute-start(bf16[384,384]{1,0:T(8,128)(2,1)S(1)} %collective-permute-done.1.refs_2_), channel_id=1, source_target_pairs={{0,4},{1,5},{2,6},{3,7},{4,0},{5,1},{6,2},{7,3},{8,12},{9,13},{10,... | collective-permute-start | bytes 884744 | tf_op jit(solution)/shard_map/ppermute | solution.py:67
  11.2 11.0 %collective-permute-start.11 = (bf16[384,384]{1,0:T(8,128)(2,1)S(1)}, bf16[384,384]{1,0:T(8,128)(2,1)S(1)}, u32[]{:S(2)}, u32[]{:S(2)}) collective-permute-start(bf16[384,384]{1,0:T(8,128)(2,1)S(1)} %broadcast_select_fusion), channel_id=1, source_target_pairs={{0,5},{2,7},{5,0},{7,2},{8,13},{10,15},{13,8},{15,10},{16,21},{18,... | collective-permute-start | bytes 884744 | tf_op jit(solution)/shard_map/ppermute | solution.py:67
  15.0 7.8 %collective-permute-start.10 = (bf16[384,384]{1,0:T(8,128)(2,1)S(1)}, bf16[384,384]{1,0:T(8,128)(2,1)S(1)}, u32[]{:S(2)}, u32[]{:S(2)}) collective-permute-start(bf16[384,384]{1,0:T(8,128)(2,1)S(1)} %collective-permute-done.1.refs_2_), channel_id=1, source_target_pairs={{2,4},{7,1},{8,14},{13,11},{18,20},{23,17},{24,30},{29,27}} | collective-permute-start | bytes 884744 | tf_op jit(solution)/shard_map/ppermute | solution.py:67
  15.7 9.7 %collective-permute-start.9 = (bf16[384,384]{1,0:T(8,128)(2,1)S(1)}, bf16[384,384]{1,0:T(8,128)(2,1)S(1)}, u32[]{:S(2)}, u32[]{:S(2)}) collective-permute-start(bf16[384,384]{1,0:T(8,128)(2,1)S(1)} %collective-permute-done.3.refs_4_), channel_id=1, source_target_pairs={{3,6},{6,3},{9,12},{12,9},{19,22},{22,19},{25,28},{28,25}} | collective-permute-start | bytes 884744 | tf_op jit(solution)/shard_map/ppermute | solution.py:67
  16.4 10.2 %collective-permute-start.8 = (bf16[384,384]{1,0:T(8,128)(2,1)S(1)}, bf16[384,384]{1,0:T(8,128)(2,1)S(1)}, u32[]{:S(2)}, u32[]{:S(2)}) collective-permute-start(bf16[384,384]{1,0:T(8,128)(2,1)S(1)} %collective-permute-done.3.refs_4_), channel_id=1, source_target_pairs={{0,4},{1,5},{2,6},{3,7},{4,0},{5,1},{6,2},{7,3},{8,12},{9,13},{10,... | collective-permute-start | bytes 884744 | tf_op jit(solution)/shard_map/ppermute | solution.py:67
  17.9 11.5 %collective-permute-start.4 = (bf16[384,384]{1,0:T(8,128)(2,1)S(1)}, bf16[384,384]{1,0:T(8,128)(2,1)S(1)}, u32[]{:S(2)}, u32[]{:S(2)}) collective-permute-start(bf16[384,384]{1,0:T(8,128)(2,1)S(1)} %collective-permute-done.3.refs_4_), channel_id=1, source_target_pairs={{0,8},{1,9},{2,10},{3,11},{4,12},{5,13},{6,14},{7,15},{8,0},{9,1},... | collective-permute-start | bytes 884744 | tf_op jit(solution)/shard_map/ppermute | solution.py:67
  22.1 6.5 %collective-permute-start.7 = (s32[12,12]{1,0:T(8,128)}, s32[12,12]{1,0:T(8,128)S(1)}, u32[]{:S(2)}, u32[]{:S(2)}) collective-permute-start(s32[12,12]{1,0:T(8,128)} %refs_3_), channel_id=1, source_target_pairs={{0,3},{1,2},{2,1},{3,0},{4,7},{5,6},{6,5},{7,4},{8,11},{9,10},{10,... | collective-permute-start | bytes 1736 | tf_op jit(solution)/shard_map/ppermute | solution.py:275
  22.8 5.8 %collective-permute-start.6 = (s32[12,12]{1,0:T(8,128)}, s32[12,12]{1,0:T(8,128)S(1)}, u32[]{:S(2)}, u32[]{:S(2)}) collective-permute-start(s32[12,12]{1,0:T(8,128)} %refs_3_), channel_id=1, source_target_pairs={{0,2},{1,3},{2,0},{3,1},{4,6},{5,7},{6,4},{7,5},{8,10},{9,11},{10,... | collective-permute-start | bytes 1736 | tf_op jit(solution)/shard_map/ppermute | solution.py:275
  25.5 3.9 %collective-permute-start.5 = (s32[12,12]{1,0:T(8,128)}, s32[12,12]{1,0:T(8,128)S(1)}, u32[]{:S(2)}, u32[]{:S(2)}) collective-permute-start(s32[12,12]{1,0:T(8,128)} %refs_3_), channel_id=1, source_target_pairs={{0,1},{1,0},{2,3},{3,2},{4,5},{5,4},{6,7},{7,6},{8,9},{9,8},{10,11... | collective-permute-start | bytes 1736 | tf_op jit(solution)/shard_map/ppermute | solution.py:275
  26.5 2.9 %copy-start.1 = (s32[12,12]{1,0:T(8,128)S(1)}, s32[12,12]{1,0:T(8,128)}, u32[]{:S(2)}) copy-start(s32[12,12]{1,0:T(8,128)} %refs_3_) | copy-start | bytes 1732
  26.6 2.8 %collective-permute-start.12 = (bf16[384,384]{1,0:T(8,128)(2,1)S(1)}, bf16[384,384]{1,0:T(8,128)(2,1)S(1)}, u32[]{:S(2)}, u32[]{:S(2)}) collective-permute-start(bf16[384,384]{1,0:T(8,128)(2,1)S(1)} %select_select_fusion.refs_1_), channel_id=1, source_target_pairs={{0,4},{1,5},{2,6},{3,7},{4,0},{5,1},{6,2},{7,3},{8,12},{9,13},{10,... | collective-permute-start | bytes 884744 | tf_op jit(solution)/shard_map/ppermute | solution.py:67
  26.7 1.0 %copy-start = (bf16[384,384]{1,0:T(8,128)(2,1)S(1)}, bf16[384,384]{1,0:T(8,128)(2,1)}, u32[]{:S(2)}) copy-start(bf16[384,384]{1,0:T(8,128)(2,1)} %refs_0_.1) | copy-start | bytes 884740
  29.4 2.0 %collective-permute-start.13 = (bf16[384,384]{1,0:T(8,128)(2,1)S(1)}, bf16[384,384]{1,0:T(8,128)(2,1)S(1)}, u32[]{:S(2)}, u32[]{:S(2)}) collective-permute-start(bf16[384,384]{1,0:T(8,128)(2,1)S(1)} %collective-permute-done.4.refs_0_), channel_id=1, source_target_pairs={{0,4},{1,5},{2,6},{3,7},{4,0},{5,1},{6,2},{7,3},{8,12},{9,13},{10,... | collective-permute-start | bytes 884744 | tf_op jit(solution)/shard_map/ppermute | solution.py:67

commit v10 on v8

--- a/solution.py
+++ b/solution.py
@@ -140,9 +140,8 @@
     for t in range(count):
         cols = pl.ds(pl.multiple_of(first + 256 * t, 128), 256)
         s = jnp.dot(panel, full[:, cols], preferred_element_type=F32)
-        s = masked(s, rows[:, cols])
         square[:, cols] = s
-        low[:, cols] = s.astype(BF16)
+        low[:, cols] = masked(s, rows[:, cols]).astype(BF16)
 
 
 def masked(x, rows):
@@ -197,8 +196,9 @@
     for part in range(2):
         some = slice(part * edge // 2, (part + 1) * edge // 2)
         cube = jnp.dot(low[some], full[:, mine], preferred_element_type=F32)
-        cube = masked(cube, rows[part * n // 2 : (part + 1) * n // 2, mine])
-        result[some] = (3.0 * square[some, mine] - 2.0 * cube).astype(BF16)
+        both = 3.0 * square[some, mine] - 2.0 * cube
+        both = masked(both, rows[part * n // 2 : (part + 1) * n // 2, mine])
+        result[some] = both.astype(BF16)
         writes.append(pltpu.make_async_copy(result.at[some], out.at[some], done.at[part]))
         writes[-1].start()
     for write in writes:

time: 34.2 us -> 34.2 us (level)
  no operation moved by 1% of the time
where the time goes in v10:
time: 34.2 us; the launch traced here: 34 us
  starting transfers between devices  21.9 us (64%)
  Pallas kernels  5.53 us (16%)
  waiting for transfers between devices  4.39 us (13%)
  other arithmetic  1.05 us (3%)
  local copies, waits for them, and re-layouts  0.96 us (3%)
    ppermute x11, starting transfers between devices, send(): return lax.ppermute(array, AXES, moves)  17.5 us
    ppermute x3, starting transfers between devices, block_body(): lax.ppermute(pattern, 'narrow', [(c, c ^ k) for c in range(4)])  4.39 us
    ppermute x11, waiting for transfers between devices, send(): return lax.ppermute(array, AXES, moves)  3.7 us
    pallas_call x1, Pallas kernels, purify(): pl.pallas_call(purify_kernel, out_shape=(jax.ShapeDtypeStruct((edge, edge...  2.64 us
    pallas_call x1, Pallas kernels, middle(): pl.pallas_call(middle_kernel, out_shape=(pltpu.VMEM((order, order), BF16)...  1.93 us
    select_n x1, other arithmetic, block_body(): near = send(jnp.where(kind == 0, own, across), NEAR_DIAGONAL)  1 us
    pallas_call x1, Pallas kernels, early(): pl.pallas_call(early_kernel, out_shape=pltpu.VMEM((order, order), BF16),...  0.96 us
    unnamed x4, local copies, waits for them, and re-layouts  0.96 us
  transfers between devices with their start and end apart: 14, of which 3 were waited for; matrix products, arithmetic and copies ran while one was open for 3% of the time, Pallas kernels for 9%

profile of v10, /device:TPU:0, one launch (start us, length us, event | category | flops | bytes accessed | tf_op | source)
XLA Modules:
  0.0 34.0 jit_solution(12519046568303929573)
XLA Ops:
  0.0 3.0 %collective-permute-start.1 = (bf16[384,384]{1,0:T(8,128)(2,1)}, bf16[384,384]{1,0:T(8,128)(2,1)S(1)}, u32[]{:S(2)}, u32[]{:S(2)}) collective-permute-start(bf16[384,384]{1,0:T(8,128)(2,1)} %refs_0_.1), channel_id=1, source_target_pairs={{0,8},{1,9},{2,10},{3,11},{4,12},{5,13},{6,14},{7,15},{8,0},{9,1},... | collective-permute-start | bytes 884744 | tf_op jit(solution)/shard_map/ppermute | solution.py:67
  3.0 3.6 %collective-permute-start.3 = (bf16[384,384]{1,0:T(8,128)(2,1)}, bf16[384,384]{1,0:T(8,128)(2,1)S(1)}, u32[]{:S(2)}, u32[]{:S(2)}) collective-permute-start(bf16[384,384]{1,0:T(8,128)(2,1)} %refs_0_.1), channel_id=1, source_target_pairs={{8,15},{9,11},{12,10},{13,14},{10,9},{14,13},{11,8},{15,12},{7,0},... | collective-permute-start | bytes 884744 | tf_op jit(solution)/shard_map/ppermute | solution.py:67
  6.6 0.0 collective-permute-start
  6.6 3.6 %collective-permute-done.1.refs_2_ = bf16[384,384]{1,0:T(8,128)(2,1)S(1)} collective-permute-done((bf16[384,384]{1,0:T(8,128)(2,1)}, bf16[384,384]{1,0:T(8,128)(2,1)S(1)}, u32[]{:S(2)}, u32[]{:S(2)}) %collective-permute-start.1) | collective-permute-done | bytes 294944 | tf_op jit(solution)/shard_map/ppermute | solution.py:67
  10.2 0.0 collective-permute-start.2
  10.2 1.0 %broadcast_select_fusion = bf16[384,384]{1,0:T(8,128)(2,1)S(1)} fusion(bf16[384,384]{1,0:T(8,128)(2,1)} %refs_0_.1, bf16[384,384]{1,0:T(8,128)(2,1)S(1)} %collective-permute-done.1.refs_2_, pred[]{:T(512)S(6)} %eq.11), kind=kLoop, calls=%fused_computation.1 | loop fusion | flops 147456 | bytes 884737 | tf_op jit(solution)/shard_map/jit(_where)/select_n | solution.py:282
  11.2 3.8 %collective-permute-start.11 = (bf16[384,384]{1,0:T(8,128)(2,1)S(1)}, bf16[384,384]{1,0:T(8,128)(2,1)S(1)}, u32[]{:S(2)}, u32[]{:S(2)}) collective-permute-start(bf16[384,384]{1,0:T(8,128)(2,1)S(1)} %broadcast_select_fusion), channel_id=1, source_target_pairs={{0,5},{2,7},{5,0},{7,2},{8,13},{10,15},{13,8},{15,10},{16,21},{18,... | collective-permute-start | bytes 884744 | tf_op jit(solution)/shard_map/ppermute | solution.py:67
  15.0 0.7 %collective-permute-start.10 = (bf16[384,384]{1,0:T(8,128)(2,1)S(1)}, bf16[384,384]{1,0:T(8,128)(2,1)S(1)}, u32[]{:S(2)}, u32[]{:S(2)}) collective-permute-start(bf16[384,384]{1,0:T(8,128)(2,1)S(1)} %collective-permute-done.1.refs_2_), channel_id=1, source_target_pairs={{2,4},{7,1},{8,14},{13,11},{18,20},{23,17},{24,30},{29,27}} | collective-permute-start | bytes 884744 | tf_op jit(solution)/shard_map/ppermute | solution.py:67
  15.7 0.0 collective-permute-done.3.refs_4_
  15.7 0.0 collective-permute-done.refs_1_
  15.7 0.0 collective-permute-done.2.refs_3_
  15.7 0.7 %collective-permute-start.9 = (bf16[384,384]{1,0:T(8,128)(2,1)S(1)}, bf16[384,384]{1,0:T(8,128)(2,1)S(1)}, u32[]{:S(2)}, u32[]{:S(2)}) collective-permute-start(bf16[384,384]{1,0:T(8,128)(2,1)S(1)} %collective-permute-done.3.refs_4_), channel_id=1, source_target_pairs={{3,6},{6,3},{9,12},{12,9},{19,22},{22,19},{25,28},{28,25}} | collective-permute-start | bytes 884744 | tf_op jit(solution)/shard_map/ppermute | solution.py:67
  16.4 1.4 %collective-permute-start.8 = (bf16[384,384]{1,0:T(8,128)(2,1)S(1)}, bf16[384,384]{1,0:T(8,128)(2,1)S(1)}, u32[]{:S(2)}, u32[]{:S(2)}) collective-permute-start(bf16[384,384]{1,0:T(8,128)(2,1)S(1)} %collective-permute-done.3.refs_4_), channel_id=1, source_target_pairs={{0,4},{1,5},{2,6},{3,7},{4,0},{5,1},{6,2},{7,3},{8,12},{9,13},{10,... | collective-permute-start | bytes 884744 | tf_op jit(solution)/shard_map/ppermute | solution.py:67
  17.9 4.3 %collective-permute-start.4 = (bf16[384,384]{1,0:T(8,128)(2,1)S(1)}, bf16[384,384]{1,0:T(8,128)(2,1)S(1)}, u32[]{:S(2)}, u32[]{:S(2)}) collective-permute-start(bf16[384,384]{1,0:T(8,128)(2,1)S(1)} %collective-permute-done.3.refs_4_), channel_id=1, source_target_pairs={{0,8},{1,9},{2,10},{3,11},{4,12},{5,13},{6,14},{7,15},{8,0},{9,1},... | collective-permute-start | bytes 884744 | tf_op jit(solution)/shard_map/ppermute | solution.py:67
  22.1 0.0 collective-permute-done.11
  22.1 0.6 %collective-permute-start.7 = (s32[12,12]{1,0:T(8,128)}, s32[12,12]{1,0:T(8,128)S(1)}, u32[]{:S(2)}, u32[]{:S(2)}) collective-permute-start(s32[12,12]{1,0:T(8,128)} %refs_3_), channel_id=1, source_target_pairs={{0,3},{1,2},{2,1},{3,0},{4,7},{5,6},{6,5},{7,4},{8,11},{9,10},{10,... | collective-permute-start | bytes 1736 | tf_op jit(solution)/shard_map/ppermute | solution.py:289
  22.8 0.0 collective-permute-done.10
  22.8 2.7 %collective-permute-start.6 = (s32[12,12]{1,0:T(8,128)}, s32[12,12]{1,0:T(8,128)S(1)}, u32[]{:S(2)}, u32[]{:S(2)}) collective-permute-start(s32[12,12]{1,0:T(8,128)} %refs_3_), channel_id=1, source_target_pairs={{0,2},{1,3},{2,0},{3,1},{4,6},{5,7},{6,4},{7,5},{8,10},{9,11},{10,... | collective-permute-start | bytes 1736 | tf_op jit(solution)/shard_map/ppermute | solution.py:289
  25.5 0.0 collective-permute-done.9
  25.5 1.1 %collective-permute-start.5 = (s32[12,12]{1,0:T(8,128)}, s32[12,12]{1,0:T(8,128)S(1)}, u32[]{:S(2)}, u32[]{:S(2)}) collective-permute-start(s32[12,12]{1,0:T(8,128)} %refs_3_), channel_id=1, source_target_pairs={{0,1},{1,0},{2,3},{3,2},{4,5},{5,4},{6,7},{7,6},{8,9},{9,8},{10,11... | collective-permute-start | bytes 1736 | tf_op jit(solution)/shard_map/ppermute | solution.py:289
  26.6 0.0 collective-permute-done.8.refs_5_
  26.6 0.1 collective-permute-start.12
  26.7 0.0 copy-start
  26.7 1.0 %copy-done = bf16[384,384]{1,0:T(8,128)(2,1)S(1)} copy-done((bf16[384,384]{1,0:T(8,128)(2,1)S(1)}, bf16[384,384]{1,0:T(8,128)(2,1)}, u32[]{:S(2)}) %copy-start) | copy-done | bytes 294936
  27.7 1.0 %early.1.full_in = bf16[1536,1536]{1,0:T(8,128)(2,1)S(1)} custom-call(bf16[384,384]{1,0:T(8,128)(2,1)S(1)} %copy-done, bf16[384,384]{1,0:T(8,128)(2,1)S(1)} %collective-permute-done.refs_1_, bf16[384,384]{1,0:T(8,128)(2,1)S(1)} %collective-permute-done.1.refs_2_, bf16[384,384]{1,0:T(8,128)(2,1)S(1)} %collective-permute-done.2.refs_3_, ...), custom_call_target="tpu_custom_call" | custom-call | tf_op jit(solution)/shard_map/early/pallas_call | solution.py:219
  28.6 0.0 collective-permute-done.7.refs_6_
  28.6 0.0 collective-permute-done.6.refs_5_
  28.6 0.7 %collective-permute-done.5.refs_4_ = s32[12,12]{1,0:T(8,128)S(1)} collective-permute-done((s32[12,12]{1,0:T(8,128)}, s32[12,12]{1,0:T(8,128)S(1)}, u32[]{:S(2)}, u32[]{:S(2)}) %collective-permute-start.5) | collective-permute-done | bytes 608 | tf_op jit(solution)/shard_map/ppermute | solution.py:289
  29.3 0.1 collective-permute-done.4.refs_0_
  29.4 1.9 %middle.1 = (bf16[1536,1536]{1,0:T(8,128)(2,1)S(1)}, f32[12,1536]{1,0:T(8,128)S(1)}, f32[384,1536]{1,0:T(8,128)S(1)}, bf16[384,1536]{1,0:T(8,128)(2,1)S(1)}) custom-call(bf16[1536,1536]{1,0:T(8,128)(2,1)S(1)} %early.1.full_in, bf16[384,384]{1,0:T(8,128)(2,1)S(1)} %collective-permute-done.4.refs_0_, ...), custom_call_target="tpu_custom_call", output_to_operand_aliasing={{0}: (0, {})} | custom-call | tf_op jit(solution)/shard_map/middle/pallas_call | solution.py:234
  31.3 0.0 collective-permute-done.13.refs_0_
  31.4 2.6 %purify.1 = (bf16[384,384]{1,0:T(8,128)(2,1)}, bf16[1536,1536]{1,0:T(8,128)(2,1)S(1)}, f32[384,1536]{1,0:T(8,128)S(1)}, bf16[384,1536]{1,0:T(8,128)(2,1)S(1)}) custom-call(bf16[1536,1536]{1,0:T(8,128)(2,1)S(1)} %get-tuple-element.34.full_in, f32[12,1536]{1,0:T(8,128)S(1)} %get-tuple-element.35.rows, ...), custom_call_target="tpu_custom_call", output_to_operand_aliasing={{1}: (0, {}), {2}: (2, {}), {3}: (3, {})} | custom-call | tf_op jit(solution)/shard_map/purify/pallas_call | solution.py:256
  (5 shorter events, 0.1 us)
Async XLA Ops:
  0.0 10.2 %collective-permute-start.1 = (bf16[384,384]{1,0:T(8,128)(2,1)}, bf16[384,384]{1,0:T(8,128)(2,1)S(1)}, u32[]{:S(2)}, u32[]{:S(2)}) collective-permute-start(bf16[384,384]{1,0:T(8,128)(2,1)} %refs_0_.1), channel_id=1, source_target_pairs={{0,8},{1,9},{2,10},{3,11},{4,12},{5,13},{6,14},{7,15},{8,0},{9,1},... | collective-permute-start | bytes 884744 | tf_op jit(solution)/shard_map/ppermute | solution.py:67
  3.0 12.7 %collective-permute-start.3 = (bf16[384,384]{1,0:T(8,128)(2,1)}, bf16[384,384]{1,0:T(8,128)(2,1)S(1)}, u32[]{:S(2)}, u32[]{:S(2)}) collective-permute-start(bf16[384,384]{1,0:T(8,128)(2,1)} %refs_0_.1), channel_id=1, source_target_pairs={{8,15},{9,11},{12,10},{13,14},{10,9},{14,13},{11,8},{15,12},{7,0},... | collective-permute-start | bytes 884744 | tf_op jit(solution)/shard_map/ppermute | solution.py:67
  6.6 9.1 %collective-permute-start = (bf16[384,384]{1,0:T(8,128)(2,1)}, bf16[384,384]{1,0:T(8,128)(2,1)S(1)}, u32[]{:S(2)}, u32[]{:S(2)}) collective-permute-start(bf16[384,384]{1,0:T(8,128)(2,1)} %refs_0_.1), channel_id=1, source_target_pairs={{0,4},{1,5},{2,6},{3,7},{4,0},{5,1},{6,2},{7,3},{8,12},{9,13},{10,... | collective-permute-start | bytes 884744 | tf_op jit(solution)/shard_map/ppermute | solution.py:67
  10.2 5.5 %collective-permute-start.2 = (bf16[384,384]{1,0:T(8,128)(2,1)S(1)}, bf16[384,384]{1,0:T(8,128)(2,1)S(1)}, u32[]{:S(2)}, u32[]{:S(2)}) collective-permute-start(bf16[384,384]{1,0:T(8,128)(2,1)S(1)} %collective-permute-done.1.refs_2_), channel_id=1, source_target_pairs={{0,4},{1,5},{2,6},{3,7},{4,0},{5,1},{6,2},{7,3},{8,12},{9,13},{10,... | collective-permute-start | bytes 884744 | tf_op jit(solution)/shard_map/ppermute | solution.py:67
  11.2 11.0 %collective-permute-start.11 = (bf16[384,384]{1,0:T(8,128)(2,1)S(1)}, bf16[384,384]{1,0:T(8,128)(2,1)S(1)}, u32[]{:S(2)}, u32[]{:S(2)}) collective-permute-start(bf16[384,384]{1,0:T(8,128)(2,1)S(1)} %broadcast_select_fusion), channel_id=1, source_target_pairs={{0,5},{2,7},{5,0},{7,2},{8,13},{10,15},{13,8},{15,10},{16,21},{18,... | collective-permute-start | bytes 884744 | tf_op jit(solution)/shard_map/ppermute | solution.py:67
  15.0 7.8 %collective-permute-start.10 = (bf16[384,384]{1,0:T(8,128)(2,1)S(1)}, bf16[384,384]{1,0:T(8,128)(2,1)S(1)}, u32[]{:S(2)}, u32[]{:S(2)}) collective-permute-start(bf16[384,384]{1,0:T(8,128)(2,1)S(1)} %collective-permute-done.1.refs_2_), channel_id=1, source_target_pairs={{2,4},{7,1},{8,14},{13,11},{18,20},{23,17},{24,30},{29,27}} | collective-permute-start | bytes 884744 | tf_op jit(solution)/shard_map/ppermute | solution.py:67
  15.7 9.7 %collective-permute-start.9 = (bf16[384,384]{1,0:T(8,128)(2,1)S(1)}, bf16[384,384]{1,0:T(8,128)(2,1)S(1)}, u32[]{:S(2)}, u32[]{:S(2)}) collective-permute-start(bf16[384,384]{1,0:T(8,128)(2,1)S(1)} %collective-permute-done.3.refs_4_), channel_id=1, source_target_pairs={{3,6},{6,3},{9,12},{12,9},{19,22},{22,19},{25,28},{28,25}} | collective-permute-start | bytes 884744 | tf_op jit(solution)/shard_map/ppermute | solution.py:67
  16.4 10.2 %collective-permute-start.8 = (bf16[384,384]{1,0:T(8,128)(2,1)S(1)}, bf16[384,384]{1,0:T(8,128)(2,1)S(1)}, u32[]{:S(2)}, u32[]{:S(2)}) collective-permute-start(bf16[384,384]{1,0:T(8,128)(2,1)S(1)} %collective-permute-done.3.refs_4_), channel_id=1, source_target_pairs={{0,4},{1,5},{2,6},{3,7},{4,0},{5,1},{6,2},{7,3},{8,12},{9,13},{10,... | collective-permute-start | bytes 884744 | tf_op jit(solution)/shard_map/ppermute | solution.py:67
  17.9 11.5 %collective-permute-start.4 = (bf16[384,384]{1,0:T(8,128)(2,1)S(1)}, bf16[384,384]{1,0:T(8,128)(2,1)S(1)}, u32[]{:S(2)}, u32[]{:S(2)}) collective-permute-start(bf16[384,384]{1,0:T(8,128)(2,1)S(1)} %collective-permute-done.3.refs_4_), channel_id=1, source_target_pairs={{0,8},{1,9},{2,10},{3,11},{4,12},{5,13},{6,14},{7,15},{8,0},{9,1},... | collective-permute-start | bytes 884744 | tf_op jit(solution)/shard_map/ppermute | solution.py:67
  22.1 6.5 %collective-permute-start.7 = (s32[12,12]{1,0:T(8,128)}, s32[12,12]{1,0:T(8,128)S(1)}, u32[]{:S(2)}, u32[]{:S(2)}) collective-permute-start(s32[12,12]{1,0:T(8,128)} %refs_3_), channel_id=1, source_target_pairs={{0,3},{1,2},{2,1},{3,0},{4,7},{5,6},{6,5},{7,4},{8,11},{9,10},{10,... | collective-permute-start | bytes 1736 | tf_op jit(solution)/shard_map/ppermute | solution.py:289
  22.8 5.8 %collective-permute-start.6 = (s32[12,12]{1,0:T(8,128)}, s32[12,12]{1,0:T(8,128)S(1)}, u32[]{:S(2)}, u32[]{:S(2)}) collective-permute-start(s32[12,12]{1,0:T(8,128)} %refs_3_), channel_id=1, source_target_pairs={{0,2},{1,3},{2,0},{3,1},{4,6},{5,7},{6,4},{7,5},{8,10},{9,11},{10,... | collective-permute-start | bytes 1736 | tf_op jit(solution)/shard_map/ppermute | solution.py:289
  25.5 3.9 %collective-permute-start.5 = (s32[12,12]{1,0:T(8,128)}, s32[12,12]{1,0:T(8,128)S(1)}, u32[]{:S(2)}, u32[]{:S(2)}) collective-permute-start(s32[12,12]{1,0:T(8,128)} %refs_3_), channel_id=1, source_target_pairs={{0,1},{1,0},{2,3},{3,2},{4,5},{5,4},{6,7},{7,6},{8,9},{9,8},{10,11... | collective-permute-start | bytes 1736 | tf_op jit(solution)/shard_map/ppermute | solution.py:289
  26.5 2.9 %copy-start.1 = (s32[12,12]{1,0:T(8,128)S(1)}, s32[12,12]{1,0:T(8,128)}, u32[]{:S(2)}) copy-start(s32[12,12]{1,0:T(8,128)} %refs_3_) | copy-start | bytes 1732
  26.6 2.8 %collective-permute-start.12 = (bf16[384,384]{1,0:T(8,128)(2,1)S(1)}, bf16[384,384]{1,0:T(8,128)(2,1)S(1)}, u32[]{:S(2)}, u32[]{:S(2)}) collective-permute-start(bf16[384,384]{1,0:T(8,128)(2,1)S(1)} %select_select_fusion.refs_1_), channel_id=1, source_target_pairs={{0,4},{1,5},{2,6},{3,7},{4,0},{5,1},{6,2},{7,3},{8,12},{9,13},{10,... | collective-permute-start | bytes 884744 | tf_op jit(solution)/shard_map/ppermute | solution.py:67
  26.7 1.0 %copy-start = (bf16[384,384]{1,0:T(8,128)(2,1)S(1)}, bf16[384,384]{1,0:T(8,128)(2,1)}, u32[]{:S(2)}) copy-start(bf16[384,384]{1,0:T(8,128)(2,1)} %refs_0_.1) | copy-start | bytes 884740
  29.4 2.0 %collective-permute-start.13 = (bf16[384,384]{1,0:T(8,128)(2,1)S(1)}, bf16[384,384]{1,0:T(8,128)(2,1)S(1)}, u32[]{:S(2)}, u32[]{:S(2)}) collective-permute-start(bf16[384,384]{1,0:T(8,128)(2,1)S(1)} %collective-permute-done.4.refs_0_), channel_id=1, source_target_pairs={{0,4},{1,5},{2,6},{3,7},{4,0},{5,1},{6,2},{7,3},{8,12},{9,13},{10,... | collective-permute-start | bytes 884744 | tf_op jit(solution)/shard_map/ppermute | solution.py:67
